TPU v7x, 32 devices: a whole 2x2x4 slice. The times are simulated.
32 devices in a mesh: board: 2 (over y), sub: 16 (over z, x, core).
Axes of the slice: x: 2, y: 2, z: 4, core: 2. Of those that a mesh axis runs over, the one named last changes fastest.
Arguments:
- rhs: float32 [2, 32, 4096], P('board', None, 'sub')
- schur: float32 [2, 12288, 768], P('board', 'sub'), as said below
- block_list: int32 [2, 96], P('board', 'sub'), may hold values from 0 to 31, as said below
- pad_rows: int32 [2, 1024], P('board', 'sub'), may hold values from 0 to 255, as said below
- pad_cond: float32 [2, 1024], P('board', 'sub'), may hold values from 0.5 to 2
- sink: float32 [2, 4096], P('board', 'sub'), may hold values from 0.2 to 2
- precond: float32 [2, 4096], P('board', 'sub'), may hold values from 0.3 to 1
Outputs:
- solution: float32 [2, 32, 4096], P('board', None, 'sub')
- residual: float32 [2, 32, 4096], P('board', None, 'sub')
Inputs may be any that keep to these rules, and one draw needn't show every extreme that they name: `block_list`: every entry of a subdomain s's list is a block owned by a subdomain at most 3 away from s on the same board; the entries of one list are different and rising, and include all blocks that s owns. `pad_rows`: A subdomain's pad rows are different and rising, and include its first and last owned row. `schur`: each Schur block is symmetric and positive definite.
All inputs are finite; a program needn't handle non-finite values.
Results may differ from a plain program's by a relative error of at most 0.0003.
Values sent between devices are 32-bit elements; how exact they have to be, the bound alone decides.
No kernel may reach another device: no remote copies, remote signals or barrier semaphores. Data moves between devices by JAX's collectives and lax.ppermute only.
A program may use at most 64 MiB of HBM per device.

v0:
```python
import jax
import jax.numpy as jnp
from jax import lax
from jax.sharding import PartitionSpec as P

BR = 128
REACH = 3
ITERS = 2


def passed_along(value, axis, steps):
    count = lax.axis_size(axis)
    leading, last = (max(0, -steps), min(count, count - steps))
    return lax.ppermute(value, axis, [(source, source + steps) for source in range(leading, last)])


def from_partner(shard, axis, bit):
    return lax.ppermute(shard, axis, [(i, i ^ 1 << bit) for i in range(lax.axis_size(axis))])


def case_sums(left, right):
    return jnp.sum(left * right, axis=1)


def on_device(rhs, schur, block_list, pad_rows, pad_cond, sink, precond):
    right_side = rhs[0]
    matrix = schur[0]
    block_ids = block_list[0]
    pad_local = pad_rows[0]
    conduct = pad_cond[0]
    sink_rows = sink[0][None, :]
    scaling = precond[0][None, :]
    cases = right_side.shape[0]
    owned_rows = right_side.shape[1]
    blocks_owned = owned_rows // BR
    inner = matrix.shape[0]
    touched = block_ids.shape[0]
    position = lax.axis_index("sub")
    shifted_ids = block_ids - (position - REACH) * blocks_owned
    solution = jnp.zeros_like(right_side)
    residual = right_side
    precon = scaling * residual
    direction = precon
    norm_now = lax.psum(case_sums(residual, precon), ("board", "sub"))
    for iteration in range(ITERS):
        segments = []
        for offset in range(-REACH, REACH + 1):
            if offset == 0:
                segments.append(direction)
            else:
                segments.append(passed_along(direction, "sub", -offset))
        apply_blocks = jnp.concatenate(segments, axis=1).reshape(cases, -1, BR)
        picked = jnp.take(apply_blocks, shifted_ids, axis=1).reshape(cases, inner)
        product = jnp.dot(picked, matrix, precision=lax.Precision.HIGHEST)
        partial_value = (
            jnp.zeros(apply_blocks.shape, jnp.float32)
            .at[:, shifted_ids]
            .add(product.reshape(cases, touched, BR))
        )
        pieces = partial_value.reshape(cases, 2 * REACH + 1, owned_rows)
        result = pieces[:, REACH]
        for offset in range(-REACH, REACH + 1):
            if offset != 0:
                result = result + passed_along(pieces[:, REACH + offset], "sub", offset)
        pad_values = jnp.take(direction, pad_local, axis=1)
        other_values, other_cond = from_partner((pad_values, conduct), "board", 0)
        mean_cond = 0.5 * (conduct + other_cond)
        result = result.at[:, pad_local].add(mean_cond[None, :] * (pad_values - other_values))
        image = result + sink_rows * direction
        final = iteration == ITERS - 1
        curve = lax.psum(case_sums(direction, image), ("board", "sub"))
        alpha = norm_now / curve
        solution = solution + alpha[:, None] * direction
        residual = residual - alpha[:, None] * image
        if not final:
            precon = scaling * residual
            fresh = lax.psum(case_sums(residual, precon), ("board", "sub"))
            direction = precon + (fresh / norm_now)[:, None] * direction
            norm_now = fresh
    return (solution[None], residual[None])


def solution(mesh):
    in_specs = (
        P("board", None, "sub"),
        P("board", "sub", None),
        P("board", "sub"),
        P("board", "sub"),
        P("board", "sub"),
        P("board", "sub"),
        P("board", "sub"),
    )
    out_specs = (P("board", None, "sub"), P("board", None, "sub"))
    return jax.shard_map(
        on_device, mesh=mesh, in_specs=in_specs, out_specs=out_specs, check_vma=False
    )
```

profile of v0, /device:TPU:0, one launch (start us, length us, event | category | flops | bytes accessed | tf_op | source)
XLA Modules:
  0.0 238.5 jit_solution(10911073602321200998)
XLA Ops:
  2.3 4.3 %collective-permute-start = (f32[32,256]{0,1:T(8,128)S(1)}, f32[32,256]{0,1:T(8,128)S(1)}, u32[]{:S(2)}, u32[]{:S(2)}) collective-permute-start(f32[32,256]{0,1:T(8,128)S(1)} %bitcast_multiply_fusion.1), channel_id=1, source_target_pairs={{0,3},{1,4},{2,5},{3,6},{4,7},{5,8},{6,9},{7,10},{8,11},{9,12},{10... | collective-permute-start | bytes 98312 | tf_op jit(solution)/shard_map/ppermute | solution.py:14
  6.6 3.5 %collective-permute-start.1 = (f32[32,256]{0,1:T(8,128)S(1)}, f32[32,256]{0,1:T(8,128)S(1)}, u32[]{:S(2)}, u32[]{:S(2)}) collective-permute-start(f32[32,256]{0,1:T(8,128)S(1)} %bitcast_multiply_fusion.1), channel_id=1, source_target_pairs={{0,2},{1,3},{2,4},{3,5},{4,6},{5,7},{6,8},{7,9},{8,10},{9,11},{10,... | collective-permute-start | bytes 98312 | tf_op jit(solution)/shard_map/ppermute | solution.py:14
  10.0 2.3 collective-permute-start.2
  19.5 2.0 copy.104
  24.3 1.5 collective-permute-start.12
  27.6 2.3 collective-permute-done.5
  30.8 2.2 convolution_bitcast_fusion.1
  33.7 2.1 scatter_fusion
  37.1 5.7 %collective-permute-start.10 = (f32[32,256]{0,1:T(8,128)S(1)}, f32[32,256]{0,1:T(8,128)S(1)}, u32[]{:S(2)}, u32[]{:S(2)}) collective-permute-start(f32[32,256]{0,1:T(8,128)S(1)} %get-tuple-element.32), channel_id=1, source_target_pairs={{0,2},{1,3},{2,4},{3,5},{4,6},{5,7},{6,8},{7,9},{8,10},{9,11},{10,... | collective-permute-start | bytes 98312 | tf_op jit(solution)/shard_map/ppermute | solution.py:14
  43.4 2.9 %collective-permute-start.11 = (f32[32,256]{0,1:T(8,128)S(1)}, f32[32,256]{0,1:T(8,128)S(1)}, u32[]{:S(2)}, u32[]{:S(2)}) collective-permute-start(f32[32,256]{0,1:T(8,128)S(1)} %get-tuple-element.31), channel_id=1, source_target_pairs={{0,3},{1,4},{2,5},{3,6},{4,7},{5,8},{6,9},{7,10},{8,11},{9,12},{10... | collective-permute-start | bytes 98312 | tf_op jit(solution)/shard_map/ppermute | solution.py:14
  50.2 4.3 %collective-permute-start.9 = (f32[32,256]{0,1:T(8,128)S(1)}, f32[32,256]{0,1:T(8,128)S(1)}, u32[]{:S(2)}, u32[]{:S(2)}) collective-permute-start(f32[32,256]{0,1:T(8,128)S(1)} %get-tuple-element.33), channel_id=1, source_target_pairs={{0,1},{1,2},{2,3},{3,4},{4,5},{5,6},{6,7},{7,8},{8,9},{9,10},{10,1... | collective-permute-start | bytes 98312 | tf_op jit(solution)/shard_map/ppermute | solution.py:14
  58.2 1.8 collective-permute-done.13
  61.4 42.9 %all-reduce = (f32[32]{0:T(128)S(1)}, f32[32]{0:T(128)S(1)}) all-reduce(f32[32]{0:T(128)S(1)} %get-tuple-element.17, f32[32]{0:T(128)S(1)} %get-tuple-element.16), channel_id=1, replica_groups=mesh['board'=2,'sub'=16] {'board','sub'}, use_global_device_ids=true, to_apply=%region_1.0 | all-reduce | flops 64 | bytes 512 | tf_op jit(solution)/shard_map/psum | solution.py:44
  104.4 40.1 %psum.30 = f32[32]{0:T(128)S(1)} all-reduce(f32[32]{0:T(128)S(1)} %get-tuple-element.20), channel_id=1, replica_groups=mesh['board'=2,'sub'=16] {'board','sub'}, use_global_device_ids=true, to_apply=%region_7.10 | all-reduce | flops 32 | bytes 256 | tf_op jit(solution)/shard_map/psum | solution.py:77
  145.2 2.5 %collective-permute-start.14 = (f32[32,256]{0,1:T(8,128)S(1)}, f32[32,256]{0,1:T(8,128)S(1)}, u32[]{:S(2)}, u32[]{:S(2)}) collective-permute-start(f32[32,256]{0,1:T(8,128)S(1)} %multiply_add_fusion), channel_id=1, source_target_pairs={{0,3},{1,4},{2,5},{3,6},{4,7},{5,8},{6,9},{7,10},{8,11},{9,12},{10... | collective-permute-start | bytes 98312 | tf_op jit(solution)/shard_map/ppermute | solution.py:14
  147.7 3.7 %collective-permute-start.15 = (f32[32,256]{0,1:T(8,128)S(1)}, f32[32,256]{0,1:T(8,128)}, u32[]{:S(2)}, u32[]{:S(2)}) collective-permute-start(f32[32,256]{0,1:T(8,128)S(1)} %multiply_add_fusion), channel_id=1, source_target_pairs={{0,2},{1,3},{2,4},{3,5},{4,6},{5,7},{6,8},{7,9},{8,10},{9,11},{10,... | collective-permute-start | bytes 98312 | tf_op jit(solution)/shard_map/ppermute | solution.py:14
  151.4 3.6 %collective-permute-start.16 = (f32[32,256]{0,1:T(8,128)S(1)}, f32[32,256]{0,1:T(8,128)S(1)}, u32[]{:S(2)}, u32[]{:S(2)}) collective-permute-start(f32[32,256]{0,1:T(8,128)S(1)} %multiply_add_fusion), channel_id=1, source_target_pairs={{0,1},{1,2},{2,3},{3,4},{4,5},{5,6},{6,7},{7,8},{8,9},{9,10},{10,1... | collective-permute-start | bytes 98312 | tf_op jit(solution)/shard_map/ppermute | solution.py:14
  160.3 1.6 copy.114
  167.6 2.2 convolution_bitcast_fusion
  175.6 3.9 %collective-permute-start.23 = (f32[32,256]{0,1:T(8,128)S(1)}, f32[32,256]{0,1:T(8,128)S(1)}, u32[]{:S(2)}, u32[]{:S(2)}) collective-permute-start(f32[32,256]{0,1:T(8,128)S(1)} %get-tuple-element.27), channel_id=1, source_target_pairs={{0,1},{1,2},{2,3},{3,4},{4,5},{5,6},{6,7},{7,8},{8,9},{9,10},{10,1... | collective-permute-start | bytes 98312 | tf_op jit(solution)/shard_map/ppermute | solution.py:14
  179.5 4.3 %collective-permute-start.24 = (f32[32,256]{0,1:T(8,128)S(1)}, f32[32,256]{0,1:T(8,128)S(1)}, u32[]{:S(2)}, u32[]{:S(2)}) collective-permute-start(f32[32,256]{0,1:T(8,128)S(1)} %get-tuple-element.26), channel_id=1, source_target_pairs={{0,2},{1,3},{2,4},{3,5},{4,6},{5,7},{6,8},{7,9},{8,10},{9,11},{10,... | collective-permute-start | bytes 98312 | tf_op jit(solution)/shard_map/ppermute | solution.py:14
  183.8 6.1 %collective-permute-start.25 = (f32[32,256]{0,1:T(8,128)S(1)}, f32[32,256]{0,1:T(8,128)S(1)}, u32[]{:S(2)}, u32[]{:S(2)}) collective-permute-start(f32[32,256]{0,1:T(8,128)S(1)} %get-tuple-element.25), channel_id=1, source_target_pairs={{0,3},{1,4},{2,5},{3,6},{4,7},{5,8},{6,9},{7,10},{8,11},{9,12},{10... | collective-permute-start | bytes 98312 | tf_op jit(solution)/shard_map/ppermute | solution.py:14
  189.9 1.6 collective-permute-start.26
  195.1 41.8 %psum.31 = f32[32]{0:T(128)S(1)} all-reduce(f32[32]{0:T(128)S(1)} %multiply_reduce_fusion), channel_id=1, replica_groups=mesh['board'=2,'sub'=16] {'board','sub'}, use_global_device_ids=true, to_apply=%region_11.14 | all-reduce | flops 32 | bytes 256 | tf_op jit(solution)/shard_map/psum | solution.py:71
  (135 shorter events, 48.0 us)
Async XLA Ops:
  2.3 19.3 %collective-permute-start = (f32[32,256]{0,1:T(8,128)S(1)}, f32[32,256]{0,1:T(8,128)S(1)}, u32[]{:S(2)}, u32[]{:S(2)}) collective-permute-start(f32[32,256]{0,1:T(8,128)S(1)} %bitcast_multiply_fusion.1), channel_id=1, source_target_pairs={{0,3},{1,4},{2,5},{3,6},{4,7},{5,8},{6,9},{7,10},{8,11},{9,12},{10... | collective-permute-start | bytes 98312 | tf_op jit(solution)/shard_map/ppermute | solution.py:14
  6.6 17.8 %collective-permute-start.1 = (f32[32,256]{0,1:T(8,128)S(1)}, f32[32,256]{0,1:T(8,128)S(1)}, u32[]{:S(2)}, u32[]{:S(2)}) collective-permute-start(f32[32,256]{0,1:T(8,128)S(1)} %bitcast_multiply_fusion.1), channel_id=1, source_target_pairs={{0,2},{1,3},{2,4},{3,5},{4,6},{5,7},{6,8},{7,9},{8,10},{9,11},{10,... | collective-permute-start | bytes 98312 | tf_op jit(solution)/shard_map/ppermute | solution.py:14
  10.0 17.3 %collective-permute-start.2 = (f32[32,256]{0,1:T(8,128)S(1)}, f32[32,256]{0,1:T(8,128)S(1)}, u32[]{:S(2)}, u32[]{:S(2)}) collective-permute-start(f32[32,256]{0,1:T(8,128)S(1)} %bitcast_multiply_fusion.1), channel_id=1, source_target_pairs={{0,1},{1,2},{2,3},{3,4},{4,5},{5,6},{6,7},{7,8},{8,9},{9,10},{10,1... | collective-permute-start | bytes 98312 | tf_op jit(solution)/shard_map/ppermute | solution.py:14
  12.4 15.0 %collective-permute-start.3 = (f32[32,256]{0,1:T(8,128)S(1)}, f32[32,256]{0,1:T(8,128)S(1)}, u32[]{:S(2)}, u32[]{:S(2)}) collective-permute-start(f32[32,256]{0,1:T(8,128)S(1)} %bitcast_multiply_fusion.1), channel_id=1, source_target_pairs={{1,0},{2,1},{3,2},{4,3},{5,4},{6,5},{7,6},{8,7},{9,8},{10,9},{11,1... | collective-permute-start | bytes 98312 | tf_op jit(solution)/shard_map/ppermute | solution.py:14
  13.7 13.8 %collective-permute-start.4 = (f32[32,256]{0,1:T(8,128)S(1)}, f32[32,256]{0,1:T(8,128)S(1)}, u32[]{:S(2)}, u32[]{:S(2)}) collective-permute-start(f32[32,256]{0,1:T(8,128)S(1)} %bitcast_multiply_fusion.1), channel_id=1, source_target_pairs={{2,0},{3,1},{4,2},{5,3},{6,4},{7,5},{8,6},{9,7},{10,8},{11,9},{12,... | collective-permute-start | bytes 98312 | tf_op jit(solution)/shard_map/ppermute | solution.py:14
  21.6 8.3 %collective-permute-start.5 = (f32[32,256]{0,1:T(8,128)S(1)}, f32[32,256]{0,1:T(8,128)S(1)}, u32[]{:S(2)}, u32[]{:S(2)}) collective-permute-start(f32[32,256]{0,1:T(8,128)S(1)} %bitcast_multiply_fusion.1), channel_id=1, source_target_pairs={{3,0},{4,1},{5,2},{6,3},{7,4},{8,5},{9,6},{10,7},{11,8},{12,9},{13... | collective-permute-start | bytes 98312 | tf_op jit(solution)/shard_map/ppermute | solution.py:14
  24.3 24.6 %collective-permute-start.12 = (f32[64]{0:T(128)}, f32[64]{0:T(128)}, u32[]{:S(2)}, u32[]{:S(2)}) collective-permute-start(f32[64]{0:T(128)} %bitcast.155), channel_id=1, source_target_pairs={{0,16},{16,0},{1,17},{17,1},{2,18},{18,2},{3,19},{19,3},{4,20},{20... | collective-permute-start | bytes 776 | tf_op jit(solution)/shard_map/ppermute | solution.py:18
  37.1 13.1 %collective-permute-start.10 = (f32[32,256]{0,1:T(8,128)S(1)}, f32[32,256]{0,1:T(8,128)S(1)}, u32[]{:S(2)}, u32[]{:S(2)}) collective-permute-start(f32[32,256]{0,1:T(8,128)S(1)} %get-tuple-element.32), channel_id=1, source_target_pairs={{0,2},{1,3},{2,4},{3,5},{4,6},{5,7},{6,8},{7,9},{8,10},{9,11},{10,... | collective-permute-start | bytes 98312 | tf_op jit(solution)/shard_map/ppermute | solution.py:14
  43.4 12.4 %collective-permute-start.11 = (f32[32,256]{0,1:T(8,128)S(1)}, f32[32,256]{0,1:T(8,128)S(1)}, u32[]{:S(2)}, u32[]{:S(2)}) collective-permute-start(f32[32,256]{0,1:T(8,128)S(1)} %get-tuple-element.31), channel_id=1, source_target_pairs={{0,3},{1,4},{2,5},{3,6},{4,7},{5,8},{6,9},{7,10},{8,11},{9,12},{10... | collective-permute-start | bytes 98312 | tf_op jit(solution)/shard_map/ppermute | solution.py:14
  46.3 11.0 %collective-permute-start.6 = (f32[32,256]{0,1:T(8,128)S(1)}, f32[32,256]{0,1:T(8,128)S(1)}, u32[]{:S(2)}, u32[]{:S(2)}) collective-permute-start(f32[32,256]{0,1:T(8,128)S(1)} %get-tuple-element.30), channel_id=1, source_target_pairs={{3,0},{4,1},{5,2},{6,3},{7,4},{8,5},{9,6},{10,7},{11,8},{12,9},{13... | collective-permute-start | bytes 98312 | tf_op jit(solution)/shard_map/ppermute | solution.py:14
  47.6 9.7 %collective-permute-start.7 = (f32[32,256]{0,1:T(8,128)S(1)}, f32[32,256]{0,1:T(8,128)S(1)}, u32[]{:S(2)}, u32[]{:S(2)}) collective-permute-start(f32[32,256]{0,1:T(8,128)S(1)} %get-tuple-element.35), channel_id=1, source_target_pairs={{2,0},{3,1},{4,2},{5,3},{6,4},{7,5},{8,6},{9,7},{10,8},{11,9},{12,... | collective-permute-start | bytes 98312 | tf_op jit(solution)/shard_map/ppermute | solution.py:14
  48.9 8.4 %collective-permute-start.8 = (f32[32,256]{0,1:T(8,128)S(1)}, f32[32,256]{0,1:T(8,128)S(1)}, u32[]{:S(2)}, u32[]{:S(2)}) collective-permute-start(f32[32,256]{0,1:T(8,128)S(1)} %get-tuple-element.34), channel_id=1, source_target_pairs={{1,0},{2,1},{3,2},{4,3},{5,4},{6,5},{7,6},{8,7},{9,8},{10,9},{11,1... | collective-permute-start | bytes 98312 | tf_op jit(solution)/shard_map/ppermute | solution.py:14
  145.2 12.4 %collective-permute-start.14 = (f32[32,256]{0,1:T(8,128)S(1)}, f32[32,256]{0,1:T(8,128)S(1)}, u32[]{:S(2)}, u32[]{:S(2)}) collective-permute-start(f32[32,256]{0,1:T(8,128)S(1)} %multiply_add_fusion), channel_id=1, source_target_pairs={{0,3},{1,4},{2,5},{3,6},{4,7},{5,8},{6,9},{7,10},{8,11},{9,12},{10... | collective-permute-start | bytes 98312 | tf_op jit(solution)/shard_map/ppermute | solution.py:14
  147.7 12.7 %collective-permute-start.15 = (f32[32,256]{0,1:T(8,128)S(1)}, f32[32,256]{0,1:T(8,128)}, u32[]{:S(2)}, u32[]{:S(2)}) collective-permute-start(f32[32,256]{0,1:T(8,128)S(1)} %multiply_add_fusion), channel_id=1, source_target_pairs={{0,2},{1,3},{2,4},{3,5},{4,6},{5,7},{6,8},{7,9},{8,10},{9,11},{10,... | collective-permute-start | bytes 98312 | tf_op jit(solution)/shard_map/ppermute | solution.py:14
  151.4 11.4 %collective-permute-start.16 = (f32[32,256]{0,1:T(8,128)S(1)}, f32[32,256]{0,1:T(8,128)S(1)}, u32[]{:S(2)}, u32[]{:S(2)}) collective-permute-start(f32[32,256]{0,1:T(8,128)S(1)} %multiply_add_fusion), channel_id=1, source_target_pairs={{0,1},{1,2},{2,3},{3,4},{4,5},{5,6},{6,7},{7,8},{8,9},{9,10},{10,1... | collective-permute-start | bytes 98312 | tf_op jit(solution)/shard_map/ppermute | solution.py:14
  155.0 9.2 %collective-permute-start.17 = (f32[32,256]{0,1:T(8,128)S(1)}, f32[32,256]{0,1:T(8,128)S(1)}, u32[]{:S(2)}, u32[]{:S(2)}) collective-permute-start(f32[32,256]{0,1:T(8,128)S(1)} %multiply_add_fusion), channel_id=1, source_target_pairs={{1,0},{2,1},{3,2},{4,3},{5,4},{6,5},{7,6},{8,7},{9,8},{10,9},{11,1... | collective-permute-start | bytes 98312 | tf_op jit(solution)/shard_map/ppermute | solution.py:14
  156.3 8.5 %collective-permute-start.18 = (f32[32,256]{0,1:T(8,128)S(1)}, f32[32,256]{0,1:T(8,128)S(1)}, u32[]{:S(2)}, u32[]{:S(2)}) collective-permute-start(f32[32,256]{0,1:T(8,128)S(1)} %multiply_add_fusion), channel_id=1, source_target_pairs={{2,0},{3,1},{4,2},{5,3},{6,4},{7,5},{8,6},{9,7},{10,8},{11,9},{12,... | collective-permute-start | bytes 98312 | tf_op jit(solution)/shard_map/ppermute | solution.py:14
  157.6 8.5 %collective-permute-start.19 = (f32[32,256]{0,1:T(8,128)S(1)}, f32[32,256]{0,1:T(8,128)S(1)}, u32[]{:S(2)}, u32[]{:S(2)}) collective-permute-start(f32[32,256]{0,1:T(8,128)S(1)} %multiply_add_fusion), channel_id=1, source_target_pairs={{3,0},{4,1},{5,2},{6,3},{7,4},{8,5},{9,6},{10,7},{11,8},{12,9},{13... | collective-permute-start | bytes 98312 | tf_op jit(solution)/shard_map/ppermute | solution.py:14
  171.1 12.7 %collective-permute-start.20 = (f32[32,256]{0,1:T(8,128)S(1)}, f32[32,256]{0,1:T(8,128)S(1)}, u32[]{:S(2)}, u32[]{:S(2)}) collective-permute-start(f32[32,256]{0,1:T(8,128)S(1)} %get-tuple-element.24), channel_id=1, source_target_pairs={{3,0},{4,1},{5,2},{6,3},{7,4},{8,5},{9,6},{10,7},{11,8},{12,9},{13... | collective-permute-start | bytes 98312 | tf_op jit(solution)/shard_map/ppermute | solution.py:14
  173.0 16.9 %collective-permute-start.21 = (f32[32,256]{0,1:T(8,128)S(1)}, f32[32,256]{0,1:T(8,128)S(1)}, u32[]{:S(2)}, u32[]{:S(2)}) collective-permute-start(f32[32,256]{0,1:T(8,128)S(1)} %get-tuple-element.29), channel_id=1, source_target_pairs={{2,0},{3,1},{4,2},{5,3},{6,4},{7,5},{8,6},{9,7},{10,8},{11,9},{12,... | collective-permute-start | bytes 98312 | tf_op jit(solution)/shard_map/ppermute | solution.py:14
  174.3 17.3 %collective-permute-start.22 = (f32[32,256]{0,1:T(8,128)S(1)}, f32[32,256]{0,1:T(8,128)S(1)}, u32[]{:S(2)}, u32[]{:S(2)}) collective-permute-start(f32[32,256]{0,1:T(8,128)S(1)} %get-tuple-element.28), channel_id=1, source_target_pairs={{1,0},{2,1},{3,2},{4,3},{5,4},{6,5},{7,6},{8,7},{9,8},{10,9},{11,1... | collective-permute-start | bytes 98312 | tf_op jit(solution)/shard_map/ppermute | solution.py:14
  175.6 16.0 %collective-permute-start.23 = (f32[32,256]{0,1:T(8,128)S(1)}, f32[32,256]{0,1:T(8,128)S(1)}, u32[]{:S(2)}, u32[]{:S(2)}) collective-permute-start(f32[32,256]{0,1:T(8,128)S(1)} %get-tuple-element.27), channel_id=1, source_target_pairs={{0,1},{1,2},{2,3},{3,4},{4,5},{5,6},{6,7},{7,8},{8,9},{9,10},{10,1... | collective-permute-start | bytes 98312 | tf_op jit(solution)/shard_map/ppermute | solution.py:14
  179.5 12.1 %collective-permute-start.24 = (f32[32,256]{0,1:T(8,128)S(1)}, f32[32,256]{0,1:T(8,128)S(1)}, u32[]{:S(2)}, u32[]{:S(2)}) collective-permute-start(f32[32,256]{0,1:T(8,128)S(1)} %get-tuple-element.26), channel_id=1, source_target_pairs={{0,2},{1,3},{2,4},{3,5},{4,6},{5,7},{6,8},{7,9},{8,10},{9,11},{10,... | collective-permute-start | bytes 98312 | tf_op jit(solution)/shard_map/ppermute | solution.py:14
  183.8 8.6 %collective-permute-start.25 = (f32[32,256]{0,1:T(8,128)S(1)}, f32[32,256]{0,1:T(8,128)S(1)}, u32[]{:S(2)}, u32[]{:S(2)}) collective-permute-start(f32[32,256]{0,1:T(8,128)S(1)} %get-tuple-element.25), channel_id=1, source_target_pairs={{0,3},{1,4},{2,5},{3,6},{4,7},{5,8},{6,9},{7,10},{8,11},{9,12},{10... | collective-permute-start | bytes 98312 | tf_op jit(solution)/shard_map/ppermute | solution.py:14
  (16 other events, 325.0 us)
where the time goes:
time: 240 us; the launch traced here: 238 us
  blocking collectives  125 us (52%)
  starting transfers between devices  67.1 us (28%)
  local copies, waits for them, and re-layouts  18.5 us (8%)
  other arithmetic  14.1 us (6%)
  waiting for transfers between devices  8.2 us (3%)
  matrix products  4.43 us (2%)
    ppermute x24, starting transfers between devices, passed_along(): lax.ppermute(value, axis, [(source, source + steps) for source in range(l...  62.4 us
    psum x1, blocking collectives, on_device(): norm_now = lax.psum(case_sums(residual, precon), ('board', 'sub'))  42.9 us
    psum x1, blocking collectives, on_device(): curve = lax.psum(case_sums(direction, image), ('board', 'sub'))  41.8 us
    psum x1, blocking collectives, on_device(): fresh = lax.psum(case_sums(residual, precon), ('board', 'sub'))  40.1 us
    unnamed x42, local copies, waits for them, and re-layouts  8.71 us
    ppermute x24, waiting for transfers between devices, passed_along(): lax.ppermute(value, axis, [(source, source + steps) for source in range(l...  4.89 us
  transfers between devices with their start and end apart: 27, of which 6 were waited for; matrix products, arithmetic and copies ran while one was open for 11% of the time, Pallas kernels for 0%

commit v1 on v0

v1 whole, which is shorter than its diff:
```python
import jax
import jax.numpy as jnp
from jax import lax
from jax.experimental import pallas as pl
from jax.experimental.pallas import tpu as pltpu
from jax.sharding import PartitionSpec as P

BR = 128
REACH = 3
ITERS = 2
F32 = jnp.float32
HALF = jnp.bfloat16
barrier = lax.optimization_barrier


def passed_along(value, axis, steps):
    count = lax.axis_size(axis)
    leading, last = (max(0, -steps), min(count, count - steps))
    return lax.ppermute(value, axis, [(source, source + steps) for source in range(leading, last)])


def case_sums(left, right):
    return jnp.sum(left * right, axis=1)


def step_by_step(right_side, matrix, block_ids, pad_local, conduct, sink_rows, scaling):
    cases, owned_rows = right_side.shape
    blocks_owned = owned_rows // BR
    inner = matrix.shape[0]
    touched = block_ids.shape[0]
    across = [(i, i ^ 1) for i in range(lax.axis_size("board"))]
    shifted_ids = block_ids - (lax.axis_index("sub") - REACH) * blocks_owned
    solution = jnp.zeros_like(right_side)
    residual = right_side
    precon = scaling * residual
    direction = precon
    norm_now = lax.psum(case_sums(residual, precon), ("board", "sub"))
    for iteration in range(ITERS):
        segments = [
            direction if offset == 0 else passed_along(direction, "sub", -offset)
            for offset in range(-REACH, REACH + 1)
        ]
        apply_blocks = jnp.concatenate(segments, axis=1).reshape(cases, -1, BR)
        picked = jnp.take(apply_blocks, shifted_ids, axis=1).reshape(cases, inner)
        product = jnp.dot(picked, matrix, precision=lax.Precision.HIGHEST)
        partial_value = (
            jnp.zeros(apply_blocks.shape, F32).at[:, shifted_ids].add(product.reshape(cases, touched, BR))
        )
        pieces = partial_value.reshape(cases, 2 * REACH + 1, owned_rows)
        result = pieces[:, REACH]
        for offset in range(-REACH, REACH + 1):
            if offset != 0:
                result = result + passed_along(pieces[:, REACH + offset], "sub", offset)
        pad_values = jnp.take(direction, pad_local, axis=1)
        other_values = lax.ppermute(pad_values, "board", across)
        mean_cond = 0.5 * (conduct + lax.ppermute(conduct, "board", across))
        result = result.at[:, pad_local].add(mean_cond[None, :] * (pad_values - other_values))
        image = result + sink_rows * direction
        alpha = norm_now / lax.psum(case_sums(direction, image), ("board", "sub"))
        solution = solution + alpha[:, None] * direction
        residual = residual - alpha[:, None] * image
        if iteration < ITERS - 1:
            precon = scaling * residual
            fresh = lax.psum(case_sums(residual, precon), ("board", "sub"))
            direction = precon + (fresh / norm_now)[:, None] * direction
            norm_now = fresh
    return solution, residual


def climb(count, step):
    pairs = []
    for source in range(count):
        chip, core = divmod(source, 2)
        target = chip - step if core else chip + step
        inside = 0 <= target < count // 2
        pairs.append((source, target * 2 + core if inside else source ^ 1))
    return pairs


def leap(count):
    pairs = []
    for source in range(count):
        chip, core = divmod(source, 2)
        target = chip + 2 if core else chip - 2
        if 0 <= target < count // 2:
            pairs.append((source, target * 2 + 1 - core))
        else:
            pairs.append((source, source ^ 2))
    return pairs


def turned(pairs):
    return [(target, source) for source, target in pairs]


def thirds(value):
    high = value.astype(HALF)
    rest = value - high.astype(F32)
    middle = rest.astype(HALF)
    return high, middle, (rest - middle.astype(F32)).astype(HALF)


def dot(left, right):
    return jnp.dot(left, right, preferred_element_type=F32)


def times_ones(value, ones, turn):
    rows = value.shape[0]
    parts = jnp.concatenate(thirds(value))
    if turn:
        out = lax.dot_general(parts, ones, (((1,), (1,)), ((), ())), preferred_element_type=F32)
    else:
        out = dot(parts, ones)
    return out[:rows] + (out[rows : 2 * rows] + out[2 * rows :])


def product_of(value, high, middle, low):
    rows = value.shape[0]
    one, two, three = thirds(value)
    first = dot(jnp.concatenate([one, two, three]), high[...])
    second = dot(jnp.concatenate([one, two]), middle[...])
    small = first[2 * rows :] + second[rows:] + dot(one, low[...])
    return (small + (first[rows : 2 * rows] + second[:rows])) + first[:rows]


def wide(pair):
    return jnp.concatenate([pair[0], pair[1]], axis=1)


def put_wide(ref, start, value):
    ref[start] = value[:, :BR]
    ref[start + 1] = value[:, BR:]


def lanes_of(cases, slot):
    lane = lax.broadcasted_iota(jnp.int32, (cases, BR), 1)
    return lane == lax.broadcasted_iota(jnp.int32, (cases, BR), 0) + slot * cases


def as_row(column, slot):
    return jnp.sum(jnp.where(lanes_of(column.shape[0], slot), column, 0.0), axis=0, keepdims=True)


def as_column(row, slot, cases):
    return jnp.sum(jnp.where(lanes_of(cases, slot), row, 0.0), axis=1, keepdims=True)


def begin_kernel(rhs, precond, sink, pads, cond, rhs_out, rows_out, z_out, ones_out, pads_out, pad_at, cond_at, sems):
    copies = [
        pltpu.make_async_copy(rhs, rhs_out, sems.at[0]),
        pltpu.make_async_copy(precond, rows_out.at[0], sems.at[1]),
        pltpu.make_async_copy(sink, rows_out.at[1], sems.at[2]),
        pltpu.make_async_copy(pads, pad_at, sems.at[3]),
        pltpu.make_async_copy(cond, cond_at, sems.at[4]),
    ]
    for copy in copies:
        copy.start()
    for copy in copies:
        copy.wait()
    z = rows_out[0] * rhs_out[...]
    cases, owned = z.shape
    put_wide(z_out, 0, z)
    count = pad_at.shape[1]
    here = lax.broadcasted_iota(jnp.int32, (owned, count), 0)
    ones = (here == pad_at[...]).astype(F32).astype(HALF)
    ones_out[...] = ones
    pads_out[...] = jnp.zeros_like(pads_out)
    pads_out[:cases, :count] = times_ones(z, ones, False)
    pads_out[cases : cases + 1, :count] = cond_at[...]


def prepare_kernel(schur, blocks, high, middle, low, places, held, listed, sems):
    chunk = held.shape[0] // (sems.shape[0] - 1)
    copies = []
    for i in range(sems.shape[0] - 1):
        rows = slice(i * chunk, (i + 1) * chunk)
        copies.append(pltpu.make_async_copy(schur.at[rows], held.at[rows], sems.at[i]))
    lists = pltpu.make_async_copy(blocks, listed, sems.at[sems.shape[0] - 1])
    lists.start()
    for copy in copies:
        copy.start()
    position = lax.axis_index("sub")
    chip, core = position // 2, lax.rem(position, 2)
    above, below = lax.axis_size("sub") // 2 - 1 - chip, chip
    lists.wait()
    touched = listed.shape[1]
    offset = listed[...] // 2 - position
    mirrored = jnp.where(core == 0, offset, -offset)
    place = jnp.where(mirrored == 2, 6, jnp.where(mirrored == 3, 5, mirrored + REACH))
    place = place * 2 + lax.rem(listed[...], 2)
    spots = 2 * (2 * REACH + 1)
    for i in range(touched):
        here = jnp.broadcast_to(place[:, i : i + 1], places.shape[1:])
        for j in range(spots):
            places[i * spots + j] = (here == j).astype(F32)
    near = jnp.where(core == 0, above, below) >= 1
    far = jnp.where(core == 0, below, above) >= 2
    for i, sender in enumerate((near, far)):
        places[touched * spots + i] = jnp.full(places.shape[1:], sender.astype(F32))
    for i, copy in enumerate(copies):
        rows = slice(i * chunk, (i + 1) * chunk)
        copy.wait()
        high[rows], middle[rows], low[rows] = thirds(held[rows])


def product_kernel(first, places, high, middle, low, p2, p1, own, a, b, there, conds, mine, ones, rows, *rest):
    if first:
        back, to_p1, to_p2, kept = rest
    else:
        sums, back, to_p1, to_p2, kept, sums_out = rest
    touched = high.shape[0] // BR
    cases = own.shape[1]
    spots = 2 * (2 * REACH + 1)
    held = [p2[0], p2[1], p1[0], p1[1], p1[2], p1[3], own[0], own[1], a[0], a[1], b[0], b[1], b[2], b[3]]

    def spot(i, j):
        return jnp.concatenate([places[i * spots + j]] * (cases // 8))

    picked = []
    for i in range(touched):
        total = spot(i, 0) * held[0]
        for j in range(1, spots):
            total = total + spot(i, j) * held[j]
        picked.append(total)
    picked = jnp.concatenate(picked, axis=1)
    product = product_of(picked, high, middle, low)

    def landed(j):
        total = spot(0, j) * product[:, :BR]
        for i in range(1, touched):
            total = total + spot(i, j) * product[:, i * BR : (i + 1) * BR]
        return total

    for j in range(2):
        to_p2[j] = landed(j)
    for j in range(4):
        back[j] = landed(10 + j)
        to_p1[j] = landed(2 + j)
    kept[2] = landed(8)
    kept[3] = landed(9)
    count = ones.shape[1]
    mean_cond = 0.5 * (mine[cases : cases + 8, :count] + conds[cases : cases + 8, :count])
    spread = jnp.concatenate([mean_cond[:1] * there[:cases, :count], mean_cond])
    spread = times_ones(spread, ones[...], True)
    here = wide(own)
    local = (rows[1] + spread[cases : cases + 1]) * here - spread[:cases]
    kept[0] = landed(6) + local[:, :BR]
    kept[1] = landed(7) + local[:, BR:]
    if not first:
        energy = jnp.sum(picked * product, axis=1, keepdims=True) + jnp.sum(here * local, axis=1, keepdims=True)
        total = sums[...] + as_row(energy, 3)
        sums_out[...] = jnp.broadcast_to(total[None], sums_out.shape)


def gather_parts(places, kept, from_p1, from_p2):
    near, far = [
        jnp.concatenate([places[places.shape[0] - 2 + i]] * (kept.shape[1] // 8))[None] for i in range(2)
    ]
    one = from_p1[...] * near
    return kept[0:2] + one[0:2] + from_p2[...] * far, kept[2:4] + one[2:4]


def part_kernel(places, kept, from_p1, from_p2, rows, part):
    mine, other = gather_parts(places, kept, from_p1, from_p2)
    part[0:2] = mine
    part[2:4] = other
    part[4] = jnp.zeros(part.shape[1:], F32)
    part[4, 0:1] = rows[0, :, :BR]
    part[4, 1:2] = rows[0, :, BR:]


def turn_kernel(part, there, rhs, z, rows, ones, image_out, both_out, own_out, pads_out, sums_out):
    image = wide(part[0:2] + there[2:4])
    other = part[2:4] + there[0:2]
    image_out[...] = image
    scaled = rows[0] * image
    put_wide(both_out, 0, scaled)
    put_wide(own_out, 0, scaled)
    both_out[2] = there[4, 0:1] * other[0]
    both_out[3] = there[4, 1:2] * other[1]
    count = ones.shape[1]
    pads_out[...] = jnp.zeros_like(pads_out)
    pads_out[:, :count] = times_ones(scaled, ones[...], False)
    start = wide(z)
    one = jnp.sum(rhs[...] * start, axis=1, keepdims=True)
    two = jnp.sum(start * image, axis=1, keepdims=True)
    three = jnp.sum(image * scaled, axis=1, keepdims=True)
    sums_out[...] = as_row(one, 0) + as_row(two, 1) + as_row(three, 2)


def last_part_kernel(places, kept, from_p1, from_p2, mine_out, other_out):
    mine_out[...], other_out[...] = gather_parts(places, kept, from_p1, from_p2)


def steps_kernel(sums, steps, fine):
    cases = steps.shape[1]
    total = jnp.sum(sums[...], axis=0)
    norm, curve, cross, energy = [as_column(total, slot, cases) for slot in range(4)]
    alpha = norm / curve
    fresh = alpha * alpha * cross - norm
    grown = 1.0 + fresh / norm
    terms = [grown * grown * curve, 2.0 * alpha * grown * cross, alpha * alpha * energy]
    bend = terms[0] - terms[1] + terms[2]
    good = (norm > 1e-30) & (energy < 1e30) & (cross < 1e30) & (curve > 0.0) & (fresh > 0.02 * norm)
    good = good & (bend > 0.004 * (terms[0] + terms[1] + terms[2]))
    fine[0, 0] = jnp.sum(jnp.where(good, 1, 0))
    for i, value in enumerate((alpha, grown, fresh / bend)):
        steps[i] = jnp.broadcast_to(value, steps.shape[1:])


def end_kernel(rhs, z, image, scaled, mine, there, steps, solution, residual):
    alpha, grown, step = [wide([steps[i], steps[i]]) for i in range(3)]
    start = wide(z)
    direction = grown * start - alpha * wide(scaled)
    solution[...] = alpha * start + step * direction
    second = wide(mine[...] + there[...])
    residual[...] = rhs[...] - alpha * image[...] - step * (grown * image[...] - alpha * second)


def call(kernel, outs, *operands, scratch=(), far=(), scalar=()):
    def space(outside, i, smem=()):
        return pl.BlockSpec(memory_space=pl.ANY if i in outside else pltpu.SMEM if i in smem else pltpu.VMEM)

    return pl.pallas_call(
        kernel,
        in_specs=[space(far, i) for i in range(len(operands))],
        out_specs=[space((), i, scalar) for i in range(len(outs))],
        out_shape=[jax.ShapeDtypeStruct(shape, kind) for shape, kind in outs],
        scratch_shapes=list(scratch),
        compiler_params=pltpu.CompilerParams(vmem_limit_bytes=32 * 1024 * 1024),
    )(*operands)


def on_device(rhs, schur, block_list, pad_rows, pad_cond, sink, precond):
    matrix = schur[0]
    cases, owned = rhs.shape[1:]
    inner = matrix.shape[0]
    blocks = owned // BR
    touched = inner // BR
    count = lax.axis_size("sub")
    everyone = count * lax.axis_size("board")
    pads = pad_rows.shape[1]
    swap = [(i, i ^ 1) for i in range(count)]
    across = [(i, i ^ 1) for i in range(lax.axis_size("board"))]
    near, far = climb(count, 1), leap(count)
    pair = ((blocks, cases, BR), F32)
    both = ((2 * blocks, cases, BR), F32)
    row = ((1, BR), F32)
    full = ((cases, owned), F32)
    semaphores = pltpu.SemaphoreType.DMA

    right_side, rows, z, ones, pads_sent = call(
        begin_kernel,
        [full, ((2, 1, owned), F32), pair, ((owned, pads), HALF), ((cases + 8, BR), F32)],
        rhs[0], precond, sink, pad_rows, pad_cond,
        far=range(5),
        scratch=[pltpu.VMEM((1, pads), jnp.int32), pltpu.VMEM((1, pads), F32), semaphores((5,))],
    )
    chunks = 6
    spots = 2 * (2 * REACH + 1)
    high, middle, low, places = call(
        prepare_kernel,
        [((inner, inner), HALF)] * 3 + [((touched * spots + 2, 8, BR), F32)],
        matrix, block_list,
        far=range(2),
        scratch=[pltpu.VMEM((inner, inner), F32), pltpu.VMEM((1, touched), jnp.int32), semaphores((chunks + 1,))],
    )

    def product(first, *operands):
        return call(
            lambda *refs: product_kernel(first, *refs),
            [both, both, pair, both] + ([] if first else [((everyone, 1, BR), F32)]),
            places, high, middle, low, *operands,
        )

    def collect(back, to_p1, to_p2):
        from_p2 = lax.ppermute(to_p2, "sub", far)
        to_p1 = to_p1 + lax.ppermute(back, "sub", swap)
        return to_p1, from_p2

    other = lax.ppermute(z, "sub", swap)
    p2 = lax.ppermute(z, "sub", far)
    conds = lax.ppermute(pads_sent, "board", across)
    p1 = lax.ppermute(jnp.concatenate([z, other]), "sub", near)
    p1, p2, conds = barrier((p1, p2, conds))
    b = lax.ppermute(p1, "sub", swap)
    back, to_p1, to_p2, kept = product(True, p2, p1, z, other, b, conds, conds, pads_sent, ones, rows)
    to_p1, from_p2 = collect(back, to_p1, to_p2)
    from_p1 = lax.ppermute(to_p1, "sub", turned(near))
    (part,) = call(part_kernel, [((2 * blocks + 1, cases, BR), F32)], places, kept, from_p1, from_p2, rows)
    part_there = lax.ppermute(part, "sub", swap)
    image, four, own, values, sums = call(
        turn_kernel, [full, both, pair, ((cases, BR), F32), row], part, part_there, right_side, z, rows, ones
    )
    p1 = lax.ppermute(four, "sub", near)
    p2 = lax.ppermute(own, "sub", far)
    there = lax.ppermute(values, "board", across)
    p1, p2, there = barrier((p1, p2, there))
    b = lax.ppermute(p1, "sub", swap)
    back, to_p1, to_p2, kept, sums = product(
        False, p2, p1, own, four[blocks:], b, there, conds, pads_sent, ones, rows, sums
    )
    to_p1, from_p2 = collect(back, to_p1, to_p2)
    to_p1, sums = barrier((to_p1, sums))
    from_p1 = lax.ppermute(to_p1, "sub", turned(near))
    all_sums = lax.all_to_all(sums, ("board", "sub"), 0, 0)
    from_p1, from_p2, all_sums = barrier((from_p1, from_p2, all_sums))
    mine, to_other = call(last_part_kernel, [pair, pair], places, kept, from_p1, from_p2)
    there = lax.ppermute(to_other, "sub", swap)
    steps, fine = call(
        steps_kernel, [((3, cases, BR), F32), ((1, 1), jnp.int32)], all_sums, scalar=(1,)
    )
    solution, residual = lax.cond(
        fine[0, 0] == cases,
        lambda: tuple(call(end_kernel, [full, full], right_side, z, image, own, mine, there, steps)),
        lambda: step_by_step(rhs[0], matrix, block_list[0], pad_rows[0], pad_cond[0], sink, precond),
    )
    return (solution[None], residual[None])


def solution(mesh):
    in_specs = (
        P("board", None, "sub"),
        P("board", "sub", None),
        P("board", "sub"),
        P("board", "sub"),
        P("board", "sub"),
        P("board", "sub"),
        P("board", "sub"),
    )
    out_specs = (P("board", None, "sub"), P("board", None, "sub"))
    return jax.shard_map(
        on_device, mesh=mesh, in_specs=in_specs, out_specs=out_specs, check_vma=False
    )
```

time: 240 us -> 49.1 us (0.20)
  blocking collectives: 125 us -> 0 us
  starting transfers between devices: 67.1 us -> 19 us
  local copies, waits for them, and re-layouts: 18.5 us -> 0.04 us
  other arithmetic: 14.1 us -> 0.03 us
  waiting for transfers between devices: 8.2 us -> 19.5 us
  Pallas kernels: 0 us -> 8.54 us
  matrix products: 4.43 us -> 0 us
    psum x3 -> x0, blocking collectives: 125 us -> none  [the longest x1 42.9 us: on_device(): norm_now = lax.psum(case_sums(residual, precon), ('board', 'sub'))]
    ppermute x27 -> x17, starting transfers between devices: 67.1 us -> 15.2 us  [the longest x2 3.54 us: collect(): from_p2 = lax.ppermute(to_p2, 'sub', far)]
    unnamed x42 -> x16, local copies, waits for them, and re-layouts: 8.71 us -> 0.03 us
    pallas_call x0 -> x9, Pallas kernels: none -> 8.54 us  [call(): pl.pallas_call(kernel, in_specs=[space(far, i) for i in range(len(operand...]
    all_to_all x0 -> x1, waiting for transfers between devices: none -> 7.06 us  [on_device(): all_sums = lax.all_to_all(sums, ('board', 'sub'), 0, 0)]
    scatter-add x4 -> x0, other arithmetic: 5.37 us -> none  [the longest x2 2.88 us: on_device(): partial_value = jnp.zeros(apply_blocks.shape, jnp.float32).at[:, shifted_...]
    ppermute x12 -> x0, local copies, waits for them, and re-layouts: 4.8 us -> none  [passed_along(): lax.ppermute(value, axis, [(source, source + steps) for source in range(l...]
    dot_general x2 -> x0, matrix products: 4.43 us -> none  [on_device(): product = jnp.dot(picked, matrix, precision=lax.Precision.HIGHEST)]
  transfers between devices with their start and end apart: 27 -> 18, of which waited for: 6 -> 9; matrix products, arithmetic and copies ran while one was open for 11% -> 0% of each run, Pallas kernels for 0% -> 5%
where the time goes in v1:
time: 49.1 us; the launch traced here: 48.8 us
  waiting for transfers between devices  19.5 us (40%)
  starting transfers between devices  19 us (39%)
  Pallas kernels  8.54 us (17%)
  between operations  1.46 us (3%)
    pallas_call x9, Pallas kernels, call(): pl.pallas_call(kernel, in_specs=[space(far, i) for i in range(len(operand...  8.54 us
    all_to_all x1, waiting for transfers between devices, on_device(): all_sums = lax.all_to_all(sums, ('board', 'sub'), 0, 0)  7.06 us
    all_to_all x1, starting transfers between devices, on_device(): all_sums = lax.all_to_all(sums, ('board', 'sub'), 0, 0)  3.72 us
    ppermute x2, starting transfers between devices, collect(): from_p2 = lax.ppermute(to_p2, 'sub', far)  3.54 us
    ppermute x1, starting transfers between devices, on_device(): p1 = lax.ppermute(jnp.concatenate([z, other]), 'sub', near)  2.83 us
    ppermute x2, waiting for transfers between devices, collect(): from_p2 = lax.ppermute(to_p2, 'sub', far)  2.59 us
    ppermute x1, waiting for transfers between devices, on_device(): conds = lax.ppermute(pads_sent, 'board', across)  2.26 us
    ppermute x1, waiting for transfers between devices, on_device(): there = lax.ppermute(values, 'board', across)  2.22 us
  transfers between devices with their start and end apart: 18, of which 9 were waited for; matrix products, arithmetic and copies ran while one was open for 0% of the time, Pallas kernels for 5%

profile of v1, /device:TPU:0, one launch (start us, length us, event | category | flops | bytes accessed | tf_op | source)
XLA Modules:
  0.0 48.8 jit_solution(8134102273117037822)
XLA Ops:
  0.6 1.0 %shard_map.91 = (f32[32,256]{1,0:T(8,128)S(1)}, f32[2,1,256]{2,1,0:T(1,128)S(1)}, f32[2,32,128]{2,1,0:T(8,128)S(1)}, bf16[256,64]{1,0:T(8,128)(2,1)S(1)}, f32[40,128]{1,0:T(8,128)S(1)}) custom-call(f32[32,256]{1,0:T(8,128)} %bitcast.152, f32[1,256]{1,0:T(1,128)} %precond.1, f32[1,256]{1,0:T(1,128)} %sink.1, s32[1,64]{1,0:T(1,128)} %pads.1, f32[1,64]{1,0:T(1,128)} %cond.11), custom_call_target="tpu_custom_call" | custom-call | tf_op jit(solution)/shard_map/pallas_call | solution.py:324
  2.1 0.9 %collective-permute-done.27.refs_7_ = f32[2,32,128]{2,1,0:T(8,128)S(1)} collective-permute-done((f32[2,32,128]{2,1,0:T(8,128)S(1)}, f32[2,32,128]{2,1,0:T(8,128)S(1)}, u32[]{:S(2)}, u32[]{:S(2)}) %collective-permute-start.27) | collective-permute-done | bytes 32800 | tf_op jit(solution)/shard_map/ppermute | solution.py:381
  3.0 2.8 %collective-permute-start.28 = (f32[4,32,128]{2,1,0:T(8,128)S(1)}, f32[4,32,128]{2,1,0:T(8,128)S(1)}, u32[]{:S(2)}, u32[]{:S(2)}) collective-permute-start(f32[4,32,128]{2,1,0:T(8,128)S(1)} %pad_maximum_fusion), channel_id=1, source_target_pairs={{0,2},{1,0},{2,4},{3,1},{4,6},{5,3},{6,8},{7,5},{8,10},{9,7},{10,1... | collective-permute-start | bytes 196616 | tf_op jit(solution)/shard_map/ppermute | solution.py:384
  5.8 1.5 %collective-permute-start.29 = (f32[2,32,128]{2,1,0:T(8,128)S(1)}, f32[2,32,128]{2,1,0:T(8,128)S(1)}, u32[]{:S(2)}, u32[]{:S(2)}) collective-permute-start(f32[2,32,128]{2,1,0:T(8,128)S(1)} %get-tuple-element.94.refs_6_.z), channel_id=1, source_target_pairs={{0,2},{1,4},{2,0},{3,6},{4,1},{5,8},{6,3},{7,10},{8,5},{9,12},{10,... | collective-permute-start | bytes 98312 | tf_op jit(solution)/shard_map/ppermute | solution.py:382
  7.4 1.5 %collective-permute-start.30 = (f32[40,128]{1,0:T(8,128)S(1)}, f32[40,128]{1,0:T(8,128)S(1)}, u32[]{:S(2)}, u32[]{:S(2)}) collective-permute-start(f32[40,128]{1,0:T(8,128)S(1)} %get-tuple-element.95.refs_11_), channel_id=1, source_target_pairs={{0,16},{16,0},{1,17},{17,1},{2,18},{18,2},{3,19},{19,3},{4,20},{20... | collective-permute-start | bytes 61448 | tf_op jit(solution)/shard_map/ppermute | solution.py:383
  8.9 2.3 %collective-permute-done.30.refs_9_.refs_10_ = f32[40,128]{1,0:T(8,128)S(1)} collective-permute-done((f32[40,128]{1,0:T(8,128)S(1)}, f32[40,128]{1,0:T(8,128)S(1)}, u32[]{:S(2)}, u32[]{:S(2)}) %collective-permute-start.30) | collective-permute-done | bytes 20512 | tf_op jit(solution)/shard_map/ppermute | solution.py:383
  11.2 1.8 %shard_map.90 = (bf16[768,768]{1,0:T(8,128)(2,1)S(1)}, bf16[768,768]{1,0:T(8,128)(2,1)S(1)}, bf16[768,768]{1,0:T(8,128)(2,1)S(1)}, f32[86,8,128]{2,1,0:T(8,128)S(1)}) custom-call(f32[768,768]{1,0:T(8,128)} %bitcast.146, s32[1,6]{1,0:T(1,128)} %blocks.1), custom_call_target="tpu_custom_call" | custom-call | tf_op jit(solution)/shard_map/pallas_call | solution.py:324
  13.0 0.8 %shard_map.92 = (f32[4,32,128]{2,1,0:T(8,128)S(1)}, f32[4,32,128]{2,1,0:T(8,128)S(1)}, f32[2,32,128]{2,1,0:T(8,128)S(1)}, f32[4,32,128]{2,1,0:T(8,128)S(1)}) custom-call(f32[86,8,128]{2,1,0:T(8,128)S(1)} %get-tuple-element.90.refs_0_.places, bf16[768,768]{1,0:T(8,128)(2,1)S(1)} %get-tuple-element.91.refs_1_, bf16[768,768]{1,0:T(8,128)(2,1)S(1)} %get-tuple-element.92.refs_2_, ...), custom_call_target="tpu_custom_call" | custom-call | tf_op jit(solution)/shard_map/pallas_call | solution.py:324
  14.3 0.9 %collective-permute-done.32 = f32[4,32,128]{2,1,0:T(8,128)S(1)} collective-permute-done((f32[4,32,128]{2,1,0:T(8,128)S(1)}, f32[4,32,128]{2,1,0:T(8,128)S(1)}, u32[]{:S(2)}, u32[]{:S(2)}) %collective-permute-start.32) | collective-permute-done | bytes 65568 | tf_op jit(solution)/shard_map/ppermute | solution.py:378
  15.7 1.7 %collective-permute-start.34 = (f32[2,32,128]{2,1,0:T(8,128)S(1)}, f32[2,32,128]{2,1,0:T(8,128)S(1)}, u32[]{:S(2)}, u32[]{:S(2)}) collective-permute-start(f32[2,32,128]{2,1,0:T(8,128)S(1)} %get-tuple-element.104), channel_id=1, source_target_pairs={{0,2},{1,4},{2,0},{3,6},{4,1},{5,8},{6,3},{7,10},{8,5},{9,12},{10,... | collective-permute-start | bytes 98312 | tf_op jit(solution)/shard_map/ppermute | solution.py:377
  17.3 2.6 %collective-permute-done.34.from_p2 = f32[2,32,128]{2,1,0:T(8,128)S(1)} collective-permute-done((f32[2,32,128]{2,1,0:T(8,128)S(1)}, f32[2,32,128]{2,1,0:T(8,128)S(1)}, u32[]{:S(2)}, u32[]{:S(2)}) %collective-permute-start.34) | collective-permute-done | bytes 32800 | tf_op jit(solution)/shard_map/ppermute | solution.py:377
  20.0 1.2 %collective-permute-done.35.there = f32[5,32,128]{2,1,0:T(8,128)S(1)} collective-permute-done((f32[5,32,128]{2,1,0:T(8,128)S(1)}, f32[5,32,128]{2,1,0:T(8,128)S(1)}, u32[]{:S(2)}, u32[]{:S(2)}) %collective-permute-start.35) | collective-permute-done | bytes 81952 | tf_op jit(solution)/shard_map/ppermute | solution.py:391
  21.9 1.4 %collective-permute-start.36 = (f32[4,32,128]{2,1,0:T(8,128)S(1)}, f32[4,32,128]{2,1,0:T(8,128)S(1)}, u32[]{:S(2)}, u32[]{:S(2)}) collective-permute-start(f32[4,32,128]{2,1,0:T(8,128)S(1)} %get-tuple-element.106), channel_id=1, source_target_pairs={{0,2},{1,0},{2,4},{3,1},{4,6},{5,3},{6,8},{7,5},{8,10},{9,7},{10,1... | collective-permute-start | bytes 196616 | tf_op jit(solution)/shard_map/ppermute | solution.py:395
  23.3 0.9 %collective-permute-start.37 = (f32[2,32,128]{2,1,0:T(8,128)S(1)}, f32[2,32,128]{2,1,0:T(8,128)S(1)}, u32[]{:S(2)}, u32[]{:S(2)}) collective-permute-start(f32[2,32,128]{2,1,0:T(8,128)S(1)} %get-tuple-element.107.refs_6_), channel_id=1, source_target_pairs={{0,2},{1,4},{2,0},{3,6},{4,1},{5,8},{6,3},{7,10},{8,5},{9,12},{10,... | collective-permute-start | bytes 98312 | tf_op jit(solution)/shard_map/ppermute | solution.py:396
  24.2 1.5 %collective-permute-start.38 = (f32[32,128]{1,0:T(8,128)S(1)}, f32[32,128]{1,0:T(8,128)S(1)}, u32[]{:S(2)}, u32[]{:S(2)}) collective-permute-start(f32[32,128]{1,0:T(8,128)S(1)} %get-tuple-element.108), channel_id=1, source_target_pairs={{0,16},{16,0},{1,17},{17,1},{2,18},{18,2},{3,19},{19,3},{4,20},{20... | collective-permute-start | bytes 49160 | tf_op jit(solution)/shard_map/ppermute | solution.py:397
  25.8 2.2 %collective-permute-done.38.refs_9_ = f32[32,128]{1,0:T(8,128)S(1)} collective-permute-done((f32[32,128]{1,0:T(8,128)S(1)}, f32[32,128]{1,0:T(8,128)S(1)}, u32[]{:S(2)}, u32[]{:S(2)}) %collective-permute-start.38) | collective-permute-done | bytes 16416 | tf_op jit(solution)/shard_map/ppermute | solution.py:397
  28.0 1.2 %collective-permute-done.39.refs_8_ = f32[4,32,128]{2,1,0:T(8,128)S(1)} collective-permute-done((f32[4,32,128]{2,1,0:T(8,128)S(1)}, f32[4,32,128]{2,1,0:T(8,128)S(1)}, u32[]{:S(2)}, u32[]{:S(2)}) %collective-permute-start.39) | collective-permute-done | bytes 65568 | tf_op jit(solution)/shard_map/ppermute | solution.py:399
  29.3 1.5 %shard_map.95 = (f32[4,32,128]{2,1,0:T(8,128)S(1)}, f32[4,32,128]{2,1,0:T(8,128)S(1)}, f32[2,32,128]{2,1,0:T(8,128)S(1)}, f32[4,32,128]{2,1,0:T(8,128)S(1)}, f32[32,1,128]{2,1,0:T(1,128)}) custom-call(f32[86,8,128]{2,1,0:T(8,128)S(1)} %get-tuple-element.90.refs_0_.places, bf16[768,768]{1,0:T(8,128)(2,1)S(1)} %get-tuple-element.91.refs_1_, ...), custom_call_target="tpu_custom_call" | custom-call | tf_op jit(solution)/shard_map/pallas_call | solution.py:324
  30.9 1.1 %collective-permute-done.40 = f32[4,32,128]{2,1,0:T(8,128)S(1)} collective-permute-done((f32[4,32,128]{2,1,0:T(8,128)S(1)}, f32[4,32,128]{2,1,0:T(8,128)S(1)}, u32[]{:S(2)}, u32[]{:S(2)}) %collective-permute-start.40) | collective-permute-done | bytes 65568 | tf_op jit(solution)/shard_map/ppermute | solution.py:378
  32.2 1.9 %collective-permute-start.42 = (f32[2,32,128]{2,1,0:T(8,128)S(1)}, f32[2,32,128]{2,1,0:T(8,128)S(1)}, u32[]{:S(2)}, u32[]{:S(2)}) collective-permute-start(f32[2,32,128]{2,1,0:T(8,128)S(1)} %get-tuple-element.117), channel_id=1, source_target_pairs={{0,2},{1,4},{2,0},{3,6},{4,1},{5,8},{6,3},{7,10},{8,5},{9,12},{10,... | collective-permute-start | bytes 98312 | tf_op jit(solution)/shard_map/ppermute | solution.py:377
  34.1 3.7 %all-to-all-start = ((f32[32,1,128]{2,1,0:T(1,128)}), f32[32,1,128]{2,1,0:T(1,128)S(1)}, u32[]{:S(2)}, u32[]{:S(2)}) async-start(f32[32,1,128]{2,1,0:T(1,128)} %get-tuple-element.118), calls=%async_computation | async-start | bytes 32768 | tf_op jit(solution)/shard_map/all_to_all | solution.py:406
  37.8 7.1 %all-to-all-done.sums = f32[32,1,128]{2,1,0:T(1,128)S(1)} async-done(((f32[32,1,128]{2,1,0:T(1,128)}), f32[32,1,128]{2,1,0:T(1,128)S(1)}, u32[]{:S(2)}, u32[]{:S(2)}) %all-to-all-start) | async-done | bytes 16416 | tf_op jit(solution)/shard_map/all_to_all | solution.py:406
  47.0 1.8 %conditional.1 = (f32[1,32,256]{2,1,0:T(8,128)}, f32[1,32,256]{2,1,0:T(8,128)}) conditional(s32[]{:T(128)} %bitcast.42, (f32[1,32,256]{2,1,0:T(8,128)S(1)}, f32[1,256]{1,0:T(1,128)S(1)}, s32[1,6]{1,0:T(1,128)S(1)}, f32[768,768]{1,0:T(8,128)}, f32[1,256]{1,0:T(1,128)S(1)}, /*index=5*/s32[1,64]{1,0:T(1,128)S(1)}, f32[1,64]{1,0:T(1,128)}) %tuple.82, ...), branch_computations={%region_0.15_spmd, %region_13.16_spmd} | conditional | flops 453434400 | bytes 21824418 | solution.py:413
  47.2 1.5 %branch_1_fun.1 = (f32[32,256]{1,0:T(8,128)}, f32[32,256]{1,0:T(8,128)}) custom-call(f32[32,256]{1,0:T(8,128)} %get-tuple-element.41.rhs, f32[2,32,128]{2,1,0:T(8,128)} %get-tuple-element.42.z, f32[32,256]{1,0:T(8,128)} %get-tuple-element.43.image, f32[2,32,128]{2,1,0:T(8,128)} %get-tuple-element.44.scaled, f32[2,32,128]{2,1,0:T(8,128)} %get-tuple-element.45.mine, ...), custom_call_target="tpu_custom_call" | custom-call | tf_op jit(solution)/shard_map/cond/branch_1_fun/pallas_call | solution.py:324
  (42 shorter events, 4.1 us)
Async XLA Ops:
  1.6 19.7 %copy-start = (f32[2,32,128]{2,1,0:T(8,128)}, f32[2,32,128]{2,1,0:T(8,128)S(1)}, u32[]{:S(2)}) copy-start(f32[2,32,128]{2,1,0:T(8,128)S(1)} %get-tuple-element.94.refs_6_.z) | copy-start | bytes 98308
  1.6 19.7 %copy-start.3 = (f32[32,256]{1,0:T(8,128)}, f32[32,256]{1,0:T(8,128)S(1)}, u32[]{:S(2)}) copy-start(f32[32,256]{1,0:T(8,128)S(1)} %get-tuple-element.105.rhs) | copy-start | bytes 98308
  1.6 1.4 %collective-permute-start.27 = (f32[2,32,128]{2,1,0:T(8,128)S(1)}, f32[2,32,128]{2,1,0:T(8,128)S(1)}, u32[]{:S(2)}, u32[]{:S(2)}) collective-permute-start(f32[2,32,128]{2,1,0:T(8,128)S(1)} %get-tuple-element.94.refs_6_.z), channel_id=1, source_target_pairs={{0,1},{1,0},{2,3},{3,2},{4,5},{5,4},{6,7},{7,6},{8,9},{9,8},{10,11... | collective-permute-start | bytes 98312 | tf_op jit(solution)/shard_map/ppermute | solution.py:381
  3.0 8.2 %collective-permute-start.28 = (f32[4,32,128]{2,1,0:T(8,128)S(1)}, f32[4,32,128]{2,1,0:T(8,128)S(1)}, u32[]{:S(2)}, u32[]{:S(2)}) collective-permute-start(f32[4,32,128]{2,1,0:T(8,128)S(1)} %pad_maximum_fusion), channel_id=1, source_target_pairs={{0,2},{1,0},{2,4},{3,1},{4,6},{5,3},{6,8},{7,5},{8,10},{9,7},{10,1... | collective-permute-start | bytes 196616 | tf_op jit(solution)/shard_map/ppermute | solution.py:384
  5.8 5.3 %collective-permute-start.29 = (f32[2,32,128]{2,1,0:T(8,128)S(1)}, f32[2,32,128]{2,1,0:T(8,128)S(1)}, u32[]{:S(2)}, u32[]{:S(2)}) collective-permute-start(f32[2,32,128]{2,1,0:T(8,128)S(1)} %get-tuple-element.94.refs_6_.z), channel_id=1, source_target_pairs={{0,2},{1,4},{2,0},{3,6},{4,1},{5,8},{6,3},{7,10},{8,5},{9,12},{10,... | collective-permute-start | bytes 98312 | tf_op jit(solution)/shard_map/ppermute | solution.py:382
  7.4 3.8 %collective-permute-start.30 = (f32[40,128]{1,0:T(8,128)S(1)}, f32[40,128]{1,0:T(8,128)S(1)}, u32[]{:S(2)}, u32[]{:S(2)}) collective-permute-start(f32[40,128]{1,0:T(8,128)S(1)} %get-tuple-element.95.refs_11_), channel_id=1, source_target_pairs={{0,16},{16,0},{1,17},{17,1},{2,18},{18,2},{3,19},{19,3},{4,20},{20... | collective-permute-start | bytes 61448 | tf_op jit(solution)/shard_map/ppermute | solution.py:383
  11.2 1.8 %collective-permute-start.31 = (f32[4,32,128]{2,1,0:T(8,128)S(1)}, f32[4,32,128]{2,1,0:T(8,128)S(1)}, u32[]{:S(2)}, u32[]{:S(2)}) collective-permute-start(f32[4,32,128]{2,1,0:T(8,128)S(1)} %collective-permute-done.28.refs_5_), channel_id=1, source_target_pairs={{0,1},{1,0},{2,3},{3,2},{4,5},{5,4},{6,7},{7,6},{8,9},{9,8},{10,11... | collective-permute-start | bytes 196616 | tf_op jit(solution)/shard_map/ppermute | solution.py:386
  13.8 1.5 %collective-permute-start.32 = (f32[4,32,128]{2,1,0:T(8,128)S(1)}, f32[4,32,128]{2,1,0:T(8,128)S(1)}, u32[]{:S(2)}, u32[]{:S(2)}) collective-permute-start(f32[4,32,128]{2,1,0:T(8,128)S(1)} %get-tuple-element.103), channel_id=1, source_target_pairs={{0,1},{1,0},{2,3},{3,2},{4,5},{5,4},{6,7},{7,6},{8,9},{9,8},{10,11... | collective-permute-start | bytes 196616 | tf_op jit(solution)/shard_map/ppermute | solution.py:378
  15.2 4.7 %collective-permute-start.33 = (f32[4,32,128]{2,1,0:T(8,128)S(1)}, f32[4,32,128]{2,1,0:T(8,128)S(1)}, u32[]{:S(2)}, u32[]{:S(2)}) collective-permute-start(f32[4,32,128]{2,1,0:T(8,128)S(1)} %add.108), channel_id=1, source_target_pairs={{2,0},{0,1},{4,2},{1,3},{6,4},{3,5},{8,6},{5,7},{10,8},{7,9},{12,1... | collective-permute-start | bytes 196616 | tf_op jit(solution)/shard_map/ppermute | solution.py:389
  15.7 4.3 %collective-permute-start.34 = (f32[2,32,128]{2,1,0:T(8,128)S(1)}, f32[2,32,128]{2,1,0:T(8,128)S(1)}, u32[]{:S(2)}, u32[]{:S(2)}) collective-permute-start(f32[2,32,128]{2,1,0:T(8,128)S(1)} %get-tuple-element.104), channel_id=1, source_target_pairs={{0,2},{1,4},{2,0},{3,6},{4,1},{5,8},{6,3},{7,10},{8,5},{9,12},{10,... | collective-permute-start | bytes 98312 | tf_op jit(solution)/shard_map/ppermute | solution.py:377
  19.9 1.3 %collective-permute-start.35 = (f32[5,32,128]{2,1,0:T(8,128)S(1)}, f32[5,32,128]{2,1,0:T(8,128)S(1)}, u32[]{:S(2)}, u32[]{:S(2)}) collective-permute-start(f32[5,32,128]{2,1,0:T(8,128)S(1)} %shard_map.93.part), channel_id=1, source_target_pairs={{0,1},{1,0},{2,3},{3,2},{4,5},{5,4},{6,7},{7,6},{8,9},{9,8},{10,11... | collective-permute-start | bytes 245768 | tf_op jit(solution)/shard_map/ppermute | solution.py:391
  21.9 6.1 %collective-permute-start.36 = (f32[4,32,128]{2,1,0:T(8,128)S(1)}, f32[4,32,128]{2,1,0:T(8,128)S(1)}, u32[]{:S(2)}, u32[]{:S(2)}) collective-permute-start(f32[4,32,128]{2,1,0:T(8,128)S(1)} %get-tuple-element.106), channel_id=1, source_target_pairs={{0,2},{1,0},{2,4},{3,1},{4,6},{5,3},{6,8},{7,5},{8,10},{9,7},{10,1... | collective-permute-start | bytes 196616 | tf_op jit(solution)/shard_map/ppermute | solution.py:395
  23.3 4.7 %collective-permute-start.37 = (f32[2,32,128]{2,1,0:T(8,128)S(1)}, f32[2,32,128]{2,1,0:T(8,128)S(1)}, u32[]{:S(2)}, u32[]{:S(2)}) collective-permute-start(f32[2,32,128]{2,1,0:T(8,128)S(1)} %get-tuple-element.107.refs_6_), channel_id=1, source_target_pairs={{0,2},{1,4},{2,0},{3,6},{4,1},{5,8},{6,3},{7,10},{8,5},{9,12},{10,... | collective-permute-start | bytes 98312 | tf_op jit(solution)/shard_map/ppermute | solution.py:396
  24.2 3.7 %collective-permute-start.38 = (f32[32,128]{1,0:T(8,128)S(1)}, f32[32,128]{1,0:T(8,128)S(1)}, u32[]{:S(2)}, u32[]{:S(2)}) collective-permute-start(f32[32,128]{1,0:T(8,128)S(1)} %get-tuple-element.108), channel_id=1, source_target_pairs={{0,16},{16,0},{1,17},{17,1},{2,18},{18,2},{3,19},{19,3},{4,20},{20... | collective-permute-start | bytes 49160 | tf_op jit(solution)/shard_map/ppermute | solution.py:397
  28.0 1.3 %collective-permute-start.39 = (f32[4,32,128]{2,1,0:T(8,128)S(1)}, f32[4,32,128]{2,1,0:T(8,128)S(1)}, u32[]{:S(2)}, u32[]{:S(2)}) collective-permute-start(f32[4,32,128]{2,1,0:T(8,128)S(1)} %collective-permute-done.36.refs_5_), channel_id=1, source_target_pairs={{0,1},{1,0},{2,3},{3,2},{4,5},{5,4},{6,7},{7,6},{8,9},{9,8},{10,11... | collective-permute-start | bytes 196616 | tf_op jit(solution)/shard_map/ppermute | solution.py:399
  29.2 17.7 %copy-start.5 = (f32[1,256]{1,0:T(1,128)S(1)}, f32[1,256]{1,0:T(1,128)}, u32[]{:S(2)}) copy-start(f32[1,256]{1,0:T(1,128)} %precond.1) | copy-start | bytes 3076
  29.2 17.7 %copy-start.6 = (f32[1,256]{1,0:T(1,128)S(1)}, f32[1,256]{1,0:T(1,128)}, u32[]{:S(2)}) copy-start(f32[1,256]{1,0:T(1,128)} %sink.1) | copy-start | bytes 3076
  29.3 17.7 %copy-start.12 = (s32[1,6]{1,0:T(1,128)S(1)}, s32[1,6]{1,0:T(1,128)}, u32[]{:S(2)}) copy-start(s32[1,6]{1,0:T(1,128)} %blocks.1) | copy-start | bytes 76
  29.3 17.7 %copy-start.13 = (s32[1,64]{1,0:T(1,128)S(1)}, s32[1,64]{1,0:T(1,128)}, u32[]{:S(2)}) copy-start(s32[1,64]{1,0:T(1,128)} %pads.1) | copy-start | bytes 772
  30.7 1.3 %collective-permute-start.40 = (f32[4,32,128]{2,1,0:T(8,128)S(1)}, f32[4,32,128]{2,1,0:T(8,128)S(1)}, u32[]{:S(2)}, u32[]{:S(2)}) collective-permute-start(f32[4,32,128]{2,1,0:T(8,128)S(1)} %get-tuple-element.114), channel_id=1, source_target_pairs={{0,1},{1,0},{2,3},{3,2},{4,5},{5,4},{6,7},{7,6},{8,9},{9,8},{10,11... | collective-permute-start | bytes 196616 | tf_op jit(solution)/shard_map/ppermute | solution.py:378
  32.0 12.9 %collective-permute-start.41 = (f32[4,32,128]{2,1,0:T(8,128)S(1)}, f32[4,32,128]{2,1,0:T(8,128)S(1)}, u32[]{:S(2)}, u32[]{:S(2)}) collective-permute-start(f32[4,32,128]{2,1,0:T(8,128)S(1)} %add.109), channel_id=1, source_target_pairs={{2,0},{0,1},{4,2},{1,3},{6,4},{3,5},{8,6},{5,7},{10,8},{7,9},{12,1... | collective-permute-start | bytes 196616 | tf_op jit(solution)/shard_map/ppermute | solution.py:405
  32.2 5.6 %collective-permute-start.42 = (f32[2,32,128]{2,1,0:T(8,128)S(1)}, f32[2,32,128]{2,1,0:T(8,128)S(1)}, u32[]{:S(2)}, u32[]{:S(2)}) collective-permute-start(f32[2,32,128]{2,1,0:T(8,128)S(1)} %get-tuple-element.117), channel_id=1, source_target_pairs={{0,2},{1,4},{2,0},{3,6},{4,1},{5,8},{6,3},{7,10},{8,5},{9,12},{10,... | collective-permute-start | bytes 98312 | tf_op jit(solution)/shard_map/ppermute | solution.py:377
  34.1 10.8 %all-to-all-start = ((f32[32,1,128]{2,1,0:T(1,128)}), f32[32,1,128]{2,1,0:T(1,128)S(1)}, u32[]{:S(2)}, u32[]{:S(2)}) async-start(f32[32,1,128]{2,1,0:T(1,128)} %get-tuple-element.118), calls=%async_computation | async-start | bytes 32768 | tf_op jit(solution)/shard_map/all_to_all | solution.py:406
  45.5 1.4 %collective-permute-start.43 = (f32[2,32,128]{2,1,0:T(8,128)S(1)}, f32[2,32,128]{2,1,0:T(8,128)S(1)}, u32[]{:S(2)}, u32[]{:S(2)}) collective-permute-start(f32[2,32,128]{2,1,0:T(8,128)S(1)} %get-tuple-element.126), channel_id=1, source_target_pairs={{0,1},{1,0},{2,3},{3,2},{4,5},{5,4},{6,7},{7,6},{8,9},{9,8},{10,11... | collective-permute-start | bytes 98312 | tf_op jit(solution)/shard_map/ppermute | solution.py:409
  (2 other events, 28.0 us)

commit v2 on v1

--- a/solution.py
+++ b/solution.py
@@ -292,9 +292,9 @@
     mine_out[...], other_out[...] = gather_parts(places, kept, from_p1, from_p2)
 
 
-def steps_kernel(sums, steps, fine):
+def steps_kernel(sums, steps):
     cases = steps.shape[1]
-    total = jnp.sum(sums[...], axis=0)
+    total = jnp.sum(sums[...], axis=0)[:1]
     norm, curve, cross, energy = [as_column(total, slot, cases) for slot in range(4)]
     alpha = norm / curve
     fresh = alpha * alpha * cross - norm
@@ -303,12 +303,12 @@
     bend = terms[0] - terms[1] + terms[2]
     good = (norm > 1e-30) & (energy < 1e30) & (cross < 1e30) & (curve > 0.0) & (fresh > 0.02 * norm)
     good = good & (bend > 0.004 * (terms[0] + terms[1] + terms[2]))
-    fine[0, 0] = jnp.sum(jnp.where(good, 1, 0))
-    for i, value in enumerate((alpha, grown, fresh / bend)):
+    good = jnp.where(good, 1.0, 0.0)
+    for i, value in enumerate((alpha, grown, fresh / bend, good)):
         steps[i] = jnp.broadcast_to(value, steps.shape[1:])
 
 
-def end_kernel(rhs, z, image, scaled, mine, there, steps, solution, residual):
+def end_kernel(rhs, z, image, scaled, mine, there, steps, spare_one, spare_two, solution, residual, sems):
     alpha, grown, step = [wide([steps[i], steps[i]]) for i in range(3)]
     start = wide(z)
     direction = grown * start - alpha * wide(scaled)
@@ -316,17 +316,29 @@
     second = wide(mine[...] + there[...])
     residual[...] = rhs[...] - alpha * image[...] - step * (grown * image[...] - alpha * second)
 
-
-def call(kernel, outs, *operands, scratch=(), far=(), scalar=()):
-    def space(outside, i, smem=()):
-        return pl.BlockSpec(memory_space=pl.ANY if i in outside else pltpu.SMEM if i in smem else pltpu.VMEM)
+    @pl.when(jnp.min(steps[3]) < 0.5)
+    def _():
+        copies = [
+            pltpu.make_async_copy(spare_one, solution, sems.at[0]),
+            pltpu.make_async_copy(spare_two, residual, sems.at[1]),
+        ]
+        for copy in copies:
+            copy.start()
+        for copy in copies:
+            copy.wait()
+
+
+def call(kernel, outs, *operands, scratch=(), far=(), far_outs=(), smem=(), smem_outs=(), cost=None):
+    def space(outside, scalar, i):
+        return pl.BlockSpec(memory_space=pl.ANY if i in outside else pltpu.SMEM if i in scalar else pltpu.VMEM)
 
     return pl.pallas_call(
         kernel,
-        in_specs=[space(far, i) for i in range(len(operands))],
-        out_specs=[space((), i, scalar) for i in range(len(outs))],
+        in_specs=[space(far, smem, i) for i in range(len(operands))],
+        out_specs=[space(far_outs, smem_outs, i) for i in range(len(outs))],
         out_shape=[jax.ShapeDtypeStruct(shape, kind) for shape, kind in outs],
         scratch_shapes=list(scratch),
+        cost_estimate=cost,
         compiler_params=pltpu.CompilerParams(vmem_limit_bytes=32 * 1024 * 1024),
     )(*operands)
 
@@ -369,7 +381,7 @@
     def product(first, *operands):
         return call(
             lambda *refs: product_kernel(first, *refs),
-            [both, both, pair, both] + ([] if first else [((everyone, 1, BR), F32)]),
+            [both, both, pair, both] + ([] if first else [((everyone, 8, BR), F32)]),
             places, high, middle, low, *operands,
         )
 
@@ -382,7 +394,7 @@
     p2 = lax.ppermute(z, "sub", far)
     conds = lax.ppermute(pads_sent, "board", across)
     p1 = lax.ppermute(jnp.concatenate([z, other]), "sub", near)
-    p1, p2, conds = barrier((p1, p2, conds))
+    p1, p2, conds, high, middle, low, places = barrier((p1, p2, conds, high, middle, low, places))
     b = lax.ppermute(p1, "sub", swap)
     back, to_p1, to_p2, kept = product(True, p2, p1, z, other, b, conds, conds, pads_sent, ones, rows)
     to_p1, from_p2 = collect(back, to_p1, to_p2)
@@ -401,19 +413,22 @@
         False, p2, p1, own, four[blocks:], b, there, conds, pads_sent, ones, rows, sums
     )
     to_p1, from_p2 = collect(back, to_p1, to_p2)
-    to_p1, sums = barrier((to_p1, sums))
     from_p1 = lax.ppermute(to_p1, "sub", turned(near))
     all_sums = lax.all_to_all(sums, ("board", "sub"), 0, 0)
-    from_p1, from_p2, all_sums = barrier((from_p1, from_p2, all_sums))
     mine, to_other = call(last_part_kernel, [pair, pair], places, kept, from_p1, from_p2)
     there = lax.ppermute(to_other, "sub", swap)
-    steps, fine = call(
-        steps_kernel, [((3, cases, BR), F32), ((1, 1), jnp.int32)], all_sums, scalar=(1,)
-    )
-    solution, residual = lax.cond(
-        fine[0, 0] == cases,
-        lambda: tuple(call(end_kernel, [full, full], right_side, z, image, own, mine, there, steps)),
+    all_sums, there = barrier((all_sums, there))
+    (steps,) = call(steps_kernel, [((4, cases, BR), F32)], all_sums)
+    spare = lax.cond(
+        jnp.min(steps[3]) > 0.5,
+        lambda: tuple(call(lambda *refs: None, [full, full], far_outs=range(2))),
         lambda: step_by_step(rhs[0], matrix, block_list[0], pad_rows[0], pad_cond[0], sink, precond),
+    )
+    solution, residual = call(
+        end_kernel,
+        [full, full],
+        right_side, z, image, own, mine, there, steps, *spare,
+        far=(7, 8), scratch=[semaphores((2,))],
     )
     return (solution[None], residual[None])
 

time: 49.1 us -> 44.4 us (0.904)
  waiting for transfers between devices: 19.5 us -> 16.2 us
  Pallas kernels: 8.54 us -> 6.12 us
  other arithmetic: 0.03 us -> 0.63 us
    all_to_all x1, waiting for transfers between devices: 7.06 us -> 0.01 us  [on_device(): all_sums = lax.all_to_all(sums, ('board', 'sub'), 0, 0)]
    ppermute x2, waiting for transfers between devices: 2.59 us -> 5.53 us  [collect(): from_p2 = lax.ppermute(to_p2, 'sub', far)]
    pallas_call x9 -> x10, Pallas kernels: 8.54 us -> 6.12 us  [call(): pl.pallas_call(kernel, in_specs=[space(far, smem, i) for i in range(len(o...]
    ppermute x1, waiting for transfers between devices: 2.26 us -> 0.48 us  [on_device(): conds = lax.ppermute(pads_sent, 'board', across)]
    ppermute x1, starting transfers between devices: 0.01 us -> 1.34 us  [on_device(): there = lax.ppermute(to_other, 'sub', swap)]
    ppermute x2, waiting for transfers between devices: 1.24 us -> 2.48 us  [on_device(): b = lax.ppermute(p1, 'sub', swap)]
    ppermute x1, waiting for transfers between devices: 0.01 us -> 0.86 us  [on_device(): there = lax.ppermute(to_other, 'sub', swap)]
    all_to_all x1, starting transfers between devices: 3.72 us -> 2.95 us  [on_device(): all_sums = lax.all_to_all(sums, ('board', 'sub'), 0, 0)]
  transfers between devices with their start and end apart: 18 -> 18, of which waited for: 9 -> 11; matrix products, arithmetic and copies ran while one was open for 0% -> 0% of each run, Pallas kernels for 5% -> 4%
where the time goes in v2:
time: 44.4 us; the launch traced here: 44.2 us
  starting transfers between devices  19.3 us (43%)
  waiting for transfers between devices  16.2 us (36%)
  Pallas kernels  6.12 us (14%)
  between operations  1.64 us (4%)
  other arithmetic  0.63 us (1%)
    pallas_call x10, Pallas kernels, call(): pl.pallas_call(kernel, in_specs=[space(far, smem, i) for i in range(len(o...  6.12 us
    ppermute x2, waiting for transfers between devices, collect(): from_p2 = lax.ppermute(to_p2, 'sub', far)  5.53 us
    ppermute x2, starting transfers between devices, collect(): from_p2 = lax.ppermute(to_p2, 'sub', far)  3.64 us
    all_to_all x1, starting transfers between devices, on_device(): all_sums = lax.all_to_all(sums, ('board', 'sub'), 0, 0)  2.95 us
    ppermute x1, starting transfers between devices, on_device(): p1 = lax.ppermute(jnp.concatenate([z, other]), 'sub', near)  2.83 us
    ppermute x1, waiting for transfers between devices, on_device(): there = lax.ppermute(values, 'board', across)  2.69 us
    ppermute x2, waiting for transfers between devices, on_device(): b = lax.ppermute(p1, 'sub', swap)  2.48 us
    ppermute x2, waiting for transfers between devices, collect(): to_p1 = to_p1 + lax.ppermute(back, 'sub', swap)  2.1 us
  transfers between devices with their start and end apart: 18, of which 11 were waited for; matrix products, arithmetic and copies ran while one was open for 0% of the time, Pallas kernels for 4%

profile of v2, /device:TPU:0, one launch (start us, length us, event | category | flops | bytes accessed | tf_op | source)
XLA Modules:
  0.0 44.2 jit_solution(9635236925106643407)
XLA Ops:
  0.6 1.0 %shard_map.86 = (f32[32,256]{1,0:T(8,128)S(1)}, f32[2,1,256]{2,1,0:T(1,128)S(1)}, f32[2,32,128]{2,1,0:T(8,128)S(1)}, bf16[256,64]{1,0:T(8,128)(2,1)S(1)}, f32[40,128]{1,0:T(8,128)S(1)}) custom-call(f32[32,256]{1,0:T(8,128)} %bitcast.147, f32[1,256]{1,0:T(1,128)} %precond.1, f32[1,256]{1,0:T(1,128)} %sink.1, s32[1,64]{1,0:T(1,128)} %pads.1, f32[1,64]{1,0:T(1,128)} %cond.11), custom_call_target="tpu_custom_call" | custom-call | tf_op jit(solution)/shard_map/pallas_call | solution.py:335
  2.1 0.9 %collective-permute-done.27.refs_7_ = f32[2,32,128]{2,1,0:T(8,128)S(1)} collective-permute-done((f32[2,32,128]{2,1,0:T(8,128)S(1)}, f32[2,32,128]{2,1,0:T(8,128)S(1)}, u32[]{:S(2)}, u32[]{:S(2)}) %collective-permute-start.27) | collective-permute-done | bytes 32800 | tf_op jit(solution)/shard_map/ppermute | solution.py:393
  3.0 2.8 %collective-permute-start.28 = (f32[4,32,128]{2,1,0:T(8,128)S(1)}, f32[4,32,128]{2,1,0:T(8,128)S(1)}, u32[]{:S(2)}, u32[]{:S(2)}) collective-permute-start(f32[4,32,128]{2,1,0:T(8,128)S(1)} %pad_maximum_fusion), channel_id=1, source_target_pairs={{0,2},{1,0},{2,4},{3,1},{4,6},{5,3},{6,8},{7,5},{8,10},{9,7},{10,1... | collective-permute-start | bytes 196616 | tf_op jit(solution)/shard_map/ppermute | solution.py:396
  5.8 1.5 %collective-permute-start.29 = (f32[2,32,128]{2,1,0:T(8,128)S(1)}, f32[2,32,128]{2,1,0:T(8,128)S(1)}, u32[]{:S(2)}, u32[]{:S(2)}) collective-permute-start(f32[2,32,128]{2,1,0:T(8,128)S(1)} %get-tuple-element.67.refs_6_.z), channel_id=1, source_target_pairs={{0,2},{1,4},{2,0},{3,6},{4,1},{5,8},{6,3},{7,10},{8,5},{9,12},{10,... | collective-permute-start | bytes 98312 | tf_op jit(solution)/shard_map/ppermute | solution.py:394
  7.4 1.5 %collective-permute-start.30 = (f32[40,128]{1,0:T(8,128)S(1)}, f32[40,128]{1,0:T(8,128)S(1)}, u32[]{:S(2)}, u32[]{:S(2)}) collective-permute-start(f32[40,128]{1,0:T(8,128)S(1)} %get-tuple-element.68.refs_11_), channel_id=1, source_target_pairs={{0,16},{16,0},{1,17},{17,1},{2,18},{18,2},{3,19},{19,3},{4,20},{20... | collective-permute-start | bytes 61448 | tf_op jit(solution)/shard_map/ppermute | solution.py:395
  8.9 1.8 %shard_map.87 = (bf16[768,768]{1,0:T(8,128)(2,1)S(1)}, bf16[768,768]{1,0:T(8,128)(2,1)S(1)}, bf16[768,768]{1,0:T(8,128)(2,1)S(1)}, f32[86,8,128]{2,1,0:T(8,128)S(1)}) custom-call(f32[768,768]{1,0:T(8,128)} %bitcast.141, s32[1,6]{1,0:T(1,128)} %blocks.1), custom_call_target="tpu_custom_call" | custom-call | tf_op jit(solution)/shard_map/pallas_call | solution.py:335
  11.2 1.2 %collective-permute-done.31.refs_8_ = f32[4,32,128]{2,1,0:T(8,128)S(1)} collective-permute-done((f32[4,32,128]{2,1,0:T(8,128)S(1)}, f32[4,32,128]{2,1,0:T(8,128)S(1)}, u32[]{:S(2)}, u32[]{:S(2)}) %collective-permute-start.31) | collective-permute-done | bytes 65568 | tf_op jit(solution)/shard_map/ppermute | solution.py:398
  13.4 1.1 %collective-permute-done.32 = f32[4,32,128]{2,1,0:T(8,128)S(1)} collective-permute-done((f32[4,32,128]{2,1,0:T(8,128)S(1)}, f32[4,32,128]{2,1,0:T(8,128)S(1)}, u32[]{:S(2)}, u32[]{:S(2)}) %collective-permute-start.32) | collective-permute-done | bytes 65568 | tf_op jit(solution)/shard_map/ppermute | solution.py:390
  14.7 1.9 %collective-permute-start.34 = (f32[2,32,128]{2,1,0:T(8,128)S(1)}, f32[2,32,128]{2,1,0:T(8,128)S(1)}, u32[]{:S(2)}, u32[]{:S(2)}) collective-permute-start(f32[2,32,128]{2,1,0:T(8,128)S(1)} %get-tuple-element.85), channel_id=1, source_target_pairs={{0,2},{1,4},{2,0},{3,6},{4,1},{5,8},{6,3},{7,10},{8,5},{9,12},{10,... | collective-permute-start | bytes 98312 | tf_op jit(solution)/shard_map/ppermute | solution.py:389
  16.6 2.6 %collective-permute-done.34.from_p2 = f32[2,32,128]{2,1,0:T(8,128)S(1)} collective-permute-done((f32[2,32,128]{2,1,0:T(8,128)S(1)}, f32[2,32,128]{2,1,0:T(8,128)S(1)}, u32[]{:S(2)}, u32[]{:S(2)}) %collective-permute-start.34) | collective-permute-done | bytes 32800 | tf_op jit(solution)/shard_map/ppermute | solution.py:389
  19.4 1.2 %collective-permute-done.35.there = f32[5,32,128]{2,1,0:T(8,128)S(1)} collective-permute-done((f32[5,32,128]{2,1,0:T(8,128)S(1)}, f32[5,32,128]{2,1,0:T(8,128)S(1)}, u32[]{:S(2)}, u32[]{:S(2)}) %collective-permute-start.35) | collective-permute-done | bytes 81952 | tf_op jit(solution)/shard_map/ppermute | solution.py:403
  20.7 1.6 %collective-permute-start.36 = (f32[4,32,128]{2,1,0:T(8,128)S(1)}, f32[4,32,128]{2,1,0:T(8,128)S(1)}, u32[]{:S(2)}, u32[]{:S(2)}) collective-permute-start(f32[4,32,128]{2,1,0:T(8,128)S(1)} %get-tuple-element.88), channel_id=1, source_target_pairs={{0,2},{1,0},{2,4},{3,1},{4,6},{5,3},{6,8},{7,5},{8,10},{9,7},{10,1... | collective-permute-start | bytes 196616 | tf_op jit(solution)/shard_map/ppermute | solution.py:407
  22.3 1.0 %collective-permute-start.37 = (f32[2,32,128]{2,1,0:T(8,128)S(1)}, f32[2,32,128]{2,1,0:T(8,128)S(1)}, u32[]{:S(2)}, u32[]{:S(2)}) collective-permute-start(f32[2,32,128]{2,1,0:T(8,128)S(1)} %get-tuple-element.87.refs_6_.scaled), channel_id=1, source_target_pairs={{0,2},{1,4},{2,0},{3,6},{4,1},{5,8},{6,3},{7,10},{8,5},{9,12},{10,... | collective-permute-start | bytes 98312 | tf_op jit(solution)/shard_map/ppermute | solution.py:408
  23.4 1.0 %collective-permute-start.38 = (f32[32,128]{1,0:T(8,128)S(1)}, f32[32,128]{1,0:T(8,128)S(1)}, u32[]{:S(2)}, u32[]{:S(2)}) collective-permute-start(f32[32,128]{1,0:T(8,128)S(1)} %get-tuple-element.89), channel_id=1, source_target_pairs={{0,16},{16,0},{1,17},{17,1},{2,18},{18,2},{3,19},{19,3},{4,20},{20... | collective-permute-start | bytes 49160 | tf_op jit(solution)/shard_map/ppermute | solution.py:409
  24.4 2.7 %collective-permute-done.38.refs_9_ = f32[32,128]{1,0:T(8,128)S(1)} collective-permute-done((f32[32,128]{1,0:T(8,128)S(1)}, f32[32,128]{1,0:T(8,128)S(1)}, u32[]{:S(2)}, u32[]{:S(2)}) %collective-permute-start.38) | collective-permute-done | bytes 16416 | tf_op jit(solution)/shard_map/ppermute | solution.py:409
  27.1 1.2 %collective-permute-done.39.refs_8_ = f32[4,32,128]{2,1,0:T(8,128)S(1)} collective-permute-done((f32[4,32,128]{2,1,0:T(8,128)S(1)}, f32[4,32,128]{2,1,0:T(8,128)S(1)}, u32[]{:S(2)}, u32[]{:S(2)}) %collective-permute-start.39) | collective-permute-done | bytes 65568 | tf_op jit(solution)/shard_map/ppermute | solution.py:411
  28.4 1.5 %shard_map.91 = (f32[4,32,128]{2,1,0:T(8,128)S(1)}, f32[4,32,128]{2,1,0:T(8,128)S(1)}, f32[2,32,128]{2,1,0:T(8,128)S(1)}, f32[4,32,128]{2,1,0:T(8,128)S(1)}, f32[32,8,128]{2,1,0:T(8,128)}) custom-call(f32[86,8,128]{2,1,0:T(8,128)S(1)} %get-tuple-element.73.refs_0_.places, bf16[768,768]{1,0:T(8,128)(2,1)S(1)} %get-tuple-element.74.refs_1_, ...), custom_call_target="tpu_custom_call" | custom-call | tf_op jit(solution)/shard_map/pallas_call | solution.py:335
  29.9 3.0 %all-to-all-start = ((f32[32,8,128]{2,1,0:T(8,128)}), f32[32,8,128]{2,1,0:T(8,128)S(1)}, u32[]{:S(2)}, u32[]{:S(2)}) async-start(f32[32,8,128]{2,1,0:T(8,128)} %get-tuple-element.99), calls=%async_computation | async-start | bytes 262144 | tf_op jit(solution)/shard_map/all_to_all | solution.py:417
  33.2 1.0 %collective-permute-done.40 = f32[4,32,128]{2,1,0:T(8,128)S(1)} collective-permute-done((f32[4,32,128]{2,1,0:T(8,128)S(1)}, f32[4,32,128]{2,1,0:T(8,128)S(1)}, u32[]{:S(2)}, u32[]{:S(2)}) %collective-permute-start.40) | collective-permute-done | bytes 65568 | tf_op jit(solution)/shard_map/ppermute | solution.py:390
  34.5 1.8 %collective-permute-start.42 = (f32[2,32,128]{2,1,0:T(8,128)S(1)}, f32[2,32,128]{2,1,0:T(8,128)S(1)}, u32[]{:S(2)}, u32[]{:S(2)}) collective-permute-start(f32[2,32,128]{2,1,0:T(8,128)S(1)} %get-tuple-element.97), channel_id=1, source_target_pairs={{0,2},{1,4},{2,0},{3,6},{4,1},{5,8},{6,3},{7,10},{8,5},{9,12},{10,... | collective-permute-start | bytes 98312 | tf_op jit(solution)/shard_map/ppermute | solution.py:389
  36.3 2.9 %collective-permute-done.42.from_p2 = f32[2,32,128]{2,1,0:T(8,128)S(1)} collective-permute-done((f32[2,32,128]{2,1,0:T(8,128)S(1)}, f32[2,32,128]{2,1,0:T(8,128)S(1)}, u32[]{:S(2)}, u32[]{:S(2)}) %collective-permute-start.42) | collective-permute-done | bytes 32800 | tf_op jit(solution)/shard_map/ppermute | solution.py:389
  39.3 1.3 %collective-permute-start.43 = (f32[2,32,128]{2,1,0:T(8,128)S(1)}, f32[2,32,128]{2,1,0:T(8,128)S(1)}, u32[]{:S(2)}, u32[]{:S(2)}) collective-permute-start(f32[2,32,128]{2,1,0:T(8,128)S(1)} %get-tuple-element.100), channel_id=1, source_target_pairs={{0,1},{1,0},{2,3},{3,2},{4,5},{5,4},{6,7},{7,6},{8,9},{9,8},{10,11... | collective-permute-start | bytes 98312 | tf_op jit(solution)/shard_map/ppermute | solution.py:419
  40.6 0.9 %collective-permute-done.43.there = f32[2,32,128]{2,1,0:T(8,128)S(1)} collective-permute-done((f32[2,32,128]{2,1,0:T(8,128)S(1)}, f32[2,32,128]{2,1,0:T(8,128)S(1)}, u32[]{:S(2)}, u32[]{:S(2)}) %collective-permute-start.43) | collective-permute-done | bytes 32800 | tf_op jit(solution)/shard_map/ppermute | solution.py:419
  43.2 0.8 %shard_map.94 = (f32[32,256]{1,0:T(8,128)}, f32[32,256]{1,0:T(8,128)}) custom-call(f32[32,256]{1,0:T(8,128)S(1)} %get-tuple-element.66.rhs, f32[2,32,128]{2,1,0:T(8,128)S(1)} %get-tuple-element.67.refs_6_.z, f32[32,256]{1,0:T(8,128)S(1)} %get-tuple-element.86.image, f32[2,32,128]{2,1,0:T(8,128)S(1)} %get-tuple-element.87.refs_6_.scaled, ...), custom_call_target="tpu_custom_call" | custom-call | tf_op jit(solution)/shard_map/pallas_call | solution.py:335
  (40 shorter events, 4.2 us)
Async XLA Ops:
  1.6 1.4 %collective-permute-start.27 = (f32[2,32,128]{2,1,0:T(8,128)S(1)}, f32[2,32,128]{2,1,0:T(8,128)S(1)}, u32[]{:S(2)}, u32[]{:S(2)}) collective-permute-start(f32[2,32,128]{2,1,0:T(8,128)S(1)} %get-tuple-element.67.refs_6_.z), channel_id=1, source_target_pairs={{0,1},{1,0},{2,3},{3,2},{4,5},{5,4},{6,7},{7,6},{8,9},{9,8},{10,11... | collective-permute-start | bytes 98312 | tf_op jit(solution)/shard_map/ppermute | solution.py:393
  3.0 8.2 %collective-permute-start.28 = (f32[4,32,128]{2,1,0:T(8,128)S(1)}, f32[4,32,128]{2,1,0:T(8,128)S(1)}, u32[]{:S(2)}, u32[]{:S(2)}) collective-permute-start(f32[4,32,128]{2,1,0:T(8,128)S(1)} %pad_maximum_fusion), channel_id=1, source_target_pairs={{0,2},{1,0},{2,4},{3,1},{4,6},{5,3},{6,8},{7,5},{8,10},{9,7},{10,1... | collective-permute-start | bytes 196616 | tf_op jit(solution)/shard_map/ppermute | solution.py:396
  5.8 5.3 %collective-permute-start.29 = (f32[2,32,128]{2,1,0:T(8,128)S(1)}, f32[2,32,128]{2,1,0:T(8,128)S(1)}, u32[]{:S(2)}, u32[]{:S(2)}) collective-permute-start(f32[2,32,128]{2,1,0:T(8,128)S(1)} %get-tuple-element.67.refs_6_.z), channel_id=1, source_target_pairs={{0,2},{1,4},{2,0},{3,6},{4,1},{5,8},{6,3},{7,10},{8,5},{9,12},{10,... | collective-permute-start | bytes 98312 | tf_op jit(solution)/shard_map/ppermute | solution.py:394
  7.4 3.8 %collective-permute-start.30 = (f32[40,128]{1,0:T(8,128)S(1)}, f32[40,128]{1,0:T(8,128)S(1)}, u32[]{:S(2)}, u32[]{:S(2)}) collective-permute-start(f32[40,128]{1,0:T(8,128)S(1)} %get-tuple-element.68.refs_11_), channel_id=1, source_target_pairs={{0,16},{16,0},{1,17},{17,1},{2,18},{18,2},{3,19},{19,3},{4,20},{20... | collective-permute-start | bytes 61448 | tf_op jit(solution)/shard_map/ppermute | solution.py:395
  11.2 1.3 %collective-permute-start.31 = (f32[4,32,128]{2,1,0:T(8,128)S(1)}, f32[4,32,128]{2,1,0:T(8,128)S(1)}, u32[]{:S(2)}, u32[]{:S(2)}) collective-permute-start(f32[4,32,128]{2,1,0:T(8,128)S(1)} %collective-permute-done.28.refs_5_), channel_id=1, source_target_pairs={{0,1},{1,0},{2,3},{3,2},{4,5},{5,4},{6,7},{7,6},{8,9},{9,8},{10,11... | collective-permute-start | bytes 196616 | tf_op jit(solution)/shard_map/ppermute | solution.py:398
  13.2 1.3 %collective-permute-start.32 = (f32[4,32,128]{2,1,0:T(8,128)S(1)}, f32[4,32,128]{2,1,0:T(8,128)S(1)}, u32[]{:S(2)}, u32[]{:S(2)}) collective-permute-start(f32[4,32,128]{2,1,0:T(8,128)S(1)} %get-tuple-element.84), channel_id=1, source_target_pairs={{0,1},{1,0},{2,3},{3,2},{4,5},{5,4},{6,7},{7,6},{8,9},{9,8},{10,11... | collective-permute-start | bytes 196616 | tf_op jit(solution)/shard_map/ppermute | solution.py:390
  14.5 4.7 %collective-permute-start.33 = (f32[4,32,128]{2,1,0:T(8,128)S(1)}, f32[4,32,128]{2,1,0:T(8,128)S(1)}, u32[]{:S(2)}, u32[]{:S(2)}) collective-permute-start(f32[4,32,128]{2,1,0:T(8,128)S(1)} %add.108), channel_id=1, source_target_pairs={{2,0},{0,1},{4,2},{1,3},{6,4},{3,5},{8,6},{5,7},{10,8},{7,9},{12,1... | collective-permute-start | bytes 196616 | tf_op jit(solution)/shard_map/ppermute | solution.py:401
  14.7 4.5 %collective-permute-start.34 = (f32[2,32,128]{2,1,0:T(8,128)S(1)}, f32[2,32,128]{2,1,0:T(8,128)S(1)}, u32[]{:S(2)}, u32[]{:S(2)}) collective-permute-start(f32[2,32,128]{2,1,0:T(8,128)S(1)} %get-tuple-element.85), channel_id=1, source_target_pairs={{0,2},{1,4},{2,0},{3,6},{4,1},{5,8},{6,3},{7,10},{8,5},{9,12},{10,... | collective-permute-start | bytes 98312 | tf_op jit(solution)/shard_map/ppermute | solution.py:389
  19.2 1.3 %collective-permute-start.35 = (f32[5,32,128]{2,1,0:T(8,128)S(1)}, f32[5,32,128]{2,1,0:T(8,128)S(1)}, u32[]{:S(2)}, u32[]{:S(2)}) collective-permute-start(f32[5,32,128]{2,1,0:T(8,128)S(1)} %shard_map.89.part), channel_id=1, source_target_pairs={{0,1},{1,0},{2,3},{3,2},{4,5},{5,4},{6,7},{7,6},{8,9},{9,8},{10,11... | collective-permute-start | bytes 245768 | tf_op jit(solution)/shard_map/ppermute | solution.py:403
  20.7 6.4 %collective-permute-start.36 = (f32[4,32,128]{2,1,0:T(8,128)S(1)}, f32[4,32,128]{2,1,0:T(8,128)S(1)}, u32[]{:S(2)}, u32[]{:S(2)}) collective-permute-start(f32[4,32,128]{2,1,0:T(8,128)S(1)} %get-tuple-element.88), channel_id=1, source_target_pairs={{0,2},{1,0},{2,4},{3,1},{4,6},{5,3},{6,8},{7,5},{8,10},{9,7},{10,1... | collective-permute-start | bytes 196616 | tf_op jit(solution)/shard_map/ppermute | solution.py:407
  22.3 4.8 %collective-permute-start.37 = (f32[2,32,128]{2,1,0:T(8,128)S(1)}, f32[2,32,128]{2,1,0:T(8,128)S(1)}, u32[]{:S(2)}, u32[]{:S(2)}) collective-permute-start(f32[2,32,128]{2,1,0:T(8,128)S(1)} %get-tuple-element.87.refs_6_.scaled), channel_id=1, source_target_pairs={{0,2},{1,4},{2,0},{3,6},{4,1},{5,8},{6,3},{7,10},{8,5},{9,12},{10,... | collective-permute-start | bytes 98312 | tf_op jit(solution)/shard_map/ppermute | solution.py:408
  23.4 3.7 %collective-permute-start.38 = (f32[32,128]{1,0:T(8,128)S(1)}, f32[32,128]{1,0:T(8,128)S(1)}, u32[]{:S(2)}, u32[]{:S(2)}) collective-permute-start(f32[32,128]{1,0:T(8,128)S(1)} %get-tuple-element.89), channel_id=1, source_target_pairs={{0,16},{16,0},{1,17},{17,1},{2,18},{18,2},{3,19},{19,3},{4,20},{20... | collective-permute-start | bytes 49160 | tf_op jit(solution)/shard_map/ppermute | solution.py:409
  27.1 1.3 %collective-permute-start.39 = (f32[4,32,128]{2,1,0:T(8,128)S(1)}, f32[4,32,128]{2,1,0:T(8,128)S(1)}, u32[]{:S(2)}, u32[]{:S(2)}) collective-permute-start(f32[4,32,128]{2,1,0:T(8,128)S(1)} %collective-permute-done.36.refs_5_), channel_id=1, source_target_pairs={{0,1},{1,0},{2,3},{3,2},{4,5},{5,4},{6,7},{7,6},{8,9},{9,8},{10,11... | collective-permute-start | bytes 196616 | tf_op jit(solution)/shard_map/ppermute | solution.py:411
  28.4 14.5 %copy-start = (f32[1,32,256]{2,1,0:T(8,128)S(1)}, f32[1,32,256]{2,1,0:T(8,128)}, u32[]{:S(2)}) copy-start(f32[1,32,256]{2,1,0:T(8,128)} %param.13) | copy-start | bytes 98308
  28.4 14.5 %copy-start.1 = (f32[1,256]{1,0:T(1,128)S(1)}, f32[1,256]{1,0:T(1,128)}, u32[]{:S(2)}) copy-start(f32[1,256]{1,0:T(1,128)} %precond.1) | copy-start | bytes 3076
  28.4 14.5 %copy-start.2 = (f32[1,256]{1,0:T(1,128)S(1)}, f32[1,256]{1,0:T(1,128)}, u32[]{:S(2)}) copy-start(f32[1,256]{1,0:T(1,128)} %sink.1) | copy-start | bytes 3076
  28.4 14.5 %copy-start.3 = (s32[1,6]{1,0:T(1,128)S(1)}, s32[1,6]{1,0:T(1,128)}, u32[]{:S(2)}) copy-start(s32[1,6]{1,0:T(1,128)} %blocks.1) | copy-start | bytes 76
  28.4 14.5 %copy-start.4 = (s32[1,64]{1,0:T(1,128)S(1)}, s32[1,64]{1,0:T(1,128)}, u32[]{:S(2)}) copy-start(s32[1,64]{1,0:T(1,128)} %pads.1) | copy-start | bytes 772
  28.4 14.5 %copy-start.5 = (f32[1,64]{1,0:T(1,128)S(1)}, f32[1,64]{1,0:T(1,128)}, u32[]{:S(2)}) copy-start(f32[1,64]{1,0:T(1,128)} %cond.11) | copy-start | bytes 772
  29.9 11.5 %all-to-all-start = ((f32[32,8,128]{2,1,0:T(8,128)}), f32[32,8,128]{2,1,0:T(8,128)S(1)}, u32[]{:S(2)}, u32[]{:S(2)}) async-start(f32[32,8,128]{2,1,0:T(8,128)} %get-tuple-element.99), calls=%async_computation | async-start | bytes 262144 | tf_op jit(solution)/shard_map/all_to_all | solution.py:417
  32.9 1.3 %collective-permute-start.40 = (f32[4,32,128]{2,1,0:T(8,128)S(1)}, f32[4,32,128]{2,1,0:T(8,128)S(1)}, u32[]{:S(2)}, u32[]{:S(2)}) collective-permute-start(f32[4,32,128]{2,1,0:T(8,128)S(1)} %get-tuple-element.96), channel_id=1, source_target_pairs={{0,1},{1,0},{2,3},{3,2},{4,5},{5,4},{6,7},{7,6},{8,9},{9,8},{10,11... | collective-permute-start | bytes 196616 | tf_op jit(solution)/shard_map/ppermute | solution.py:390
  34.2 5.0 %collective-permute-start.41 = (f32[4,32,128]{2,1,0:T(8,128)S(1)}, f32[4,32,128]{2,1,0:T(8,128)S(1)}, u32[]{:S(2)}, u32[]{:S(2)}) collective-permute-start(f32[4,32,128]{2,1,0:T(8,128)S(1)} %add.109), channel_id=1, source_target_pairs={{2,0},{0,1},{4,2},{1,3},{6,4},{3,5},{8,6},{5,7},{10,8},{7,9},{12,1... | collective-permute-start | bytes 196616 | tf_op jit(solution)/shard_map/ppermute | solution.py:416
  34.5 4.7 %collective-permute-start.42 = (f32[2,32,128]{2,1,0:T(8,128)S(1)}, f32[2,32,128]{2,1,0:T(8,128)S(1)}, u32[]{:S(2)}, u32[]{:S(2)}) collective-permute-start(f32[2,32,128]{2,1,0:T(8,128)S(1)} %get-tuple-element.97), channel_id=1, source_target_pairs={{0,2},{1,4},{2,0},{3,6},{4,1},{5,8},{6,3},{7,10},{8,5},{9,12},{10,... | collective-permute-start | bytes 98312 | tf_op jit(solution)/shard_map/ppermute | solution.py:389
  39.3 2.2 %collective-permute-start.43 = (f32[2,32,128]{2,1,0:T(8,128)S(1)}, f32[2,32,128]{2,1,0:T(8,128)S(1)}, u32[]{:S(2)}, u32[]{:S(2)}) collective-permute-start(f32[2,32,128]{2,1,0:T(8,128)S(1)} %get-tuple-element.100), channel_id=1, source_target_pairs={{0,1},{1,0},{2,3},{3,2},{4,5},{5,4},{6,7},{7,6},{8,9},{9,8},{10,11... | collective-permute-start | bytes 98312 | tf_op jit(solution)/shard_map/ppermute | solution.py:419

commit v3 on v0

v3 whole, which is shorter than its diff:
```python
import jax
import jax.numpy as jnp
from jax import lax
from jax.experimental import pallas as pl
from jax.experimental.pallas import tpu as pltpu
from jax.sharding import PartitionSpec as P

BR = 128
REACH = 3
F32 = jnp.float32
HALF = jnp.bfloat16
barrier = lax.optimization_barrier


def climb(count, step):
    pairs = []
    for source in range(count):
        chip, core = divmod(source, 2)
        target = chip - step if core else chip + step
        inside = 0 <= target < count // 2
        pairs.append((source, target * 2 + core if inside else source ^ 1))
    return pairs


def leap(count):
    pairs = []
    for source in range(count):
        chip, core = divmod(source, 2)
        target = chip + 2 if core else chip - 2
        if 0 <= target < count // 2:
            pairs.append((source, target * 2 + 1 - core))
        else:
            pairs.append((source, source ^ 2))
    return pairs


def turned(pairs):
    return [(target, source) for source, target in pairs]


def thirds(value):
    high = value.astype(HALF)
    rest = value - high.astype(F32)
    middle = rest.astype(HALF)
    return high, middle, (rest - middle.astype(F32)).astype(HALF)


def dot(left, right):
    return jnp.dot(left, right, preferred_element_type=F32)


def times_ones(value, ones, turn):
    rows = value.shape[0]
    parts = jnp.concatenate(thirds(value))
    if turn:
        out = lax.dot_general(parts, ones, (((1,), (1,)), ((), ())), preferred_element_type=F32)
    else:
        out = dot(parts, ones)
    return out[:rows] + (out[rows : 2 * rows] + out[2 * rows :])


def pad_matrix(pad_rows, owned):
    here = lax.broadcasted_iota(jnp.int32, (owned, pad_rows.shape[1]), 0)
    return (here == pad_rows).astype(F32).astype(HALF)


def product_of(value, high, middle, low):
    rows = value.shape[0]
    one, two, three = thirds(value)
    first = dot(jnp.concatenate([one, two, three]), high[...])
    second = dot(jnp.concatenate([one, two]), middle[...])
    small = first[2 * rows :] + second[rows:] + dot(one, low[...])
    return (small + (first[rows : 2 * rows] + second[:rows])) + first[:rows]


def wide(pair):
    return jnp.concatenate([pair[0], pair[1]], axis=1)


def put_wide(ref, start, value):
    ref[start] = value[:, :BR]
    ref[start + 1] = value[:, BR:]


def lanes_of(cases, slot):
    lane = lax.broadcasted_iota(jnp.int32, (cases, BR), 1)
    return lane == lax.broadcasted_iota(jnp.int32, (cases, BR), 0) + slot * cases


def as_column(row, slot, cases):
    return jnp.sum(jnp.where(lanes_of(cases, slot), row, 0.0), axis=1, keepdims=True)


def begin_kernel(z, pad_rows, pad_cond, ones_out, pads_out):
    cases = z.shape[0]
    owned, count = ones_out.shape
    ones = pad_matrix(pad_rows[...], owned)
    ones_out[...] = ones
    pads_out[...] = jnp.zeros_like(pads_out)
    pads_out[:cases, :count] = times_ones(z[...], ones, False)
    pads_out[cases : cases + 1, :count] = pad_cond[...]
    pads_out[cases + 8 : cases + 9, :count] = pad_rows[...].astype(F32)


def prepare_kernel(schur, blocks, high, middle, low, places, top, held, sems):
    chunk = held.shape[0] // sems.shape[0]
    copies = []
    for i in range(sems.shape[0]):
        rows = slice(i * chunk, (i + 1) * chunk)
        copies.append(pltpu.make_async_copy(schur.at[rows], held.at[rows], sems.at[i]))
    for copy in copies:
        copy.start()
    position = lax.axis_index("sub")
    chip, core = position // 2, lax.rem(position, 2)
    above, below = lax.axis_size("sub") // 2 - 1 - chip, chip
    touched = blocks.shape[1]
    listed = blocks[...]
    offset = listed // 2 - position
    mirrored = jnp.where(core == 0, offset, -offset)
    place = jnp.where(mirrored == 2, 6, jnp.where(mirrored == 3, 5, mirrored + REACH))
    place = place * 2 + lax.rem(listed, 2)
    spots = 2 * (2 * REACH + 1)
    for i in range(touched):
        here = jnp.broadcast_to(place[:, i : i + 1], places.shape[1:])
        for j in range(spots):
            places[i * spots + j] = (here == j).astype(F32)
    near = jnp.where(core == 0, above, below) >= 1
    far = jnp.where(core == 0, below, above) >= 2
    for i, sender in enumerate((near, far)):
        places[touched * spots + i] = jnp.full(places.shape[1:], sender.astype(F32))
    largest = jnp.ones((1, chunk), F32)
    for i, copy in enumerate(copies):
        rows = slice(i * chunk, (i + 1) * chunk)
        copy.wait()
        high[rows], middle[rows], low[rows] = thirds(0.25 * held[rows])
        largest = jnp.maximum(largest, jnp.max(held[rows, rows], axis=0, keepdims=True))
    top[...] = jnp.broadcast_to(jnp.max(largest, axis=1, keepdims=True), top.shape)


def spot(places, i, cases):
    return jnp.concatenate([places[i]] * (cases // 8))


def picked_blocks(places, held, touched):
    cases, spots = held[0].shape[0], len(held)
    picked = []
    for i in range(touched):
        total = spot(places, i * spots, cases) * held[0]
        for j in range(1, spots):
            total = total + spot(places, i * spots + j, cases) * held[j]
        picked.append(total)
    return jnp.concatenate(picked, axis=1)


def landed_blocks(places, product):
    cases, touched = product.shape[0], product.shape[1] // BR
    spots = (places.shape[0] - 2) // touched
    landed = []
    for j in range(spots):
        total = spot(places, j, cases) * product[:, :BR]
        for i in range(1, touched):
            total = total + spot(places, i * spots + j, cases) * product[:, i * BR : (i + 1) * BR]
        landed.append(total)
    return landed


def halves(*values):
    return [value[:, start : start + BR] for value in values for start in (0, BR)]


def held_blocks(p2, p1, own, a, b):
    return [p2[0], p2[1], p1[0], p1[1], p1[2], p1[3], own[0], own[1], a[0], a[1], b[0], b[1], b[2], b[3]]


def mean_of(mine, conds, cases, count):
    return 0.5 * (mine[cases : cases + 1, :count] + conds[cases : cases + 1, :count])


def first_kernel(
    places, high, middle, low, p2, p1, own, a, b, back, to_p1, to_p2, kept, picked_out, product_out
):
    touched = high.shape[0] // BR
    picked = picked_blocks(places, halves(p2, p1[0], p1[1], own, a, b[0], b[1]), touched)
    product = product_of(4.0 * picked, high, middle, low)
    landed = landed_blocks(places, product)
    for j in range(2):
        to_p2[j] = landed[j]
    for j in range(4):
        back[j] = landed[10 + j]
        to_p1[j] = landed[2 + j]
    for j in range(4):
        kept[j] = landed[6 + j]
    picked_out[...] = picked
    product_out[...] = product


def ties_kernel(z, mine, conds, ones, sink, local, jump_out):
    cases, count = z.shape[0], ones.shape[1]
    jump = mine[:cases, :count] - conds[:cases, :count]
    jump_out[...] = jump
    local[...] = sink[...] * z[...] + times_ones(mean_of(mine, conds, cases, count) * jump, ones[...], True)


def folded(value):
    total = value[:, :BR]
    for i in range(1, value.shape[1] // BR):
        total = total + value[:, i * BR : (i + 1) * BR]
    return total


def across_lanes(value):
    return jnp.sum(value, axis=1, keepdims=True)


def largest_of(blocks, pads):
    size = jnp.maximum(
        jnp.max(jnp.abs(blocks), axis=1, keepdims=True), jnp.max(jnp.abs(pads), axis=1, keepdims=True)
    )
    return jnp.where(size > 0.0, size, 1.0)


def case_row(columns):
    cases = columns[0].shape[0]
    total = jnp.where(lanes_of(cases, 0), columns[0], 0.0)
    for slot in range(1, len(columns)):
        total = jnp.where(lanes_of(cases, slot), columns[slot], total)
    return jnp.sum(total, axis=0, keepdims=True)


def shares_kernel(rhs, z, image, precond, sink, picked, product, jump, mine, conds, top, known, guide):
    cases, count = jump.shape
    start = z[...]
    bulk = 0.25 * (4.0 / top[0:1, 0:1])
    mean = mean_of(mine, conds, cases, count)
    size = largest_of(picked[...], jump[...])
    inverse = 1.0 / size
    unit = picked[...] * inverse
    unit_jump = jump[...] * inverse
    unit_own = start * inverse
    pulled = (product[...] * bulk) * inverse
    energy = across_lanes(folded(unit * pulled) + bulk * folded(sink[...] * unit_own * unit_own))
    energy = energy + 0.5 * bulk * across_lanes(mean * unit_jump * unit_jump)
    norm = across_lanes(folded(rhs[...] * start))
    curve = across_lanes(folded(start * image[...]))
    reach = jnp.max(jnp.abs(image[...]), axis=1, keepdims=True)
    still = reach <= 0.0
    scale = size / jnp.where(still, 1.0, reach)
    guess = jnp.where(curve > 0.0, norm / jnp.where(curve > 0.0, curve, 1.0), 0.0)
    guess = jnp.where(still, 1.0, jnp.clip(guess, scale * (1.0 / 1024.0), scale * 8.0))
    moved = guess * image[...]
    rest = rhs[...] - moved
    weighted = precond[...] * moved
    known[0:1] = case_row([norm, guess, across_lanes(folded(precond[...] * rest * rest)), across_lanes(folded(weighted * rest))])
    known[1:2] = case_row(
        [across_lanes(folded(weighted * moved)), size, energy, jnp.broadcast_to(top[0:1, 0:1], size.shape)]
    )
    tilt = jnp.where(norm > 0.0, curve / jnp.where(norm > 0.0, norm, 1.0), 0.0) * size
    guide[0] = jnp.broadcast_to(jnp.clip(tilt, -1e37, 1e37), guide.shape[1:])
    guide[1] = jnp.broadcast_to(inverse, guide.shape[1:])


def put_tiles(ref, start, block):
    tiles = block.shape[0] // 8
    ref[start * tiles : (start + 1) * tiles] = block.reshape(tiles, 8, BR)


def second_kernel(
    places, high, middle, low, p2, p1, own, a, b, there, conds, mine, ones, sink, top,
    start_picked, start_product, start_jump, start_own, known, guide,
    back, to_p1, to_p2, kept, sums,
):
    touched = high.shape[0] // BR
    cases = own.shape[1]
    count = ones.shape[1]
    less = 4.0 / top[0:1, 0:1]
    picked = picked_blocks(places, held_blocks(p2, p1, own, a, b), touched)
    product = product_of((picked * less) * (1.0 / 1024.0), high, middle, low)
    scales = jnp.concatenate([there[4, 0:1], there[4, 1:2]], axis=1)
    values = scales * wide(there[0:2] + b[4:6])
    pads = conds[cases + 8 : cases + 9, :count].astype(jnp.int32)
    here = wide(own)
    jump = times_ones(here, ones[...], False) - times_ones(values, pad_matrix(pads, values.shape[1]), False)
    mean = mean_of(mine, conds, cases, count)
    local = sink[...] * here + times_ones(mean * jump, ones[...], True)
    local = (local * less) * (1.0 / 4096.0)
    size = largest_of(picked, jump)
    inverse = 1.0 / size
    bulk = 0.25 * less
    tilt = jnp.clip(guide[0, :, 0:1] * inverse, -1e3, 1e3)
    unit = guide[1, :, 0:1]
    tilted = tilt * unit
    rest = picked * inverse - tilted * start_picked[...]
    pulled = product * (1024.0 * inverse) - (start_product[...] * bulk) * tilted
    rest_own = here * inverse - tilted * start_own[...]
    rest_jump = jump * inverse - tilted * start_jump[...]
    sunk = sink[...] * rest_own
    tied = 0.5 * mean * rest_jump
    tail = jnp.zeros((cases, BR - count), F32)
    energy = folded(rest * pulled) + bulk * folded(sunk * rest_own)
    energy = energy + bulk * jnp.concatenate([tied * rest_jump, tail], axis=1)
    cross = folded(start_picked[...] * unit * pulled) + bulk * folded(sunk * (start_own[...] * unit))
    cross = cross + bulk * jnp.concatenate([tied * (start_jump[...] * unit), tail], axis=1)
    own_row = case_row([size, tilt, across_lanes(cross), across_lanes(energy)])
    total = jnp.concatenate([known[0:2], own_row, jnp.zeros_like(own_row)])
    sums[...] = jnp.broadcast_to(total[None], sums.shape)
    landed = landed_blocks(places, product)
    for j in range(2):
        put_tiles(to_p2, j, landed[j])
    for j in range(4):
        put_tiles(back, j, landed[10 + j])
        put_tiles(to_p1, j, landed[2 + j])
    to_p2[to_p2.shape[0] - 1] = top[...]
    to_p1[to_p1.shape[0] - 1] = top[...]
    back[back.shape[0] - 1] = jnp.zeros_like(top)
    kept[0] = landed[6] + local[:, :BR]
    kept[1] = landed[7] + local[:, BR:]
    kept[2] = landed[8]
    kept[3] = landed[9]


def part_kernel(places, kept, local, from_p1, from_p2, precond, top, part):
    cases = kept.shape[1]
    near, far = [spot(places, places.shape[0] - 2 + i, cases)[None] for i in range(2)]
    one = from_p1[...] * near
    mine = kept[0:2] + one[0:2] + from_p2[...] * far
    part[0] = mine[0] + local[:, :BR]
    part[1] = mine[1] + local[:, BR:]
    part[2:4] = kept[2:4] + one[2:4]
    part[4] = jnp.zeros(part.shape[1:], F32)
    part[4, 0:1] = precond[:, :BR]
    part[4, 1:2] = precond[:, BR:]
    part[4, 8:16] = top[...]


def turn_kernel(part, there, precond, image_out, both_out, own_out, top_out):
    image = wide(part[0:2] + there[2:4])
    other = part[2:4] + there[0:2]
    image_out[...] = image
    scaled = precond[...] * image
    put_wide(both_out, 0, scaled)
    put_wide(own_out, 0, scaled)
    both_out[2] = there[4, 0:1] * other[0]
    both_out[3] = there[4, 1:2] * other[1]
    top_out[...] = jnp.maximum(part[4, 8:16], there[4, 8:16])


def last_part_kernel(places, kept, from_p1, from_p2, top, mine, other, top_out):
    cases = kept.shape[1]
    tiles = cases // 8
    near, far = [places[places.shape[0] - 2 + i] for i in range(2)]
    near_top = from_p1[from_p1.shape[0] - 1]
    far_top = from_p2[from_p2.shape[0] - 1]
    most = jnp.maximum(top[...], jnp.maximum(near * near_top, far * far_top))
    here, one, two = top[...] / most, near * (near_top / most), far * (far_top / most)
    for j in range(4):
        block = kept[j].reshape(tiles, 8, BR) * here + from_p1[j * tiles : (j + 1) * tiles] * one
        if j < 2:
            block = block + from_p2[j * tiles : (j + 1) * tiles] * two
            mine[j] = block.reshape(cases, BR)
        else:
            other[(j - 2) * tiles : (j - 1) * tiles] = block
    other[other.shape[0] - 1] = most
    top_out[...] = most


def steps_kernel(sums, steps):
    cases = steps.shape[1]
    rows = [sums[:, i, :] for i in range(3)]

    def value(i):
        row = rows[i // 4]
        return row if i % 4 == 0 else pltpu.roll(row, BR - (i % 4) * cases, 1)

    norm, guess, rest, mixed, moved, size, energy, top, other_size, tilt, cross, other_energy = [
        value(i) for i in range(12)
    ]

    def everyone(terms):
        return jnp.sum(terms, axis=0, keepdims=True)

    norm = everyone(norm)
    alpha = norm / everyone((size * size * energy) * top)
    shift = alpha / guess - 1.0
    fresh = everyone(rest + shift * (shift * moved - 2.0 * mixed))
    grown = 1.0 + fresh / norm
    two = alpha * other_size
    one = grown * size - two * tilt
    bend = everyone(((one * one) * energy + two * (two * other_energy - 2.0 * one * cross)) * top)
    for i, row in enumerate((alpha, grown, fresh / bend)):
        steps[i] = jnp.broadcast_to(as_column(row, 0, cases), steps.shape[1:])


def end_kernel(rhs, z, image, scaled, mine, mine_top, there, steps, solution, residual):
    cases = solution.shape[0]
    tiles = cases // 8
    alpha, grown, step = [wide([steps[i], steps[i]]) for i in range(3)]
    start = z[...]
    direction = grown * start - alpha * wide(scaled)
    solution[...] = alpha * start + step * direction
    there_top = there[there.shape[0] - 1]
    most = jnp.maximum(mine_top[...], there_top)
    here, away = spot([mine_top[...] / most], 0, cases), spot([there_top / most], 0, cases)
    blocks = [mine[j] * here + there[j * tiles : (j + 1) * tiles].reshape(cases, BR) * away for j in range(2)]
    bulk = spot([most], 0, cases)
    second = ((alpha * wide(blocks)) * wide([bulk, bulk])) * 1024.0
    residual[...] = rhs[...] - alpha * image[...] - step * (grown * image[...] - second)


def call(kernel, outs, *operands, scratch=(), far=(), grant=32):
    def space(outside, i):
        return pl.BlockSpec(memory_space=pl.ANY if i in outside else pltpu.VMEM)

    return pl.pallas_call(
        kernel,
        in_specs=[space(far, i) for i in range(len(operands))],
        out_specs=[space((), i) for i in range(len(outs))],
        out_shape=[jax.ShapeDtypeStruct(shape, kind) for shape, kind in outs],
        scratch_shapes=list(scratch),
        compiler_params=pltpu.CompilerParams(vmem_limit_bytes=grant * 1024 * 1024),
    )(*operands)


def on_device(rhs, schur, block_list, pad_rows, pad_cond, sink, precond):
    matrix = schur[0]
    cases, owned = rhs.shape[1:]
    inner = matrix.shape[0]
    blocks = owned // BR
    touched = inner // BR
    count = lax.axis_size("sub")
    everyone = count * lax.axis_size("board")
    pads = pad_rows.shape[1]
    swap = [(i, i ^ 1) for i in range(count)]
    across = [(i, i ^ 1) for i in range(lax.axis_size("board"))]
    near, far = climb(count, 1), leap(count)
    pair = ((blocks, cases, BR), F32)
    both = ((2 * blocks, cases, BR), F32)
    tile = ((8, BR), F32)
    full = ((cases, owned), F32)
    semaphores = pltpu.SemaphoreType.DMA

    z = barrier(precond * rhs[0])
    ones, pads_sent = call(begin_kernel, [((owned, pads), HALF), ((4 * cases + 8, BR), F32)], z, pad_rows, pad_cond)
    chunks = touched
    spots = 2 * (2 * REACH + 1)
    high, middle, low, places, top = call(
        prepare_kernel,
        [((inner, inner), HALF)] * 3 + [((touched * spots + 2, 8, BR), F32), tile],
        matrix, block_list,
        far=range(1),
        scratch=[pltpu.VMEM((inner, inner), F32), semaphores((chunks,))],
        grant=48,
    )

    def collect(back, to_p1, to_p2):
        from_p2 = lax.ppermute(to_p2, "sub", far)
        to_p1 = to_p1 + lax.ppermute(back, "sub", swap)
        return to_p1, from_p2

    other = lax.ppermute(z, "sub", swap)
    p2 = lax.ppermute(z, "sub", far)
    p1 = lax.ppermute(jnp.stack([z, other]), "sub", near)
    p1, p2, high, middle, low, places, top = barrier((p1, p2, high, middle, low, places, top))
    b = lax.ppermute(p1, "sub", swap)
    split = (places, high, middle, low)
    back, to_p1, to_p2, kept, start_picked, start_product = call(
        first_kernel,
        [both, both, pair, both, ((cases, inner), F32), ((cases, inner), F32)],
        *split, p2, p1, z, other, b,
    )
    conds = lax.ppermute(pads_sent, "board", across)
    local, start_jump = call(ties_kernel, [full, ((cases, pads), F32)], z, pads_sent, conds, ones, sink)
    to_p1, from_p2 = collect(back, to_p1, to_p2)
    from_p1 = lax.ppermute(to_p1, "sub", turned(near))
    (part,) = call(part_kernel, [((2 * blocks + 1, cases, BR), F32)], places, kept, local, from_p1, from_p2, precond, top)
    part_there = lax.ppermute(part, "sub", swap)
    part_across = lax.ppermute(part, "board", across)
    image, four, own, top = call(turn_kernel, [full, both, pair, tile], part, part_there, precond)
    known, guide = call(
        shares_kernel,
        [((2, BR), F32), ((2, cases, BR), F32)],
        rhs[0], z, image, precond, sink, start_picked, start_product, start_jump, pads_sent, conds, top,
    )
    p1 = lax.ppermute(four, "sub", near)
    p2 = lax.ppermute(own, "sub", far)
    p1, p2, part_across, known, guide = barrier((p1, p2, part_across, known, guide))
    b = lax.ppermute(jnp.concatenate([p1, part_across[blocks : 2 * blocks]]), "sub", swap)
    tiles = cases // 8
    back, to_p1, to_p2, kept, sums = call(
        second_kernel,
        [((4 * tiles + 1, 8, BR), F32)] * 2 + [((2 * tiles + 1, 8, BR), F32), both, ((everyone, 4, BR), F32)],
        *split, p2, p1, own, four[blocks:], b, part_across, conds, pads_sent, ones, sink, top,
        start_picked, start_product, start_jump, z, known, guide,
    )
    to_p1, from_p2 = collect(back, to_p1, to_p2)
    from_p1 = lax.ppermute(to_p1, "sub", turned(near))
    all_sums = lax.all_to_all(sums, ("board", "sub"), 0, 0)
    mine, to_other, mine_top = call(
        last_part_kernel, [pair, ((2 * tiles + 1, 8, BR), F32), tile], places, kept, from_p1, from_p2, top
    )
    there = lax.ppermute(to_other, "sub", swap)
    all_sums, there = barrier((all_sums, there))
    (steps,) = call(steps_kernel, [((3, cases, BR), F32)], all_sums)
    solution, residual = call(
        end_kernel, [full, full], rhs[0], z, image, own, mine, mine_top, there, steps
    )
    return (solution[None], residual[None])


def solution(mesh):
    in_specs = (
        P("board", None, "sub"),
        P("board", "sub", None),
        P("board", "sub"),
        P("board", "sub"),
        P("board", "sub"),
        P("board", "sub"),
        P("board", "sub"),
    )
    out_specs = (P("board", None, "sub"), P("board", None, "sub"))
    return jax.shard_map(
        on_device, mesh=mesh, in_specs=in_specs, out_specs=out_specs, check_vma=False
    )
```

time: 240 us -> 41.1 us (0.17)
  blocking collectives: 125 us -> 0 us
  starting transfers between devices: 67.1 us -> 20.5 us
  local copies, waits for them, and re-layouts: 18.5 us -> 0.69 us
  other arithmetic: 14.1 us -> 0.82 us
  Pallas kernels: 0 us -> 5.94 us
  matrix products: 4.43 us -> 0 us
  waiting for transfers between devices: 8.2 us -> 12 us
    psum x3 -> x0, blocking collectives: 125 us -> none  [the longest x1 42.9 us: on_device(): norm_now = lax.psum(case_sums(residual, precon), ('board', 'sub'))]
    ppermute x27 -> x17, starting transfers between devices: 67.1 us -> 17.3 us  [the longest x2 3.73 us: collect(): from_p2 = lax.ppermute(to_p2, 'sub', far)]
    unnamed x42 -> x12, local copies, waits for them, and re-layouts: 8.71 us -> 0.69 us
    pallas_call x0 -> x11, Pallas kernels: none -> 5.94 us  [call(): pl.pallas_call(kernel, in_specs=[space(far, i) for i in range(len(operand...]
    scatter-add x4 -> x0, other arithmetic: 5.37 us -> none  [the longest x2 2.88 us: on_device(): partial_value = jnp.zeros(apply_blocks.shape, jnp.float32).at[:, shifted_...]
    ppermute x12 -> x0, local copies, waits for them, and re-layouts: 4.8 us -> none  [passed_along(): lax.ppermute(value, axis, [(source, source + steps) for source in range(l...]
    dot_general x2 -> x0, matrix products: 4.43 us -> none  [on_device(): product = jnp.dot(picked, matrix, precision=lax.Precision.HIGHEST)]
    select_n x7 -> x0, other arithmetic: 4 us -> none  [the longest x3 1.43 us: on_device(): pad_values = jnp.take(direction, pad_local, axis=1)]
  transfers between devices with their start and end apart: 27 -> 18, of which waited for: 6 -> 10; matrix products, arithmetic and copies ran while one was open for 11% -> 0% of each run, Pallas kernels for 0% -> 6%
where the time goes in v3:
time: 41.1 us; the launch traced here: 40.8 us
  starting transfers between devices  20.5 us (50%)
  waiting for transfers between devices  12 us (29%)
  Pallas kernels  5.94 us (14%)
  other arithmetic  0.82 us (2%)
  between operations  0.8 us (2%)
  local copies, waits for them, and re-layouts  0.69 us (2%)
    pallas_call x11, Pallas kernels, call(): pl.pallas_call(kernel, in_specs=[space(far, i) for i in range(len(operand...  5.94 us
    ppermute x2, waiting for transfers between devices, collect(): from_p2 = lax.ppermute(to_p2, 'sub', far)  4.58 us
    ppermute x2, starting transfers between devices, collect(): from_p2 = lax.ppermute(to_p2, 'sub', far)  3.73 us
    all_to_all x1, starting transfers between devices, on_device(): all_sums = lax.all_to_all(sums, ('board', 'sub'), 0, 0)  3.23 us
    ppermute x1, starting transfers between devices, on_device(): p1 = lax.ppermute(jnp.stack([z, other]), 'sub', near)  2.83 us
    ppermute x1, waiting for transfers between devices, on_device(): p2 = lax.ppermute(own, 'sub', far)  2.11 us
    ppermute x1, starting transfers between devices, on_device(): p1 = lax.ppermute(four, 'sub', near)  1.7 us
    ppermute x1, starting transfers between devices, on_device(): conds = lax.ppermute(pads_sent, 'board', across)  1.58 us
  transfers between devices with their start and end apart: 18, of which 10 were waited for; matrix products, arithmetic and copies ran while one was open for 0% of the time, Pallas kernels for 6%

profile of v3, /device:TPU:0, one launch (start us, length us, event | category | flops | bytes accessed | tf_op | source)
XLA Modules:
  0.0 40.8 jit_solution(6664501514539534152)
XLA Ops:
  0.6 0.8 %broadcast_multiply_fusion.own.z.start_own = f32[32,256]{1,0:T(8,128)S(1)} fusion(f32[256]{0:T(256)} %bitcast.12, f32[1,32,256]{2,1,0:T(8,128)} %param.7), kind=kLoop, calls=%fused_computation.2 | loop fusion | flops 8192 | bytes 66560 | tf_op jit(solution)/shard_map/mul | solution.py:441
  1.9 0.9 %collective-permute-done.a = f32[32,256]{1,0:T(8,128)S(1)} collective-permute-done((f32[32,256]{1,0:T(8,128)S(1)}, f32[32,256]{1,0:T(8,128)S(1)}, u32[]{:S(2)}, u32[]{:S(2)}) %collective-permute-start) | collective-permute-done | bytes 32800 | tf_op jit(solution)/shard_map/ppermute | solution.py:459
  2.7 2.8 %collective-permute-start.1 = (f32[2,32,256]{2,1,0:T(8,128)S(1)}, f32[2,32,256]{2,1,0:T(8,128)S(1)}, u32[]{:S(2)}, u32[]{:S(2)}) collective-permute-start(f32[2,32,256]{2,1,0:T(8,128)S(1)} %pad_maximum_fusion.1), channel_id=1, source_target_pairs={{0,2},{1,0},{2,4},{3,1},{4,6},{5,3},{6,8},{7,5},{8,10},{9,7},{10,1... | collective-permute-start | bytes 196616 | tf_op jit(solution)/shard_map/ppermute | solution.py:461
  5.6 1.5 %collective-permute-start.2 = (f32[32,256]{1,0:T(8,128)S(1)}, f32[32,256]{1,0:T(8,128)S(1)}, u32[]{:S(2)}, u32[]{:S(2)}) collective-permute-start(f32[32,256]{1,0:T(8,128)S(1)} %broadcast_multiply_fusion.own.z.start_own), channel_id=1, source_target_pairs={{0,2},{1,4},{2,0},{3,6},{4,1},{5,8},{6,3},{7,10},{8,5},{9,12},{10,... | collective-permute-start | bytes 98312 | tf_op jit(solution)/shard_map/ppermute | solution.py:460
  7.8 2.0 %shard_map.86 = (bf16[768,768]{1,0:T(8,128)(2,1)S(1)}, bf16[768,768]{1,0:T(8,128)(2,1)S(1)}, bf16[768,768]{1,0:T(8,128)(2,1)S(1)}, f32[86,8,128]{2,1,0:T(8,128)S(1)}, f32[8,128]{1,0:T(8,128)S(1)}) custom-call(f32[768,768]{1,0:T(8,128)} %bitcast.13, s32[1,6]{1,0:T(1,128)S(1)} %copy-done.3), custom_call_target="tpu_custom_call" | custom-call | tf_op jit(solution)/shard_map/pallas_call | solution.py:413
  10.0 1.1 %collective-permute-done.3.b = f32[2,32,256]{2,1,0:T(8,128)S(1)} collective-permute-done((f32[2,32,256]{2,1,0:T(8,128)S(1)}, f32[2,32,256]{2,1,0:T(8,128)S(1)}, u32[]{:S(2)}, u32[]{:S(2)}) %collective-permute-start.3) | collective-permute-done | bytes 65568 | tf_op jit(solution)/shard_map/ppermute | solution.py:463
  11.1 0.7 %shard_map.87 = (f32[4,32,128]{2,1,0:T(8,128)S(1)}, f32[4,32,128]{2,1,0:T(8,128)S(1)}, f32[2,32,128]{2,1,0:T(8,128)S(1)}, f32[4,32,128]{2,1,0:T(8,128)S(1)}, f32...) custom-call(f32[86,8,128]{2,1,0:T(8,128)S(1)} %get-tuple-element.52.places, bf16[768,768]{1,0:T(8,128)(2,1)S(1)} %get-tuple-element.53.high, ...), custom_call_target="tpu_custom_call" | custom-call | tf_op jit(solution)/shard_map/pallas_call | solution.py:413
  12.3 1.6 %collective-permute-start.4 = (f32[136,128]{1,0:T(8,128)S(1)}, f32[136,128]{1,0:T(8,128)S(1)}, u32[]{:S(2)}, u32[]{:S(2)}) collective-permute-start(f32[136,128]{1,0:T(8,128)S(1)} %get-tuple-element.59.mine), channel_id=1, source_target_pairs={{0,16},{16,0},{1,17},{17,1},{2,18},{18,2},{3,19},{19,3},{4,20},{20... | collective-permute-start | bytes 208904 | tf_op jit(solution)/shard_map/ppermute | solution.py:470
  14.0 2.0 %collective-permute-start.7 = (f32[2,32,128]{2,1,0:T(8,128)S(1)}, f32[2,32,128]{2,1,0:T(8,128)S(1)}, u32[]{:S(2)}, u32[]{:S(2)}) collective-permute-start(f32[2,32,128]{2,1,0:T(8,128)S(1)} %get-tuple-element.64), channel_id=1, source_target_pairs={{0,2},{1,4},{2,0},{3,6},{4,1},{5,8},{6,3},{7,10},{8,5},{9,12},{10,... | collective-permute-start | bytes 98312 | tf_op jit(solution)/shard_map/ppermute | solution.py:455
  16.0 0.8 %collective-permute-done.4.conds = f32[136,128]{1,0:T(8,128)S(1)} collective-permute-done((f32[136,128]{1,0:T(8,128)S(1)}, f32[136,128]{1,0:T(8,128)S(1)}, u32[]{:S(2)}, u32[]{:S(2)}) %collective-permute-start.4) | collective-permute-done | bytes 69664 | tf_op jit(solution)/shard_map/ppermute | solution.py:470
  16.9 1.6 %collective-permute-done.7.from_p2 = f32[2,32,128]{2,1,0:T(8,128)S(1)} collective-permute-done((f32[2,32,128]{2,1,0:T(8,128)S(1)}, f32[2,32,128]{2,1,0:T(8,128)S(1)}, u32[]{:S(2)}, u32[]{:S(2)}) %collective-permute-start.7) | collective-permute-done | bytes 32800 | tf_op jit(solution)/shard_map/ppermute | solution.py:455
  18.6 0.9 %collective-permute-start.8 = (f32[5,32,128]{2,1,0:T(8,128)S(1)}, f32[5,32,128]{2,1,0:T(8,128)S(1)}, u32[]{:S(2)}, u32[]{:S(2)}) collective-permute-start(f32[5,32,128]{2,1,0:T(8,128)S(1)} %shard_map.90.part), channel_id=1, source_target_pairs={{0,1},{1,0},{2,3},{3,2},{4,5},{5,4},{6,7},{7,6},{8,9},{9,8},{10,11... | collective-permute-start | bytes 245768 | tf_op jit(solution)/shard_map/ppermute | solution.py:475
  19.4 0.7 %collective-permute-start.11 = (f32[5,32,128]{2,1,0:T(8,128)S(1)}, f32[5,32,128]{2,1,0:T(8,128)S(1)}, u32[]{:S(2)}, u32[]{:S(2)}) collective-permute-start(f32[5,32,128]{2,1,0:T(8,128)S(1)} %shard_map.90.part), channel_id=1, source_target_pairs={{0,16},{16,0},{1,17},{17,1},{2,18},{18,2},{3,19},{19,3},{4,20},{20... | collective-permute-start | bytes 245768 | tf_op jit(solution)/shard_map/ppermute | solution.py:476
  20.4 1.7 %collective-permute-start.9 = (f32[4,32,128]{2,1,0:T(8,128)S(1)}, f32[4,32,128]{2,1,0:T(8,128)S(1)}, u32[]{:S(2)}, u32[]{:S(2)}) collective-permute-start(f32[4,32,128]{2,1,0:T(8,128)S(1)} %get-tuple-element.68), channel_id=1, source_target_pairs={{0,2},{1,0},{2,4},{3,1},{4,6},{5,3},{6,8},{7,5},{8,10},{9,7},{10,1... | collective-permute-start | bytes 196616 | tf_op jit(solution)/shard_map/ppermute | solution.py:483
  22.1 1.4 %collective-permute-start.10 = (f32[2,32,128]{2,1,0:T(8,128)S(1)}, f32[2,32,128]{2,1,0:T(8,128)S(1)}, u32[]{:S(2)}, u32[]{:S(2)}) collective-permute-start(f32[2,32,128]{2,1,0:T(8,128)S(1)} %get-tuple-element.67.own.scaled), channel_id=1, source_target_pairs={{0,2},{1,4},{2,0},{3,6},{4,1},{5,8},{6,3},{7,10},{8,5},{9,12},{10,... | collective-permute-start | bytes 98312 | tf_op jit(solution)/shard_map/ppermute | solution.py:484
  23.9 2.1 %collective-permute-done.10.p2 = f32[2,32,128]{2,1,0:T(8,128)S(1)} collective-permute-done((f32[2,32,128]{2,1,0:T(8,128)S(1)}, f32[2,32,128]{2,1,0:T(8,128)S(1)}, u32[]{:S(2)}, u32[]{:S(2)}) %collective-permute-start.10) | collective-permute-done | bytes 32800 | tf_op jit(solution)/shard_map/ppermute | solution.py:484
  26.1 1.3 %collective-permute-done.12.b = f32[6,32,128]{2,1,0:T(8,128)S(1)} collective-permute-done((f32[6,32,128]{2,1,0:T(8,128)S(1)}, f32[6,32,128]{2,1,0:T(8,128)S(1)}, u32[]{:S(2)}, u32[]{:S(2)}) %collective-permute-start.12) | collective-permute-done | bytes 98336 | tf_op jit(solution)/shard_map/ppermute | solution.py:486
  27.4 1.8 %shard_map.93 = (f32[17,8,128]{2,1,0:T(8,128)S(1)}, f32[17,8,128]{2,1,0:T(8,128)S(1)}, f32[9,8,128]{2,1,0:T(8,128)S(1)}, f32[4,32,128]{2,1,0:T(8,128)S(1)}, f32[32,4,128]{2,1,0:T(4,128)}) custom-call(f32[86,8,128]{2,1,0:T(8,128)S(1)} %get-tuple-element.52.places, bf16[768,768]{1,0:T(8,128)(2,1)S(1)} %get-tuple-element.53.high, ...), custom_call_target="tpu_custom_call" | custom-call | tf_op jit(solution)/shard_map/pallas_call | solution.py:413
  29.3 3.2 %all-to-all-start = ((f32[32,4,128]{2,1,0:T(4,128)}), f32[32,4,128]{2,1,0:T(4,128)S(1)}, u32[]{:S(2)}, u32[]{:S(2)}) async-start(f32[32,4,128]{2,1,0:T(4,128)} %get-tuple-element.86), calls=%async_computation | async-start | bytes 131072 | tf_op jit(solution)/shard_map/all_to_all | solution.py:496
  32.8 1.8 %collective-permute-start.15 = (f32[9,8,128]{2,1,0:T(8,128)S(1)}, f32[9,8,128]{2,1,0:T(8,128)S(1)}, u32[]{:S(2)}, u32[]{:S(2)}) collective-permute-start(f32[9,8,128]{2,1,0:T(8,128)S(1)} %get-tuple-element.83), channel_id=1, source_target_pairs={{0,2},{1,4},{2,0},{3,6},{4,1},{5,8},{6,3},{7,10},{8,5},{9,12},{10,... | collective-permute-start | bytes 110600 | tf_op jit(solution)/shard_map/ppermute | solution.py:455
  34.6 2.9 %collective-permute-done.15.from_p2 = f32[9,8,128]{2,1,0:T(8,128)S(1)} collective-permute-done((f32[9,8,128]{2,1,0:T(8,128)S(1)}, f32[9,8,128]{2,1,0:T(8,128)S(1)}, u32[]{:S(2)}, u32[]{:S(2)}) %collective-permute-start.15) | collective-permute-done | bytes 36896 | tf_op jit(solution)/shard_map/ppermute | solution.py:455
  37.6 1.4 %collective-permute-start.16 = (f32[9,8,128]{2,1,0:T(8,128)S(1)}, f32[9,8,128]{2,1,0:T(8,128)S(1)}, u32[]{:S(2)}, u32[]{:S(2)}) collective-permute-start(f32[9,8,128]{2,1,0:T(8,128)S(1)} %get-tuple-element.87), channel_id=1, source_target_pairs={{0,1},{1,0},{2,3},{3,2},{4,5},{5,4},{6,7},{7,6},{8,9},{9,8},{10,11... | collective-permute-start | bytes 110600 | tf_op jit(solution)/shard_map/ppermute | solution.py:500
  39.0 0.9 %all-to-all-done.sums = f32[32,4,128]{2,1,0:T(4,128)S(1)} async-done(((f32[32,4,128]{2,1,0:T(4,128)}), f32[32,4,128]{2,1,0:T(4,128)S(1)}, u32[]{:S(2)}, u32[]{:S(2)}) %all-to-all-start) | async-done | bytes 65568 | tf_op jit(solution)/shard_map/all_to_all | solution.py:496
  40.1 0.7 %shard_map.96 = (f32[32,256]{1,0:T(8,128)}, f32[32,256]{1,0:T(8,128)}) custom-call(f32[32,256]{1,0:T(8,128)S(1)} %bitcast.10, f32[32,256]{1,0:T(8,128)S(1)} %broadcast_multiply_fusion.own.z.start_own, f32[32,256]{1,0:T(8,128)S(1)} %get-tuple-element.66.image, f32[2,32,128]{2,1,0:T(8,128)S(1)} %get-tuple-element.67.own.scaled, ...), custom_call_target="tpu_custom_call" | custom-call | tf_op jit(solution)/shard_map/pallas_call | solution.py:413
  (42 shorter events, 3.5 us)
Async XLA Ops:
  1.4 1.3 %collective-permute-start = (f32[32,256]{1,0:T(8,128)S(1)}, f32[32,256]{1,0:T(8,128)S(1)}, u32[]{:S(2)}, u32[]{:S(2)}) collective-permute-start(f32[32,256]{1,0:T(8,128)S(1)} %broadcast_multiply_fusion.own.z.start_own), channel_id=1, source_target_pairs={{0,1},{1,0},{2,3},{3,2},{4,5},{5,4},{6,7},{7,6},{8,9},{9,8},{10,11... | collective-permute-start | bytes 98312 | tf_op jit(solution)/shard_map/ppermute | solution.py:459
  2.7 7.0 %collective-permute-start.1 = (f32[2,32,256]{2,1,0:T(8,128)S(1)}, f32[2,32,256]{2,1,0:T(8,128)S(1)}, u32[]{:S(2)}, u32[]{:S(2)}) collective-permute-start(f32[2,32,256]{2,1,0:T(8,128)S(1)} %pad_maximum_fusion.1), channel_id=1, source_target_pairs={{0,2},{1,0},{2,4},{3,1},{4,6},{5,3},{6,8},{7,5},{8,10},{9,7},{10,1... | collective-permute-start | bytes 196616 | tf_op jit(solution)/shard_map/ppermute | solution.py:461
  5.6 4.2 %collective-permute-start.2 = (f32[32,256]{1,0:T(8,128)S(1)}, f32[32,256]{1,0:T(8,128)S(1)}, u32[]{:S(2)}, u32[]{:S(2)}) collective-permute-start(f32[32,256]{1,0:T(8,128)S(1)} %broadcast_multiply_fusion.own.z.start_own), channel_id=1, source_target_pairs={{0,2},{1,4},{2,0},{3,6},{4,1},{5,8},{6,3},{7,10},{8,5},{9,12},{10,... | collective-permute-start | bytes 98312 | tf_op jit(solution)/shard_map/ppermute | solution.py:460
  7.1 0.7 %copy-start.3 = (s32[1,6]{1,0:T(1,128)S(1)}, s32[1,6]{1,0:T(1,128)}, u32[]{:S(2)}) copy-start(s32[1,6]{1,0:T(1,128)} %blocks.1) | copy-start | bytes 76
  9.8 2.3 %copy-start.4 = (s32[1,64]{1,0:T(1,128)S(1)}, s32[1,64]{1,0:T(1,128)}, u32[]{:S(2)}) copy-start(s32[1,64]{1,0:T(1,128)} %pad_rows.1) | copy-start | bytes 772
  9.8 2.3 %copy-start.5 = (f32[1,64]{1,0:T(1,128)S(1)}, f32[1,64]{1,0:T(1,128)}, u32[]{:S(2)}) copy-start(f32[1,64]{1,0:T(1,128)} %pad_cond.1) | copy-start | bytes 772
  9.8 7.0 %copy-start.2 = (f32[1,256]{1,0:T(1,128)S(1)}, f32[1,256]{1,0:T(1,128)}, u32[]{:S(2)}) copy-start(f32[1,256]{1,0:T(1,128)} %sink.5) | copy-start | bytes 3076
  9.8 8.8 %copy-start.1 = (f32[1,256]{1,0:T(1,128)S(1)}, f32[1,256]{1,0:T(1,128)}, u32[]{:S(2)}) copy-start(f32[1,256]{1,0:T(1,128)} %precond.5) | copy-start | bytes 3076
  9.8 1.3 %collective-permute-start.3 = (f32[2,32,256]{2,1,0:T(8,128)S(1)}, f32[2,32,256]{2,1,0:T(8,128)S(1)}, u32[]{:S(2)}, u32[]{:S(2)}) collective-permute-start(f32[2,32,256]{2,1,0:T(8,128)S(1)} %collective-permute-done.1.p1), channel_id=1, source_target_pairs={{0,1},{1,0},{2,3},{3,2},{4,5},{5,4},{6,7},{7,6},{8,9},{9,8},{10,11... | collective-permute-start | bytes 196616 | tf_op jit(solution)/shard_map/ppermute | solution.py:463
  11.9 11.6 %copy-start = (f32[1,32,256]{2,1,0:T(8,128)S(1)}, f32[1,32,256]{2,1,0:T(8,128)}, u32[]{:S(2)}) copy-start(f32[1,32,256]{2,1,0:T(8,128)} %param.7) | copy-start | bytes 98308
  11.9 2.0 %collective-permute-start.5 = (f32[4,32,128]{2,1,0:T(8,128)S(1)}, f32[4,32,128]{2,1,0:T(8,128)S(1)}, u32[]{:S(2)}, u32[]{:S(2)}) collective-permute-start(f32[4,32,128]{2,1,0:T(8,128)S(1)} %get-tuple-element.63), channel_id=1, source_target_pairs={{0,1},{1,0},{2,3},{3,2},{4,5},{5,4},{6,7},{7,6},{8,9},{9,8},{10,11... | collective-permute-start | bytes 196616 | tf_op jit(solution)/shard_map/ppermute | solution.py:456
  12.3 4.5 %collective-permute-start.4 = (f32[136,128]{1,0:T(8,128)S(1)}, f32[136,128]{1,0:T(8,128)S(1)}, u32[]{:S(2)}, u32[]{:S(2)}) collective-permute-start(f32[136,128]{1,0:T(8,128)S(1)} %get-tuple-element.59.mine), channel_id=1, source_target_pairs={{0,16},{16,0},{1,17},{17,1},{2,18},{18,2},{3,19},{19,3},{4,20},{20... | collective-permute-start | bytes 208904 | tf_op jit(solution)/shard_map/ppermute | solution.py:470
  13.9 4.7 %collective-permute-start.6 = (f32[4,32,128]{2,1,0:T(8,128)S(1)}, f32[4,32,128]{2,1,0:T(8,128)S(1)}, u32[]{:S(2)}, u32[]{:S(2)}) collective-permute-start(f32[4,32,128]{2,1,0:T(8,128)S(1)} %add.6), channel_id=1, source_target_pairs={{2,0},{0,1},{4,2},{1,3},{6,4},{3,5},{8,6},{5,7},{10,8},{7,9},{12,1... | collective-permute-start | bytes 196616 | tf_op jit(solution)/shard_map/ppermute | solution.py:473
  14.0 4.5 %collective-permute-start.7 = (f32[2,32,128]{2,1,0:T(8,128)S(1)}, f32[2,32,128]{2,1,0:T(8,128)S(1)}, u32[]{:S(2)}, u32[]{:S(2)}) collective-permute-start(f32[2,32,128]{2,1,0:T(8,128)S(1)} %get-tuple-element.64), channel_id=1, source_target_pairs={{0,2},{1,4},{2,0},{3,6},{4,1},{5,8},{6,3},{7,10},{8,5},{9,12},{10,... | collective-permute-start | bytes 98312 | tf_op jit(solution)/shard_map/ppermute | solution.py:455
  18.6 1.8 %collective-permute-start.8 = (f32[5,32,128]{2,1,0:T(8,128)S(1)}, f32[5,32,128]{2,1,0:T(8,128)S(1)}, u32[]{:S(2)}, u32[]{:S(2)}) collective-permute-start(f32[5,32,128]{2,1,0:T(8,128)S(1)} %shard_map.90.part), channel_id=1, source_target_pairs={{0,1},{1,0},{2,3},{3,2},{4,5},{5,4},{6,7},{7,6},{8,9},{9,8},{10,11... | collective-permute-start | bytes 245768 | tf_op jit(solution)/shard_map/ppermute | solution.py:475
  19.4 4.4 %collective-permute-start.11 = (f32[5,32,128]{2,1,0:T(8,128)S(1)}, f32[5,32,128]{2,1,0:T(8,128)S(1)}, u32[]{:S(2)}, u32[]{:S(2)}) collective-permute-start(f32[5,32,128]{2,1,0:T(8,128)S(1)} %shard_map.90.part), channel_id=1, source_target_pairs={{0,16},{16,0},{1,17},{17,1},{2,18},{18,2},{3,19},{19,3},{4,20},{20... | collective-permute-start | bytes 245768 | tf_op jit(solution)/shard_map/ppermute | solution.py:476
  20.4 5.6 %collective-permute-start.9 = (f32[4,32,128]{2,1,0:T(8,128)S(1)}, f32[4,32,128]{2,1,0:T(8,128)S(1)}, u32[]{:S(2)}, u32[]{:S(2)}) collective-permute-start(f32[4,32,128]{2,1,0:T(8,128)S(1)} %get-tuple-element.68), channel_id=1, source_target_pairs={{0,2},{1,0},{2,4},{3,1},{4,6},{5,3},{6,8},{7,5},{8,10},{9,7},{10,1... | collective-permute-start | bytes 196616 | tf_op jit(solution)/shard_map/ppermute | solution.py:483
  22.1 3.9 %collective-permute-start.10 = (f32[2,32,128]{2,1,0:T(8,128)S(1)}, f32[2,32,128]{2,1,0:T(8,128)S(1)}, u32[]{:S(2)}, u32[]{:S(2)}) collective-permute-start(f32[2,32,128]{2,1,0:T(8,128)S(1)} %get-tuple-element.67.own.scaled), channel_id=1, source_target_pairs={{0,2},{1,4},{2,0},{3,6},{4,1},{5,8},{6,3},{7,10},{8,5},{9,12},{10,... | collective-permute-start | bytes 98312 | tf_op jit(solution)/shard_map/ppermute | solution.py:484
  26.0 1.4 %collective-permute-start.12 = (f32[6,32,128]{2,1,0:T(8,128)S(1)}, f32[6,32,128]{2,1,0:T(8,128)S(1)}, u32[]{:S(2)}, u32[]{:S(2)}) collective-permute-start(f32[6,32,128]{2,1,0:T(8,128)S(1)} %pad_maximum_fusion), channel_id=1, source_target_pairs={{0,1},{1,0},{2,3},{3,2},{4,5},{5,4},{6,7},{7,6},{8,9},{9,8},{10,11... | collective-permute-start | bytes 294920 | tf_op jit(solution)/shard_map/ppermute | solution.py:486
  29.1 3.4 %collective-permute-start.13 = (f32[17,8,128]{2,1,0:T(8,128)S(1)}, f32[17,8,128]{2,1,0:T(8,128)S(1)}, u32[]{:S(2)}, u32[]{:S(2)}) collective-permute-start(f32[17,8,128]{2,1,0:T(8,128)S(1)} %get-tuple-element.82), channel_id=1, source_target_pairs={{0,1},{1,0},{2,3},{3,2},{4,5},{5,4},{6,7},{7,6},{8,9},{9,8},{10,11... | collective-permute-start | bytes 208904 | tf_op jit(solution)/shard_map/ppermute | solution.py:456
  29.3 10.6 %all-to-all-start = ((f32[32,4,128]{2,1,0:T(4,128)}), f32[32,4,128]{2,1,0:T(4,128)S(1)}, u32[]{:S(2)}, u32[]{:S(2)}) async-start(f32[32,4,128]{2,1,0:T(4,128)} %get-tuple-element.86), calls=%async_computation | async-start | bytes 131072 | tf_op jit(solution)/shard_map/all_to_all | solution.py:496
  32.5 5.0 %collective-permute-start.14 = (f32[17,8,128]{2,1,0:T(8,128)S(1)}, f32[17,8,128]{2,1,0:T(8,128)S(1)}, u32[]{:S(2)}, u32[]{:S(2)}) collective-permute-start(f32[17,8,128]{2,1,0:T(8,128)S(1)} %add.7), channel_id=1, source_target_pairs={{2,0},{0,1},{4,2},{1,3},{6,4},{3,5},{8,6},{5,7},{10,8},{7,9},{12,1... | collective-permute-start | bytes 208904 | tf_op jit(solution)/shard_map/ppermute | solution.py:495
  32.8 4.7 %collective-permute-start.15 = (f32[9,8,128]{2,1,0:T(8,128)S(1)}, f32[9,8,128]{2,1,0:T(8,128)S(1)}, u32[]{:S(2)}, u32[]{:S(2)}) collective-permute-start(f32[9,8,128]{2,1,0:T(8,128)S(1)} %get-tuple-element.83), channel_id=1, source_target_pairs={{0,2},{1,4},{2,0},{3,6},{4,1},{5,8},{6,3},{7,10},{8,5},{9,12},{10,... | collective-permute-start | bytes 110600 | tf_op jit(solution)/shard_map/ppermute | solution.py:455
  37.6 2.3 %collective-permute-start.16 = (f32[9,8,128]{2,1,0:T(8,128)S(1)}, f32[9,8,128]{2,1,0:T(8,128)S(1)}, u32[]{:S(2)}, u32[]{:S(2)}) collective-permute-start(f32[9,8,128]{2,1,0:T(8,128)S(1)} %get-tuple-element.87), channel_id=1, source_target_pairs={{0,1},{1,0},{2,3},{3,2},{4,5},{5,4},{6,7},{7,6},{8,9},{9,8},{10,11... | collective-permute-start | bytes 110600 | tf_op jit(solution)/shard_map/ppermute | solution.py:500

commit v4 on v3

--- a/solution.py
+++ b/solution.py
@@ -102,14 +102,7 @@
     pads_out[cases + 8 : cases + 9, :count] = pad_rows[...].astype(F32)
 
 
-def prepare_kernel(schur, blocks, high, middle, low, places, top, held, sems):
-    chunk = held.shape[0] // sems.shape[0]
-    copies = []
-    for i in range(sems.shape[0]):
-        rows = slice(i * chunk, (i + 1) * chunk)
-        copies.append(pltpu.make_async_copy(schur.at[rows], held.at[rows], sems.at[i]))
-    for copy in copies:
-        copy.start()
+def places_kernel(blocks, places):
     position = lax.axis_index("sub")
     chip, core = position // 2, lax.rem(position, 2)
     above, below = lax.axis_size("sub") // 2 - 1 - chip, chip
@@ -128,6 +121,16 @@
     far = jnp.where(core == 0, below, above) >= 2
     for i, sender in enumerate((near, far)):
         places[touched * spots + i] = jnp.full(places.shape[1:], sender.astype(F32))
+
+
+def split_kernel(schur, high, middle, low, top, held, sems):
+    chunk = held.shape[0] // sems.shape[0]
+    copies = []
+    for i in range(sems.shape[0]):
+        rows = slice(i * chunk, (i + 1) * chunk)
+        copies.append(pltpu.make_async_copy(schur.at[rows], held.at[rows], sems.at[i]))
+    for copy in copies:
+        copy.start()
     largest = jnp.ones((1, chunk), F32)
     for i, copy in enumerate(copies):
         rows = slice(i * chunk, (i + 1) * chunk)
@@ -177,10 +180,10 @@
 
 
 def first_kernel(
-    places, high, middle, low, p2, p1, own, a, b, back, to_p1, to_p2, kept, picked_out, product_out
+    places, high, middle, low, p2, p1, four, b, back, to_p1, to_p2, kept, picked_out, product_out
 ):
     touched = high.shape[0] // BR
-    picked = picked_blocks(places, halves(p2, p1[0], p1[1], own, a, b[0], b[1]), touched)
+    picked = picked_blocks(places, halves(p2, p1[0], p1[1], four[0], four[1], b[0], b[1]), touched)
     product = product_of(4.0 * picked, high, middle, low)
     landed = landed_blocks(places, product)
     for j in range(2):
@@ -442,13 +445,14 @@
     ones, pads_sent = call(begin_kernel, [((owned, pads), HALF), ((4 * cases + 8, BR), F32)], z, pad_rows, pad_cond)
     chunks = touched
     spots = 2 * (2 * REACH + 1)
-    high, middle, low, places, top = call(
-        prepare_kernel,
-        [((inner, inner), HALF)] * 3 + [((touched * spots + 2, 8, BR), F32), tile],
-        matrix, block_list,
+    (places,) = call(places_kernel, [((touched * spots + 2, 8, BR), F32)], block_list)
+    high, middle, low, top = call(
+        split_kernel,
+        [((inner, inner), HALF)] * 3 + [tile],
+        matrix,
         far=range(1),
         scratch=[pltpu.VMEM((inner, inner), F32), semaphores((chunks,))],
-        grant=48,
+        grant=49,
     )
 
     def collect(back, to_p1, to_p2):
@@ -456,16 +460,17 @@
         to_p1 = to_p1 + lax.ppermute(back, "sub", swap)
         return to_p1, from_p2
 
-    other = lax.ppermute(z, "sub", swap)
+    scale_there = lax.ppermute(precond, "sub", swap)
+    four = barrier(jnp.stack([z, scale_there * lax.ppermute(rhs[0], "sub", swap)]))
     p2 = lax.ppermute(z, "sub", far)
-    p1 = lax.ppermute(jnp.stack([z, other]), "sub", near)
-    p1, p2, high, middle, low, places, top = barrier((p1, p2, high, middle, low, places, top))
+    p1 = lax.ppermute(four, "sub", near)
+    p1, p2, high, middle, low, top = barrier((p1, p2, high, middle, low, top))
     b = lax.ppermute(p1, "sub", swap)
     split = (places, high, middle, low)
     back, to_p1, to_p2, kept, start_picked, start_product = call(
         first_kernel,
         [both, both, pair, both, ((cases, inner), F32), ((cases, inner), F32)],
-        *split, p2, p1, z, other, b,
+        *split, p2, p1, four, b,
     )
     conds = lax.ppermute(pads_sent, "board", across)
     local, start_jump = call(ties_kernel, [full, ((cases, pads), F32)], z, pads_sent, conds, ones, sink)

time: 41.1 us -> 40.8 us (level)
  local copies, waits for them, and re-layouts: 0.69 us -> 0.04 us
    ppermute x1 -> x2, starting transfers between devices: 1.7 us -> 4.4 us  [on_device(): p1 = lax.ppermute(four, 'sub', near)]
    ppermute x2, starting transfers between devices: 3.29 us -> 0.6 us  [the longest x1 0.52 us: on_device(): scale_there = lax.ppermute(precond, 'sub', swap)]
    unnamed x12, local copies, waits for them, and re-layouts: 0.69 us -> 0.04 us
    all_to_all x1, starting transfers between devices: 3.23 us -> 3.69 us  [on_device(): all_sums = lax.all_to_all(sums, ('board', 'sub'), 0, 0)]
    pallas_call x11 -> x12, Pallas kernels: 5.94 us -> 6.02 us  [call(): pl.pallas_call(kernel, in_specs=[space(far, i) for i in range(len(operand...]
  transfers between devices with their start and end apart: 18 -> 19, of which waited for: 10 -> 12; matrix products, arithmetic and copies ran while one was open for 0% -> 2% of each run, Pallas kernels for 6% -> 7%
where the time goes in v4:
time: 40.8 us; the launch traced here: 40.6 us
  starting transfers between devices  20.7 us (51%)
  waiting for transfers between devices  12.2 us (30%)
  Pallas kernels  6.02 us (15%)
  other arithmetic  0.82 us (2%)
  between operations  0.8 us (2%)
    pallas_call x12, Pallas kernels, call(): pl.pallas_call(kernel, in_specs=[space(far, i) for i in range(len(operand...  6.02 us
    ppermute x2, waiting for transfers between devices, collect(): from_p2 = lax.ppermute(to_p2, 'sub', far)  4.58 us
    ppermute x2, starting transfers between devices, on_device(): p1 = lax.ppermute(four, 'sub', near)  4.4 us
    ppermute x2, starting transfers between devices, collect(): from_p2 = lax.ppermute(to_p2, 'sub', far)  3.73 us
    all_to_all x1, starting transfers between devices, on_device(): all_sums = lax.all_to_all(sums, ('board', 'sub'), 0, 0)  3.69 us
    ppermute x1, waiting for transfers between devices, on_device(): p2 = lax.ppermute(own, 'sub', far)  2.11 us
    ppermute x1, starting transfers between devices, on_device(): conds = lax.ppermute(pads_sent, 'board', across)  1.58 us
    ppermute x1, starting transfers between devices, on_device(): p2 = lax.ppermute(z, 'sub', far)  1.55 us
  transfers between devices with their start and end apart: 19, of which 12 were waited for; matrix products, arithmetic and copies ran while one was open for 2% of the time, Pallas kernels for 7%

profile of v4, /device:TPU:0, one launch (start us, length us, event | category | flops | bytes accessed | tf_op | source)
XLA Modules:
  0.0 40.6 jit_solution(17481590010493784292)
XLA Ops:
  0.6 0.5 %collective-permute-start = (f32[1,256]{1,0:T(1,128)}, f32[1,256]{1,0:T(1,128)S(1)}, u32[]{:S(2)}, u32[]{:S(2)}) collective-permute-start(f32[1,256]{1,0:T(1,128)} %precond.5), channel_id=1, source_target_pairs={{0,1},{1,0},{2,3},{3,2},{4,5},{5,4},{6,7},{7,6},{8,9},{9,8},{10,11... | collective-permute-start | bytes 3080 | tf_op jit(solution)/shard_map/ppermute | solution.py:463
  1.2 0.8 %broadcast_multiply_fusion.z.start_own = f32[32,256]{1,0:T(8,128)S(1)} fusion(f32[256]{0:T(256)} %bitcast.14, f32[1,32,256]{2,1,0:T(8,128)} %param.7), kind=kLoop, calls=%fused_computation.3 | loop fusion | flops 8192 | bytes 66560 | tf_op jit(solution)/shard_map/mul | solution.py:444
  2.6 2.7 %collective-permute-start.2 = (f32[2,32,256]{2,1,0:T(8,128)S(1)}, f32[2,32,256]{2,1,0:T(8,128)S(1)}, u32[]{:S(2)}, u32[]{:S(2)}) collective-permute-start(f32[2,32,256]{2,1,0:T(8,128)S(1)} %pad_maximum_fusion.1.four), channel_id=1, source_target_pairs={{0,2},{1,0},{2,4},{3,1},{4,6},{5,3},{6,8},{7,5},{8,10},{9,7},{10,1... | collective-permute-start | bytes 196616 | tf_op jit(solution)/shard_map/ppermute | solution.py:466
  5.3 1.5 %collective-permute-start.3 = (f32[32,256]{1,0:T(8,128)S(1)}, f32[32,256]{1,0:T(8,128)S(1)}, u32[]{:S(2)}, u32[]{:S(2)}) collective-permute-start(f32[32,256]{1,0:T(8,128)S(1)} %broadcast_multiply_fusion.z.start_own), channel_id=1, source_target_pairs={{0,2},{1,4},{2,0},{3,6},{4,1},{5,8},{6,3},{7,10},{8,5},{9,12},{10,... | collective-permute-start | bytes 98312 | tf_op jit(solution)/shard_map/ppermute | solution.py:465
  6.8 2.0 %shard_map.87 = (bf16[768,768]{1,0:T(8,128)(2,1)S(1)}, bf16[768,768]{1,0:T(8,128)(2,1)S(1)}, bf16[768,768]{1,0:T(8,128)(2,1)S(1)}, f32[8,128]{1,0:T(8,128)S(1)}) custom-call(f32[768,768]{1,0:T(8,128)} %bitcast.15), custom_call_target="tpu_custom_call" | custom-call | tf_op jit(solution)/shard_map/pallas_call | solution.py:416
  9.4 1.1 %collective-permute-done.4.b = f32[2,32,256]{2,1,0:T(8,128)S(1)} collective-permute-done((f32[2,32,256]{2,1,0:T(8,128)S(1)}, f32[2,32,256]{2,1,0:T(8,128)S(1)}, u32[]{:S(2)}, u32[]{:S(2)}) %collective-permute-start.4) | collective-permute-done | bytes 65568 | tf_op jit(solution)/shard_map/ppermute | solution.py:468
  10.5 0.7 %shard_map.88 = (f32[4,32,128]{2,1,0:T(8,128)S(1)}, f32[4,32,128]{2,1,0:T(8,128)S(1)}, f32[2,32,128]{2,1,0:T(8,128)S(1)}, f32[4,32,128]{2,1,0:T(8,128)S(1)}, f32...) custom-call(f32[86,8,128]{2,1,0:T(8,128)S(1)} %shard_map.86.places, bf16[768,768]{1,0:T(8,128)(2,1)S(1)} %get-tuple-element.49.high, ...), custom_call_target="tpu_custom_call" | custom-call | tf_op jit(solution)/shard_map/pallas_call | solution.py:416
  11.6 1.6 %collective-permute-start.5 = (f32[136,128]{1,0:T(8,128)S(1)}, f32[136,128]{1,0:T(8,128)S(1)}, u32[]{:S(2)}, u32[]{:S(2)}) collective-permute-start(f32[136,128]{1,0:T(8,128)S(1)} %get-tuple-element.55.mine), channel_id=1, source_target_pairs={{0,16},{16,0},{1,17},{17,1},{2,18},{18,2},{3,19},{19,3},{4,20},{20... | collective-permute-start | bytes 208904 | tf_op jit(solution)/shard_map/ppermute | solution.py:475
  13.3 2.0 %collective-permute-start.8 = (f32[2,32,128]{2,1,0:T(8,128)S(1)}, f32[2,32,128]{2,1,0:T(8,128)S(1)}, u32[]{:S(2)}, u32[]{:S(2)}) collective-permute-start(f32[2,32,128]{2,1,0:T(8,128)S(1)} %get-tuple-element.60), channel_id=1, source_target_pairs={{0,2},{1,4},{2,0},{3,6},{4,1},{5,8},{6,3},{7,10},{8,5},{9,12},{10,... | collective-permute-start | bytes 98312 | tf_op jit(solution)/shard_map/ppermute | solution.py:459
  15.3 0.8 %collective-permute-done.5.conds = f32[136,128]{1,0:T(8,128)S(1)} collective-permute-done((f32[136,128]{1,0:T(8,128)S(1)}, f32[136,128]{1,0:T(8,128)S(1)}, u32[]{:S(2)}, u32[]{:S(2)}) %collective-permute-start.5) | collective-permute-done | bytes 69664 | tf_op jit(solution)/shard_map/ppermute | solution.py:475
  16.2 1.6 %collective-permute-done.8.from_p2 = f32[2,32,128]{2,1,0:T(8,128)S(1)} collective-permute-done((f32[2,32,128]{2,1,0:T(8,128)S(1)}, f32[2,32,128]{2,1,0:T(8,128)S(1)}, u32[]{:S(2)}, u32[]{:S(2)}) %collective-permute-start.8) | collective-permute-done | bytes 32800 | tf_op jit(solution)/shard_map/ppermute | solution.py:459
  17.9 0.9 %collective-permute-start.9 = (f32[5,32,128]{2,1,0:T(8,128)S(1)}, f32[5,32,128]{2,1,0:T(8,128)S(1)}, u32[]{:S(2)}, u32[]{:S(2)}) collective-permute-start(f32[5,32,128]{2,1,0:T(8,128)S(1)} %shard_map.91.part), channel_id=1, source_target_pairs={{0,1},{1,0},{2,3},{3,2},{4,5},{5,4},{6,7},{7,6},{8,9},{9,8},{10,11... | collective-permute-start | bytes 245768 | tf_op jit(solution)/shard_map/ppermute | solution.py:480
  18.8 0.9 %collective-permute-start.12 = (f32[5,32,128]{2,1,0:T(8,128)S(1)}, f32[5,32,128]{2,1,0:T(8,128)S(1)}, u32[]{:S(2)}, u32[]{:S(2)}) collective-permute-start(f32[5,32,128]{2,1,0:T(8,128)S(1)} %shard_map.91.part), channel_id=1, source_target_pairs={{0,16},{16,0},{1,17},{17,1},{2,18},{18,2},{3,19},{19,3},{4,20},{20... | collective-permute-start | bytes 245768 | tf_op jit(solution)/shard_map/ppermute | solution.py:481
  19.7 1.7 %collective-permute-start.10 = (f32[4,32,128]{2,1,0:T(8,128)S(1)}, f32[4,32,128]{2,1,0:T(8,128)S(1)}, u32[]{:S(2)}, u32[]{:S(2)}) collective-permute-start(f32[4,32,128]{2,1,0:T(8,128)S(1)} %get-tuple-element.64), channel_id=1, source_target_pairs={{0,2},{1,0},{2,4},{3,1},{4,6},{5,3},{6,8},{7,5},{8,10},{9,7},{10,1... | collective-permute-start | bytes 196616 | tf_op jit(solution)/shard_map/ppermute | solution.py:488
  21.4 1.1 %collective-permute-start.11 = (f32[2,32,128]{2,1,0:T(8,128)S(1)}, f32[2,32,128]{2,1,0:T(8,128)S(1)}, u32[]{:S(2)}, u32[]{:S(2)}) collective-permute-start(f32[2,32,128]{2,1,0:T(8,128)S(1)} %get-tuple-element.63.own.scaled), channel_id=1, source_target_pairs={{0,2},{1,4},{2,0},{3,6},{4,1},{5,8},{6,3},{7,10},{8,5},{9,12},{10,... | collective-permute-start | bytes 98312 | tf_op jit(solution)/shard_map/ppermute | solution.py:489
  23.2 2.1 %collective-permute-done.11.p2 = f32[2,32,128]{2,1,0:T(8,128)S(1)} collective-permute-done((f32[2,32,128]{2,1,0:T(8,128)S(1)}, f32[2,32,128]{2,1,0:T(8,128)S(1)}, u32[]{:S(2)}, u32[]{:S(2)}) %collective-permute-start.11) | collective-permute-done | bytes 32800 | tf_op jit(solution)/shard_map/ppermute | solution.py:489
  25.4 1.3 %collective-permute-done.13.b = f32[6,32,128]{2,1,0:T(8,128)S(1)} collective-permute-done((f32[6,32,128]{2,1,0:T(8,128)S(1)}, f32[6,32,128]{2,1,0:T(8,128)S(1)}, u32[]{:S(2)}, u32[]{:S(2)}) %collective-permute-start.13) | collective-permute-done | bytes 98336 | tf_op jit(solution)/shard_map/ppermute | solution.py:491
  26.7 1.7 %shard_map.94 = (f32[17,8,128]{2,1,0:T(8,128)S(1)}, f32[17,8,128]{2,1,0:T(8,128)S(1)}, f32[9,8,128]{2,1,0:T(8,128)S(1)}, f32[4,32,128]{2,1,0:T(8,128)S(1)}, f32[32,4,128]{2,1,0:T(4,128)}) custom-call(f32[86,8,128]{2,1,0:T(8,128)S(1)} %shard_map.86.places, bf16[768,768]{1,0:T(8,128)(2,1)S(1)} %get-tuple-element.49.high, ...), custom_call_target="tpu_custom_call" | custom-call | tf_op jit(solution)/shard_map/pallas_call | solution.py:416
  28.6 3.7 %all-to-all-start = ((f32[32,4,128]{2,1,0:T(4,128)}), f32[32,4,128]{2,1,0:T(4,128)S(1)}, u32[]{:S(2)}, u32[]{:S(2)}) async-start(f32[32,4,128]{2,1,0:T(4,128)} %get-tuple-element.82), calls=%async_computation | async-start | bytes 131072 | tf_op jit(solution)/shard_map/all_to_all | solution.py:501
  32.6 1.8 %collective-permute-start.16 = (f32[9,8,128]{2,1,0:T(8,128)S(1)}, f32[9,8,128]{2,1,0:T(8,128)S(1)}, u32[]{:S(2)}, u32[]{:S(2)}) collective-permute-start(f32[9,8,128]{2,1,0:T(8,128)S(1)} %get-tuple-element.79), channel_id=1, source_target_pairs={{0,2},{1,4},{2,0},{3,6},{4,1},{5,8},{6,3},{7,10},{8,5},{9,12},{10,... | collective-permute-start | bytes 110600 | tf_op jit(solution)/shard_map/ppermute | solution.py:459
  34.4 2.9 %collective-permute-done.16.from_p2 = f32[9,8,128]{2,1,0:T(8,128)S(1)} collective-permute-done((f32[9,8,128]{2,1,0:T(8,128)S(1)}, f32[9,8,128]{2,1,0:T(8,128)S(1)}, u32[]{:S(2)}, u32[]{:S(2)}) %collective-permute-start.16) | collective-permute-done | bytes 36896 | tf_op jit(solution)/shard_map/ppermute | solution.py:459
  37.4 1.4 %collective-permute-start.17 = (f32[9,8,128]{2,1,0:T(8,128)S(1)}, f32[9,8,128]{2,1,0:T(8,128)S(1)}, u32[]{:S(2)}, u32[]{:S(2)}) collective-permute-start(f32[9,8,128]{2,1,0:T(8,128)S(1)} %get-tuple-element.83), channel_id=1, source_target_pairs={{0,1},{1,0},{2,3},{3,2},{4,5},{5,4},{6,7},{7,6},{8,9},{9,8},{10,11... | collective-permute-start | bytes 110600 | tf_op jit(solution)/shard_map/ppermute | solution.py:505
  38.8 0.9 %all-to-all-done.sums = f32[32,4,128]{2,1,0:T(4,128)S(1)} async-done(((f32[32,4,128]{2,1,0:T(4,128)}), f32[32,4,128]{2,1,0:T(4,128)S(1)}, u32[]{:S(2)}, u32[]{:S(2)}) %all-to-all-start) | async-done | bytes 65568 | tf_op jit(solution)/shard_map/all_to_all | solution.py:501
  39.9 0.7 %shard_map.97 = (f32[32,256]{1,0:T(8,128)}, f32[32,256]{1,0:T(8,128)}) custom-call(f32[32,256]{1,0:T(8,128)S(1)} %bitcast.13, f32[32,256]{1,0:T(8,128)S(1)} %broadcast_multiply_fusion.z.start_own, f32[32,256]{1,0:T(8,128)S(1)} %get-tuple-element.62.image, f32[2,32,128]{2,1,0:T(8,128)S(1)} %get-tuple-element.63.own.scaled, ...), custom_call_target="tpu_custom_call" | custom-call | tf_op jit(solution)/shard_map/pallas_call | solution.py:416
  (46 shorter events, 3.4 us)
Async XLA Ops:
  0.6 1.5 %collective-permute-start = (f32[1,256]{1,0:T(1,128)}, f32[1,256]{1,0:T(1,128)S(1)}, u32[]{:S(2)}, u32[]{:S(2)}) collective-permute-start(f32[1,256]{1,0:T(1,128)} %precond.5), channel_id=1, source_target_pairs={{0,1},{1,0},{2,3},{3,2},{4,5},{5,4},{6,7},{7,6},{8,9},{9,8},{10,11... | collective-permute-start | bytes 3080 | tf_op jit(solution)/shard_map/ppermute | solution.py:463
  1.1 1.4 %collective-permute-start.1 = (f32[32,256]{1,0:T(8,128)}, f32[32,256]{1,0:T(8,128)S(1)}, u32[]{:S(2)}, u32[]{:S(2)}) collective-permute-start(f32[32,256]{1,0:T(8,128)} %bitcast.11), channel_id=1, source_target_pairs={{0,1},{1,0},{2,3},{3,2},{4,5},{5,4},{6,7},{7,6},{8,9},{9,8},{10,11... | collective-permute-start | bytes 98312 | tf_op jit(solution)/shard_map/ppermute | solution.py:464
  2.6 6.6 %collective-permute-start.2 = (f32[2,32,256]{2,1,0:T(8,128)S(1)}, f32[2,32,256]{2,1,0:T(8,128)S(1)}, u32[]{:S(2)}, u32[]{:S(2)}) collective-permute-start(f32[2,32,256]{2,1,0:T(8,128)S(1)} %pad_maximum_fusion.1.four), channel_id=1, source_target_pairs={{0,2},{1,0},{2,4},{3,1},{4,6},{5,3},{6,8},{7,5},{8,10},{9,7},{10,1... | collective-permute-start | bytes 196616 | tf_op jit(solution)/shard_map/ppermute | solution.py:466
  5.3 3.9 %collective-permute-start.3 = (f32[32,256]{1,0:T(8,128)S(1)}, f32[32,256]{1,0:T(8,128)S(1)}, u32[]{:S(2)}, u32[]{:S(2)}) collective-permute-start(f32[32,256]{1,0:T(8,128)S(1)} %broadcast_multiply_fusion.z.start_own), channel_id=1, source_target_pairs={{0,2},{1,4},{2,0},{3,6},{4,1},{5,8},{6,3},{7,10},{8,5},{9,12},{10,... | collective-permute-start | bytes 98312 | tf_op jit(solution)/shard_map/ppermute | solution.py:465
  6.8 2.4 %copy-start.3 = (s32[1,6]{1,0:T(1,128)S(1)}, s32[1,6]{1,0:T(1,128)}, u32[]{:S(2)}) copy-start(s32[1,6]{1,0:T(1,128)} %blocks.1) | copy-start | bytes 76
  9.2 1.3 %collective-permute-start.4 = (f32[2,32,256]{2,1,0:T(8,128)S(1)}, f32[2,32,256]{2,1,0:T(8,128)S(1)}, u32[]{:S(2)}, u32[]{:S(2)}) collective-permute-start(f32[2,32,256]{2,1,0:T(8,128)S(1)} %collective-permute-done.2.p1), channel_id=1, source_target_pairs={{0,1},{1,0},{2,3},{3,2},{4,5},{5,4},{6,7},{7,6},{8,9},{9,8},{10,11... | collective-permute-start | bytes 196616 | tf_op jit(solution)/shard_map/ppermute | solution.py:468
  9.3 2.1 %copy-start.4 = (s32[1,64]{1,0:T(1,128)S(1)}, s32[1,64]{1,0:T(1,128)}, u32[]{:S(2)}) copy-start(s32[1,64]{1,0:T(1,128)} %pad_rows.1) | copy-start | bytes 772
  9.4 6.7 %copy-start.2 = (f32[1,256]{1,0:T(1,128)S(1)}, f32[1,256]{1,0:T(1,128)}, u32[]{:S(2)}) copy-start(f32[1,256]{1,0:T(1,128)} %sink.5) | copy-start | bytes 3076
  9.4 8.5 %copy-start.1 = (f32[1,256]{1,0:T(1,128)S(1)}, f32[1,256]{1,0:T(1,128)}, u32[]{:S(2)}) copy-start(f32[1,256]{1,0:T(1,128)} %precond.5) | copy-start | bytes 3076
  11.2 11.3 %copy-start = (f32[1,32,256]{2,1,0:T(8,128)S(1)}, f32[1,32,256]{2,1,0:T(8,128)}, u32[]{:S(2)}) copy-start(f32[1,32,256]{2,1,0:T(8,128)} %param.7) | copy-start | bytes 98308
  11.2 2.0 %collective-permute-start.6 = (f32[4,32,128]{2,1,0:T(8,128)S(1)}, f32[4,32,128]{2,1,0:T(8,128)S(1)}, u32[]{:S(2)}, u32[]{:S(2)}) collective-permute-start(f32[4,32,128]{2,1,0:T(8,128)S(1)} %get-tuple-element.59), channel_id=1, source_target_pairs={{0,1},{1,0},{2,3},{3,2},{4,5},{5,4},{6,7},{7,6},{8,9},{9,8},{10,11... | collective-permute-start | bytes 196616 | tf_op jit(solution)/shard_map/ppermute | solution.py:460
  11.6 4.5 %collective-permute-start.5 = (f32[136,128]{1,0:T(8,128)S(1)}, f32[136,128]{1,0:T(8,128)S(1)}, u32[]{:S(2)}, u32[]{:S(2)}) collective-permute-start(f32[136,128]{1,0:T(8,128)S(1)} %get-tuple-element.55.mine), channel_id=1, source_target_pairs={{0,16},{16,0},{1,17},{17,1},{2,18},{18,2},{3,19},{19,3},{4,20},{20... | collective-permute-start | bytes 208904 | tf_op jit(solution)/shard_map/ppermute | solution.py:475
  13.2 4.7 %collective-permute-start.7 = (f32[4,32,128]{2,1,0:T(8,128)S(1)}, f32[4,32,128]{2,1,0:T(8,128)S(1)}, u32[]{:S(2)}, u32[]{:S(2)}) collective-permute-start(f32[4,32,128]{2,1,0:T(8,128)S(1)} %add.6), channel_id=1, source_target_pairs={{2,0},{0,1},{4,2},{1,3},{6,4},{3,5},{8,6},{5,7},{10,8},{7,9},{12,1... | collective-permute-start | bytes 196616 | tf_op jit(solution)/shard_map/ppermute | solution.py:478
  13.3 4.5 %collective-permute-start.8 = (f32[2,32,128]{2,1,0:T(8,128)S(1)}, f32[2,32,128]{2,1,0:T(8,128)S(1)}, u32[]{:S(2)}, u32[]{:S(2)}) collective-permute-start(f32[2,32,128]{2,1,0:T(8,128)S(1)} %get-tuple-element.60), channel_id=1, source_target_pairs={{0,2},{1,4},{2,0},{3,6},{4,1},{5,8},{6,3},{7,10},{8,5},{9,12},{10,... | collective-permute-start | bytes 98312 | tf_op jit(solution)/shard_map/ppermute | solution.py:459
  17.9 1.8 %collective-permute-start.9 = (f32[5,32,128]{2,1,0:T(8,128)S(1)}, f32[5,32,128]{2,1,0:T(8,128)S(1)}, u32[]{:S(2)}, u32[]{:S(2)}) collective-permute-start(f32[5,32,128]{2,1,0:T(8,128)S(1)} %shard_map.91.part), channel_id=1, source_target_pairs={{0,1},{1,0},{2,3},{3,2},{4,5},{5,4},{6,7},{7,6},{8,9},{9,8},{10,11... | collective-permute-start | bytes 245768 | tf_op jit(solution)/shard_map/ppermute | solution.py:480
  18.8 4.4 %collective-permute-start.12 = (f32[5,32,128]{2,1,0:T(8,128)S(1)}, f32[5,32,128]{2,1,0:T(8,128)S(1)}, u32[]{:S(2)}, u32[]{:S(2)}) collective-permute-start(f32[5,32,128]{2,1,0:T(8,128)S(1)} %shard_map.91.part), channel_id=1, source_target_pairs={{0,16},{16,0},{1,17},{17,1},{2,18},{18,2},{3,19},{19,3},{4,20},{20... | collective-permute-start | bytes 245768 | tf_op jit(solution)/shard_map/ppermute | solution.py:481
  19.7 5.6 %collective-permute-start.10 = (f32[4,32,128]{2,1,0:T(8,128)S(1)}, f32[4,32,128]{2,1,0:T(8,128)S(1)}, u32[]{:S(2)}, u32[]{:S(2)}) collective-permute-start(f32[4,32,128]{2,1,0:T(8,128)S(1)} %get-tuple-element.64), channel_id=1, source_target_pairs={{0,2},{1,0},{2,4},{3,1},{4,6},{5,3},{6,8},{7,5},{8,10},{9,7},{10,1... | collective-permute-start | bytes 196616 | tf_op jit(solution)/shard_map/ppermute | solution.py:488
  21.4 3.9 %collective-permute-start.11 = (f32[2,32,128]{2,1,0:T(8,128)S(1)}, f32[2,32,128]{2,1,0:T(8,128)S(1)}, u32[]{:S(2)}, u32[]{:S(2)}) collective-permute-start(f32[2,32,128]{2,1,0:T(8,128)S(1)} %get-tuple-element.63.own.scaled), channel_id=1, source_target_pairs={{0,2},{1,4},{2,0},{3,6},{4,1},{5,8},{6,3},{7,10},{8,5},{9,12},{10,... | collective-permute-start | bytes 98312 | tf_op jit(solution)/shard_map/ppermute | solution.py:489
  25.3 1.4 %collective-permute-start.13 = (f32[6,32,128]{2,1,0:T(8,128)S(1)}, f32[6,32,128]{2,1,0:T(8,128)S(1)}, u32[]{:S(2)}, u32[]{:S(2)}) collective-permute-start(f32[6,32,128]{2,1,0:T(8,128)S(1)} %pad_maximum_fusion), channel_id=1, source_target_pairs={{0,1},{1,0},{2,3},{3,2},{4,5},{5,4},{6,7},{7,6},{8,9},{9,8},{10,11... | collective-permute-start | bytes 294920 | tf_op jit(solution)/shard_map/ppermute | solution.py:491
  28.4 3.9 %collective-permute-start.14 = (f32[17,8,128]{2,1,0:T(8,128)S(1)}, f32[17,8,128]{2,1,0:T(8,128)S(1)}, u32[]{:S(2)}, u32[]{:S(2)}) collective-permute-start(f32[17,8,128]{2,1,0:T(8,128)S(1)} %get-tuple-element.78), channel_id=1, source_target_pairs={{0,1},{1,0},{2,3},{3,2},{4,5},{5,4},{6,7},{7,6},{8,9},{9,8},{10,11... | collective-permute-start | bytes 208904 | tf_op jit(solution)/shard_map/ppermute | solution.py:460
  28.6 11.1 %all-to-all-start = ((f32[32,4,128]{2,1,0:T(4,128)}), f32[32,4,128]{2,1,0:T(4,128)S(1)}, u32[]{:S(2)}, u32[]{:S(2)}) async-start(f32[32,4,128]{2,1,0:T(4,128)} %get-tuple-element.82), calls=%async_computation | async-start | bytes 131072 | tf_op jit(solution)/shard_map/all_to_all | solution.py:501
  32.3 5.0 %collective-permute-start.15 = (f32[17,8,128]{2,1,0:T(8,128)S(1)}, f32[17,8,128]{2,1,0:T(8,128)S(1)}, u32[]{:S(2)}, u32[]{:S(2)}) collective-permute-start(f32[17,8,128]{2,1,0:T(8,128)S(1)} %add.7), channel_id=1, source_target_pairs={{2,0},{0,1},{4,2},{1,3},{6,4},{3,5},{8,6},{5,7},{10,8},{7,9},{12,1... | collective-permute-start | bytes 208904 | tf_op jit(solution)/shard_map/ppermute | solution.py:500
  32.6 4.7 %collective-permute-start.16 = (f32[9,8,128]{2,1,0:T(8,128)S(1)}, f32[9,8,128]{2,1,0:T(8,128)S(1)}, u32[]{:S(2)}, u32[]{:S(2)}) collective-permute-start(f32[9,8,128]{2,1,0:T(8,128)S(1)} %get-tuple-element.79), channel_id=1, source_target_pairs={{0,2},{1,4},{2,0},{3,6},{4,1},{5,8},{6,3},{7,10},{8,5},{9,12},{10,... | collective-permute-start | bytes 110600 | tf_op jit(solution)/shard_map/ppermute | solution.py:459
  37.4 2.3 %collective-permute-start.17 = (f32[9,8,128]{2,1,0:T(8,128)S(1)}, f32[9,8,128]{2,1,0:T(8,128)S(1)}, u32[]{:S(2)}, u32[]{:S(2)}) collective-permute-start(f32[9,8,128]{2,1,0:T(8,128)S(1)} %get-tuple-element.83), channel_id=1, source_target_pairs={{0,1},{1,0},{2,3},{3,2},{4,5},{5,4},{6,7},{7,6},{8,9},{9,8},{10,11... | collective-permute-start | bytes 110600 | tf_op jit(solution)/shard_map/ppermute | solution.py:505
  (1 other events, 2.1 us)

commit v5 on v4

--- a/solution.py
+++ b/solution.py
@@ -31,6 +31,16 @@
             pairs.append((source, target * 2 + 1 - core))
         else:
             pairs.append((source, source ^ 2))
+    return pairs
+
+
+def beside(count):
+    pairs = []
+    for source in range(count):
+        chip, core = divmod(source, 2)
+        target = chip + 1 if chip % 2 else chip - 1
+        inside = 0 <= target < count // 2
+        pairs.append((source, target * 2 + core if inside else source ^ 1))
     return pairs
 
 
@@ -119,7 +129,10 @@
             places[i * spots + j] = (here == j).astype(F32)
     near = jnp.where(core == 0, above, below) >= 1
     far = jnp.where(core == 0, below, above) >= 2
-    for i, sender in enumerate((near, far)):
+    odd = lax.rem(chip, 2) == 1
+    cross = jnp.where(odd, above, below) >= 1
+    inner = odd == (core == 0)
+    for i, sender in enumerate((near, far, cross, inner)):
         places[touched * spots + i] = jnp.full(places.shape[1:], sender.astype(F32))
 
 
@@ -157,7 +170,7 @@
 
 def landed_blocks(places, product):
     cases, touched = product.shape[0], product.shape[1] // BR
-    spots = (places.shape[0] - 2) // touched
+    spots = (places.shape[0] - 4) // touched
     landed = []
     for j in range(spots):
         total = spot(places, j, cases) * product[:, :BR]
@@ -197,10 +210,12 @@
     product_out[...] = product
 
 
-def ties_kernel(z, mine, conds, ones, sink, local, jump_out):
+def ties_kernel(z, mine, conds, ones, sink, local, jump_out, ones_there):
     cases, count = z.shape[0], ones.shape[1]
     jump = mine[:cases, :count] - conds[:cases, :count]
     jump_out[...] = jump
+    pads = conds[cases + 8 : cases + 9, :count].astype(jnp.int32)
+    ones_there[...] = pad_matrix(pads, z.shape[1])
     local[...] = sink[...] * z[...] + times_ones(mean_of(mine, conds, cases, count) * jump, ones[...], True)
 
 
@@ -230,8 +245,11 @@
     return jnp.sum(total, axis=0, keepdims=True)
 
 
-def shares_kernel(rhs, z, image, precond, sink, picked, product, jump, mine, conds, top, known, guide):
+def shares_kernel(
+    rhs, z, image, scaled, ones, precond, sink, picked, product, jump, mine, conds, top, known, guide, at_pads
+):
     cases, count = jump.shape
+    at_pads[...] = times_ones(wide(scaled), ones[...], False)
     start = z[...]
     bulk = 0.25 * (4.0 / top[0:1, 0:1])
     mean = mean_of(mine, conds, cases, count)
@@ -268,9 +286,9 @@
 
 
 def second_kernel(
-    places, high, middle, low, p2, p1, own, a, b, there, conds, mine, ones, sink, top,
+    places, high, middle, low, p2, p1, own, a, b, there, conds, mine, ones, ones_there, at_pads, sink, top,
     start_picked, start_product, start_jump, start_own, known, guide,
-    back, to_p1, to_p2, kept, sums,
+    given, stays, to_p2, sums,
 ):
     touched = high.shape[0] // BR
     cases = own.shape[1]
@@ -278,11 +296,8 @@
     less = 4.0 / top[0:1, 0:1]
     picked = picked_blocks(places, held_blocks(p2, p1, own, a, b), touched)
     product = product_of((picked * less) * (1.0 / 1024.0), high, middle, low)
-    scales = jnp.concatenate([there[4, 0:1], there[4, 1:2]], axis=1)
-    values = scales * wide(there[0:2] + b[4:6])
-    pads = conds[cases + 8 : cases + 9, :count].astype(jnp.int32)
     here = wide(own)
-    jump = times_ones(here, ones[...], False) - times_ones(values, pad_matrix(pads, values.shape[1]), False)
+    jump = at_pads[...] - times_ones(wide(there[0:2]), ones_there[...], False)
     mean = mean_of(mine, conds, cases, count)
     local = sink[...] * here + times_ones(mean * jump, ones[...], True)
     local = (local * less) * (1.0 / 4096.0)
@@ -309,21 +324,18 @@
     landed = landed_blocks(places, product)
     for j in range(2):
         put_tiles(to_p2, j, landed[j])
-    for j in range(4):
-        put_tiles(back, j, landed[10 + j])
-        put_tiles(to_p1, j, landed[2 + j])
+        put_tiles(given, j, landed[4 + j])
+        put_tiles(given, 2 + j, landed[10 + j])
+        put_tiles(given, 4 + j, landed[8 + j])
+        put_tiles(stays, j, landed[2 + j])
+        put_tiles(stays, 2 + j, landed[12 + j])
+        put_tiles(stays, 4 + j, landed[6 + j] + local[:, j * BR : (j + 1) * BR])
     to_p2[to_p2.shape[0] - 1] = top[...]
-    to_p1[to_p1.shape[0] - 1] = top[...]
-    back[back.shape[0] - 1] = jnp.zeros_like(top)
-    kept[0] = landed[6] + local[:, :BR]
-    kept[1] = landed[7] + local[:, BR:]
-    kept[2] = landed[8]
-    kept[3] = landed[9]
 
 
 def part_kernel(places, kept, local, from_p1, from_p2, precond, top, part):
     cases = kept.shape[1]
-    near, far = [spot(places, places.shape[0] - 2 + i, cases)[None] for i in range(2)]
+    near, far = [spot(places, places.shape[0] - 4 + i, cases)[None] for i in range(2)]
     one = from_p1[...] * near
     mine = kept[0:2] + one[0:2] + from_p2[...] * far
     part[0] = mine[0] + local[:, :BR]
@@ -347,23 +359,17 @@
     top_out[...] = jnp.maximum(part[4, 8:16], there[4, 8:16])
 
 
-def last_part_kernel(places, kept, from_p1, from_p2, top, mine, other, top_out):
-    cases = kept.shape[1]
-    tiles = cases // 8
-    near, far = [places[places.shape[0] - 2 + i] for i in range(2)]
-    near_top = from_p1[from_p1.shape[0] - 1]
-    far_top = from_p2[from_p2.shape[0] - 1]
-    most = jnp.maximum(top[...], jnp.maximum(near * near_top, far * far_top))
-    here, one, two = top[...] / most, near * (near_top / most), far * (far_top / most)
-    for j in range(4):
-        block = kept[j].reshape(tiles, 8, BR) * here + from_p1[j * tiles : (j + 1) * tiles] * one
-        if j < 2:
-            block = block + from_p2[j * tiles : (j + 1) * tiles] * two
-            mine[j] = block.reshape(cases, BR)
-        else:
-            other[(j - 2) * tiles : (j - 1) * tiles] = block
-    other[other.shape[0] - 1] = most
-    top_out[...] = most
+def sort_kernel(places, given, stays, top, to_e, to_o, own):
+    pair = stays.shape[0] // 3
+    inner = places[places.shape[0] - 1] > 0.0
+    for i in range(pair):
+        near = stays[i] + given[pair + i]
+        away = stays[pair + i] + given[i]
+        to_e[i] = jnp.where(inner, near, away)
+        to_o[i] = jnp.where(inner, away, near)
+        own[i] = stays[2 * pair + i] + given[2 * pair + i]
+    to_e[pair] = top[...]
+    to_o[pair] = top[...]
 
 
 def steps_kernel(sums, steps):
@@ -393,17 +399,26 @@
         steps[i] = jnp.broadcast_to(as_column(row, 0, cases), steps.shape[1:])
 
 
-def end_kernel(rhs, z, image, scaled, mine, mine_top, there, steps, solution, residual):
+def end_kernel(rhs, z, image, scaled, places, own, from_e, from_o, from_p2, top, steps, solution, residual):
     cases = solution.shape[0]
     tiles = cases // 8
     alpha, grown, step = [wide([steps[i], steps[i]]) for i in range(3)]
     start = z[...]
     direction = grown * start - alpha * wide(scaled)
     solution[...] = alpha * start + step * direction
-    there_top = there[there.shape[0] - 1]
-    most = jnp.maximum(mine_top[...], there_top)
-    here, away = spot([mine_top[...] / most], 0, cases), spot([there_top / most], 0, cases)
-    blocks = [mine[j] * here + there[j * tiles : (j + 1) * tiles].reshape(cases, BR) * away for j in range(2)]
+    one = jnp.ones_like(top)
+    cross, far = places[places.shape[0] - 2], places[places.shape[0] - 3]
+    parts = [(own, top[...], one)] + [
+        (part, part[2 * tiles], valid) for part, valid in ((from_e, one), (from_o, cross), (from_p2, far))
+    ]
+    most = top[...]
+    for _, scale, valid in parts[1:]:
+        most = jnp.maximum(most, valid * scale)
+    total = 0.0
+    for part, scale, valid in parts:
+        factor = valid * (scale / most)
+        total = total + part[: 2 * tiles] * factor[None]
+    blocks = total.reshape(2, cases, BR)
     bulk = spot([most], 0, cases)
     second = ((alpha * wide(blocks)) * wide([bulk, bulk])) * 1024.0
     residual[...] = rhs[...] - alpha * image[...] - step * (grown * image[...] - second)
@@ -445,7 +460,7 @@
     ones, pads_sent = call(begin_kernel, [((owned, pads), HALF), ((4 * cases + 8, BR), F32)], z, pad_rows, pad_cond)
     chunks = touched
     spots = 2 * (2 * REACH + 1)
-    (places,) = call(places_kernel, [((touched * spots + 2, 8, BR), F32)], block_list)
+    (places,) = call(places_kernel, [((touched * spots + 4, 8, BR), F32)], block_list)
     high, middle, low, top = call(
         split_kernel,
         [((inner, inner), HALF)] * 3 + [tile],
@@ -466,6 +481,7 @@
     p1 = lax.ppermute(four, "sub", near)
     p1, p2, high, middle, low, top = barrier((p1, p2, high, middle, low, top))
     b = lax.ppermute(p1, "sub", swap)
+    b, ones, pads_sent = barrier((b, ones, pads_sent))
     split = (places, high, middle, low)
     back, to_p1, to_p2, kept, start_picked, start_product = call(
         first_kernel,
@@ -473,40 +489,48 @@
         *split, p2, p1, four, b,
     )
     conds = lax.ppermute(pads_sent, "board", across)
-    local, start_jump = call(ties_kernel, [full, ((cases, pads), F32)], z, pads_sent, conds, ones, sink)
+    local, start_jump, ones_there = call(
+        ties_kernel,
+        [full, ((cases, pads), F32), ((owned, pads), HALF)],
+        z, pads_sent, conds, ones, sink,
+    )
     to_p1, from_p2 = collect(back, to_p1, to_p2)
     from_p1 = lax.ppermute(to_p1, "sub", turned(near))
     (part,) = call(part_kernel, [((2 * blocks + 1, cases, BR), F32)], places, kept, local, from_p1, from_p2, precond, top)
     part_there = lax.ppermute(part, "sub", swap)
-    part_across = lax.ppermute(part, "board", across)
     image, four, own, top = call(turn_kernel, [full, both, pair, tile], part, part_there, precond)
-    known, guide = call(
+    known, guide, at_pads = call(
         shares_kernel,
-        [((2, BR), F32), ((2, cases, BR), F32)],
-        rhs[0], z, image, precond, sink, start_picked, start_product, start_jump, pads_sent, conds, top,
+        [((2, BR), F32), ((2, cases, BR), F32), ((cases, pads), F32)],
+        rhs[0], z, image, own, ones, precond, sink, start_picked, start_product, start_jump, pads_sent, conds, top,
     )
     p1 = lax.ppermute(four, "sub", near)
     p2 = lax.ppermute(own, "sub", far)
-    p1, p2, part_across, known, guide = barrier((p1, p2, part_across, known, guide))
-    b = lax.ppermute(jnp.concatenate([p1, part_across[blocks : 2 * blocks]]), "sub", swap)
+    there = lax.ppermute(four, "board", across)
+    p1, p2, known, guide, at_pads = barrier((p1, p2, known, guide, at_pads))
+    b = lax.ppermute(p1, "sub", swap)
     tiles = cases // 8
-    back, to_p1, to_p2, kept, sums = call(
+    pair_tiles = ((2 * tiles, 8, BR), F32)
+    sent = ((2 * tiles + 1, 8, BR), F32)
+    given, stays, to_p2, sums = call(
         second_kernel,
-        [((4 * tiles + 1, 8, BR), F32)] * 2 + [((2 * tiles + 1, 8, BR), F32), both, ((everyone, 4, BR), F32)],
-        *split, p2, p1, own, four[blocks:], b, part_across, conds, pads_sent, ones, sink, top,
+        [((6 * tiles, 8, BR), F32)] * 2 + [sent, ((everyone, 4, BR), F32)],
+        *split, p2, p1, own, four[blocks:], b, there, conds, pads_sent, ones, ones_there, at_pads, sink, top,
         start_picked, start_product, start_jump, z, known, guide,
     )
-    to_p1, from_p2 = collect(back, to_p1, to_p2)
-    from_p1 = lax.ppermute(to_p1, "sub", turned(near))
+    given = lax.ppermute(given, "sub", swap)
+    to_e, to_o, own_part = call(sort_kernel, [sent, sent, pair_tiles], places, given, stays, top)
+    to_e, to_o, to_p2 = barrier((to_e, to_o, to_p2))
+    from_o = lax.ppermute(to_o, "sub", beside(count))
+    from_e = lax.ppermute(to_e, "sub", [(i, i ^ 2) for i in range(count)])
+    from_p2 = lax.ppermute(to_p2, "sub", far)
     all_sums = lax.all_to_all(sums, ("board", "sub"), 0, 0)
-    mine, to_other, mine_top = call(
-        last_part_kernel, [pair, ((2 * tiles + 1, 8, BR), F32), tile], places, kept, from_p1, from_p2, top
-    )
-    there = lax.ppermute(to_other, "sub", swap)
-    all_sums, there = barrier((all_sums, there))
+    from_o, from_e, from_p2, all_sums = barrier((from_o, from_e, from_p2, all_sums))
     (steps,) = call(steps_kernel, [((3, cases, BR), F32)], all_sums)
     solution, residual = call(
-        end_kernel, [full, full], rhs[0], z, image, own, mine, mine_top, there, steps
+        end_kernel,
+        [full, full],
+        rhs[0], z, image, own, places, own_part, from_e, from_o, from_p2, top, steps,
     )
     return (solution[None], residual[None])
 

time: 40.8 us -> 40.7 us (level)
    all_to_all x1, waiting for transfers between devices: 0.89 us -> 4.08 us  [on_device(): all_sums = lax.all_to_all(sums, ('board', 'sub'), 0, 0)]
    ppermute x2 -> x1, waiting for transfers between devices: 4.58 us -> 1.62 us  [collect(): from_p2 = lax.ppermute(to_p2, 'sub', far)]
    ppermute x3 -> x5, starting transfers between devices: 2.37 us -> 4.43 us  [the longest x1 2.98 us: on_device(): from_e = lax.ppermute(to_e, 'sub', [(i, i ^ 2) for i in range(count)])]
    ppermute x2 -> x1, starting transfers between devices: 3.73 us -> 1.95 us  [collect(): from_p2 = lax.ppermute(to_p2, 'sub', far)]
    ppermute x1, waiting for transfers between devices: 0.05 us -> 0.92 us  [on_device(): part_there = lax.ppermute(part, 'sub', swap)]
    ppermute x1, waiting for transfers between devices: 2.11 us -> 1.42 us  [on_device(): p2 = lax.ppermute(own, 'sub', far)]
    ppermute x3 -> x5, waiting for transfers between devices: 1.69 us -> 1.48 us  [the longest x1 1.47 us: on_device(): there = lax.ppermute(four, 'board', across)]
    ppermute x1 -> x2, waiting for transfers between devices: 1.08 us -> 0.96 us  [on_device(): b = lax.ppermute(p1, 'sub', swap)]
  transfers between devices with their start and end apart: 19 -> 19, of which waited for: 12 -> 10; matrix products, arithmetic and copies ran while one was open for 2% -> 2% of each run, Pallas kernels for 7% -> 7%
where the time goes in v5:
time: 40.7 us; the launch traced here: 40.4 us
  starting transfers between devices  20.6 us (51%)
  waiting for transfers between devices  12.2 us (30%)
  Pallas kernels  6.02 us (15%)
  other arithmetic  0.8 us (2%)
  between operations  0.76 us (2%)
    pallas_call x12, Pallas kernels, call(): pl.pallas_call(kernel, in_specs=[space(far, i) for i in range(len(operand...  6.02 us
    ppermute x2, starting transfers between devices, on_device(): p1 = lax.ppermute(four, 'sub', near)  4.4 us
    all_to_all x1, waiting for transfers between devices, on_device(): all_sums = lax.all_to_all(sums, ('board', 'sub'), 0, 0)  4.08 us
    all_to_all x1, starting transfers between devices, on_device(): all_sums = lax.all_to_all(sums, ('board', 'sub'), 0, 0)  3.83 us
    ppermute x1, starting transfers between devices, on_device(): from_e = lax.ppermute(to_e, 'sub', [(i, i ^ 2) for i in range(count)])  2.98 us
    ppermute x1, starting transfers between devices, collect(): from_p2 = lax.ppermute(to_p2, 'sub', far)  1.95 us
    ppermute x1, waiting for transfers between devices, collect(): from_p2 = lax.ppermute(to_p2, 'sub', far)  1.62 us
    ppermute x1, starting transfers between devices, on_device(): p2 = lax.ppermute(z, 'sub', far)  1.55 us
  transfers between devices with their start and end apart: 19, of which 10 were waited for; matrix products, arithmetic and copies ran while one was open for 2% of the time, Pallas kernels for 7%

profile of v5, /device:TPU:0, one launch (start us, length us, event | category | flops | bytes accessed | tf_op | source)
XLA Modules:
  0.0 40.4 jit_solution(9532357998339458501)
XLA Ops:
  0.6 0.5 %collective-permute-start = (f32[1,256]{1,0:T(1,128)}, f32[1,256]{1,0:T(1,128)S(1)}, u32[]{:S(2)}, u32[]{:S(2)}) collective-permute-start(f32[1,256]{1,0:T(1,128)} %precond.5), channel_id=1, source_target_pairs={{0,1},{1,0},{2,3},{3,2},{4,5},{5,4},{6,7},{7,6},{8,9},{9,8},{10,11... | collective-permute-start | bytes 3080 | tf_op jit(solution)/shard_map/ppermute | solution.py:478
  1.2 0.8 %broadcast_multiply_fusion.z.start_own = f32[32,256]{1,0:T(8,128)S(1)} fusion(f32[256]{0:T(256)} %bitcast.14, f32[1,32,256]{2,1,0:T(8,128)} %param.7), kind=kLoop, calls=%fused_computation.2 | loop fusion | flops 8192 | bytes 66560 | tf_op jit(solution)/shard_map/mul | solution.py:459
  2.2 0.4 collective-permute-done.1
  2.6 2.7 %collective-permute-start.2 = (f32[2,32,256]{2,1,0:T(8,128)S(1)}, f32[2,32,256]{2,1,0:T(8,128)S(1)}, u32[]{:S(2)}, u32[]{:S(2)}) collective-permute-start(f32[2,32,256]{2,1,0:T(8,128)S(1)} %pad_maximum_fusion.four), channel_id=1, source_target_pairs={{0,2},{1,0},{2,4},{3,1},{4,6},{5,3},{6,8},{7,5},{8,10},{9,7},{10,1... | collective-permute-start | bytes 196616 | tf_op jit(solution)/shard_map/ppermute | solution.py:481
  5.3 1.5 %collective-permute-start.3 = (f32[32,256]{1,0:T(8,128)S(1)}, f32[32,256]{1,0:T(8,128)S(1)}, u32[]{:S(2)}, u32[]{:S(2)}) collective-permute-start(f32[32,256]{1,0:T(8,128)S(1)} %broadcast_multiply_fusion.z.start_own), channel_id=1, source_target_pairs={{0,2},{1,4},{2,0},{3,6},{4,1},{5,8},{6,3},{7,10},{8,5},{9,12},{10,... | collective-permute-start | bytes 98312 | tf_op jit(solution)/shard_map/ppermute | solution.py:480
  6.8 2.0 %shard_map.87 = (bf16[768,768]{1,0:T(8,128)(2,1)S(1)}, bf16[768,768]{1,0:T(8,128)(2,1)S(1)}, bf16[768,768]{1,0:T(8,128)(2,1)S(1)}, f32[8,128]{1,0:T(8,128)S(1)}) custom-call(f32[768,768]{1,0:T(8,128)} %bitcast.15), custom_call_target="tpu_custom_call" | custom-call | tf_op jit(solution)/shard_map/pallas_call | solution.py:431
  9.5 1.0 %collective-permute-done.4.b = f32[2,32,256]{2,1,0:T(8,128)S(1)} collective-permute-done((f32[2,32,256]{2,1,0:T(8,128)S(1)}, f32[2,32,256]{2,1,0:T(8,128)S(1)}, u32[]{:S(2)}, u32[]{:S(2)}) %collective-permute-start.4) | collective-permute-done | bytes 65568 | tf_op jit(solution)/shard_map/ppermute | solution.py:483
  10.5 0.7 %shard_map.89 = (f32[4,32,128]{2,1,0:T(8,128)S(1)}, f32[4,32,128]{2,1,0:T(8,128)S(1)}, f32[2,32,128]{2,1,0:T(8,128)S(1)}, f32[4,32,128]{2,1,0:T(8,128)S(1)}, f32...) custom-call(f32[88,8,128]{2,1,0:T(8,128)S(1)} %shard_map.86.places, bf16[768,768]{1,0:T(8,128)(2,1)S(1)} %get-tuple-element.58.high, ...), custom_call_target="tpu_custom_call" | custom-call | tf_op jit(solution)/shard_map/pallas_call | solution.py:431
  11.4 1.5 %collective-permute-start.5 = (f32[136,128]{1,0:T(8,128)S(1)}, f32[136,128]{1,0:T(8,128)S(1)}, u32[]{:S(2)}, u32[]{:S(2)}) collective-permute-start(f32[136,128]{1,0:T(8,128)S(1)} %get-tuple-element.67.mine), channel_id=1, source_target_pairs={{0,16},{16,0},{1,17},{17,1},{2,18},{18,2},{3,19},{19,3},{4,20},{20... | collective-permute-start | bytes 208904 | tf_op jit(solution)/shard_map/ppermute | solution.py:491
  13.1 2.0 %collective-permute-start.8 = (f32[2,32,128]{2,1,0:T(8,128)S(1)}, f32[2,32,128]{2,1,0:T(8,128)S(1)}, u32[]{:S(2)}, u32[]{:S(2)}) collective-permute-start(f32[2,32,128]{2,1,0:T(8,128)S(1)} %get-tuple-element.72), channel_id=1, source_target_pairs={{0,2},{1,4},{2,0},{3,6},{4,1},{5,8},{6,3},{7,10},{8,5},{9,12},{10,... | collective-permute-start | bytes 98312 | tf_op jit(solution)/shard_map/ppermute | solution.py:474
  15.1 0.8 %collective-permute-done.5.conds = f32[136,128]{1,0:T(8,128)S(1)} collective-permute-done((f32[136,128]{1,0:T(8,128)S(1)}, f32[136,128]{1,0:T(8,128)S(1)}, u32[]{:S(2)}, u32[]{:S(2)}) %collective-permute-start.5) | collective-permute-done | bytes 69664 | tf_op jit(solution)/shard_map/ppermute | solution.py:491
  16.0 1.6 %collective-permute-done.8.from_p2 = f32[2,32,128]{2,1,0:T(8,128)S(1)} collective-permute-done((f32[2,32,128]{2,1,0:T(8,128)S(1)}, f32[2,32,128]{2,1,0:T(8,128)S(1)}, u32[]{:S(2)}, u32[]{:S(2)}) %collective-permute-start.8) | collective-permute-done | bytes 32800 | tf_op jit(solution)/shard_map/ppermute | solution.py:474
  17.7 0.9 %collective-permute-start.9 = (f32[5,32,128]{2,1,0:T(8,128)S(1)}, f32[5,32,128]{2,1,0:T(8,128)S(1)}, u32[]{:S(2)}, u32[]{:S(2)}) collective-permute-start(f32[5,32,128]{2,1,0:T(8,128)S(1)} %shard_map.91.part), channel_id=1, source_target_pairs={{0,1},{1,0},{2,3},{3,2},{4,5},{5,4},{6,7},{7,6},{8,9},{9,8},{10,11... | collective-permute-start | bytes 245768 | tf_op jit(solution)/shard_map/ppermute | solution.py:500
  18.5 0.9 %collective-permute-done.9.there = f32[5,32,128]{2,1,0:T(8,128)S(1)} collective-permute-done((f32[5,32,128]{2,1,0:T(8,128)S(1)}, f32[5,32,128]{2,1,0:T(8,128)S(1)}, u32[]{:S(2)}, u32[]{:S(2)}) %collective-permute-start.9) | collective-permute-done | bytes 81952 | tf_op jit(solution)/shard_map/ppermute | solution.py:500
  19.5 1.7 %collective-permute-start.10 = (f32[4,32,128]{2,1,0:T(8,128)S(1)}, f32[4,32,128]{2,1,0:T(8,128)S(1)}, u32[]{:S(2)}, u32[]{:S(2)}) collective-permute-start(f32[4,32,128]{2,1,0:T(8,128)S(1)} %get-tuple-element.76), channel_id=1, source_target_pairs={{0,2},{1,0},{2,4},{3,1},{4,6},{5,3},{6,8},{7,5},{8,10},{9,7},{10,1... | collective-permute-start | bytes 196616 | tf_op jit(solution)/shard_map/ppermute | solution.py:507
  21.2 1.1 %collective-permute-start.11 = (f32[2,32,128]{2,1,0:T(8,128)S(1)}, f32[2,32,128]{2,1,0:T(8,128)S(1)}, u32[]{:S(2)}, u32[]{:S(2)}) collective-permute-start(f32[2,32,128]{2,1,0:T(8,128)S(1)} %get-tuple-element.75.scaled.own), channel_id=1, source_target_pairs={{0,2},{1,4},{2,0},{3,6},{4,1},{5,8},{6,3},{7,10},{8,5},{9,12},{10,... | collective-permute-start | bytes 98312 | tf_op jit(solution)/shard_map/ppermute | solution.py:508
  22.3 1.1 %collective-permute-start.13 = (f32[4,32,128]{2,1,0:T(8,128)S(1)}, f32[4,32,128]{2,1,0:T(8,128)S(1)}, u32[]{:S(2)}, u32[]{:S(2)}) collective-permute-start(f32[4,32,128]{2,1,0:T(8,128)S(1)} %get-tuple-element.76), channel_id=1, source_target_pairs={{0,16},{16,0},{1,17},{17,1},{2,18},{18,2},{3,19},{19,3},{4,20},{20... | collective-permute-start | bytes 196616 | tf_op jit(solution)/shard_map/ppermute | solution.py:509
  23.7 1.4 %collective-permute-done.11.p2 = f32[2,32,128]{2,1,0:T(8,128)S(1)} collective-permute-done((f32[2,32,128]{2,1,0:T(8,128)S(1)}, f32[2,32,128]{2,1,0:T(8,128)S(1)}, u32[]{:S(2)}, u32[]{:S(2)}) %collective-permute-start.11) | collective-permute-done | bytes 32800 | tf_op jit(solution)/shard_map/ppermute | solution.py:508
  25.1 1.5 %collective-permute-done.13.there = f32[4,32,128]{2,1,0:T(8,128)S(1)} collective-permute-done((f32[4,32,128]{2,1,0:T(8,128)S(1)}, f32[4,32,128]{2,1,0:T(8,128)S(1)}, u32[]{:S(2)}, u32[]{:S(2)}) %collective-permute-start.13) | collective-permute-done | bytes 65568 | tf_op jit(solution)/shard_map/ppermute | solution.py:509
  26.6 1.7 %shard_map.94 = (f32[24,8,128]{2,1,0:T(8,128)S(1)}, f32[24,8,128]{2,1,0:T(8,128)S(1)}, f32[9,8,128]{2,1,0:T(8,128)S(1)}, f32[32,4,128]{2,1,0:T(4,128)}) custom-call(f32[88,8,128]{2,1,0:T(8,128)S(1)} %shard_map.86.places, bf16[768,768]{1,0:T(8,128)(2,1)S(1)} %get-tuple-element.58.high, bf16[768,768]{1,0:T(8,128)(2,1)S(1)} %get-tuple-element.59.middle, ...), custom_call_target="tpu_custom_call" | custom-call | tf_op jit(solution)/shard_map/pallas_call | solution.py:431
  28.3 3.8 %all-to-all-start = ((f32[32,4,128]{2,1,0:T(4,128)}), f32[32,4,128]{2,1,0:T(4,128)S(1)}, u32[]{:S(2)}, u32[]{:S(2)}) async-start(f32[32,4,128]{2,1,0:T(4,128)} %get-tuple-element.99), calls=%async_computation | async-start | bytes 131072 | tf_op jit(solution)/shard_map/all_to_all | solution.py:527
  32.5 3.0 %collective-permute-start.16 = (f32[9,8,128]{2,1,0:T(8,128)S(1)}, f32[9,8,128]{2,1,0:T(8,128)S(1)}, u32[]{:S(2)}, u32[]{:S(2)}) collective-permute-start(f32[9,8,128]{2,1,0:T(8,128)S(1)} %get-tuple-element.97), channel_id=1, source_target_pairs={{0,2},{1,3},{2,0},{3,1},{4,6},{5,7},{6,4},{7,5},{8,10},{9,11},{10,... | collective-permute-start | bytes 110600 | tf_op jit(solution)/shard_map/ppermute | solution.py:525
  35.5 4.1 %all-to-all-done.sums = f32[32,4,128]{2,1,0:T(4,128)S(1)} async-done(((f32[32,4,128]{2,1,0:T(4,128)}), f32[32,4,128]{2,1,0:T(4,128)S(1)}, u32[]{:S(2)}, u32[]{:S(2)}) %all-to-all-start) | async-done | bytes 65568 | tf_op jit(solution)/shard_map/all_to_all | solution.py:527
  39.8 0.7 %shard_map.97 = (f32[32,256]{1,0:T(8,128)}, f32[32,256]{1,0:T(8,128)}) custom-call(f32[32,256]{1,0:T(8,128)S(1)} %bitcast.13, f32[32,256]{1,0:T(8,128)S(1)} %broadcast_multiply_fusion.z.start_own, f32[32,256]{1,0:T(8,128)S(1)} %get-tuple-element.74.image, f32[2,32,128]{2,1,0:T(8,128)S(1)} %get-tuple-element.75.scaled.own, ...), custom_call_target="tpu_custom_call" | custom-call | tf_op jit(solution)/shard_map/pallas_call | solution.py:431
  (43 shorter events, 2.3 us)
Async XLA Ops:
  0.6 1.5 %collective-permute-start = (f32[1,256]{1,0:T(1,128)}, f32[1,256]{1,0:T(1,128)S(1)}, u32[]{:S(2)}, u32[]{:S(2)}) collective-permute-start(f32[1,256]{1,0:T(1,128)} %precond.5), channel_id=1, source_target_pairs={{0,1},{1,0},{2,3},{3,2},{4,5},{5,4},{6,7},{7,6},{8,9},{9,8},{10,11... | collective-permute-start | bytes 3080 | tf_op jit(solution)/shard_map/ppermute | solution.py:478
  1.1 1.4 %collective-permute-start.1 = (f32[32,256]{1,0:T(8,128)}, f32[32,256]{1,0:T(8,128)S(1)}, u32[]{:S(2)}, u32[]{:S(2)}) collective-permute-start(f32[32,256]{1,0:T(8,128)} %bitcast.11), channel_id=1, source_target_pairs={{0,1},{1,0},{2,3},{3,2},{4,5},{5,4},{6,7},{7,6},{8,9},{9,8},{10,11... | collective-permute-start | bytes 98312 | tf_op jit(solution)/shard_map/ppermute | solution.py:479
  2.6 6.6 %collective-permute-start.2 = (f32[2,32,256]{2,1,0:T(8,128)S(1)}, f32[2,32,256]{2,1,0:T(8,128)S(1)}, u32[]{:S(2)}, u32[]{:S(2)}) collective-permute-start(f32[2,32,256]{2,1,0:T(8,128)S(1)} %pad_maximum_fusion.four), channel_id=1, source_target_pairs={{0,2},{1,0},{2,4},{3,1},{4,6},{5,3},{6,8},{7,5},{8,10},{9,7},{10,1... | collective-permute-start | bytes 196616 | tf_op jit(solution)/shard_map/ppermute | solution.py:481
  5.3 3.9 %collective-permute-start.3 = (f32[32,256]{1,0:T(8,128)S(1)}, f32[32,256]{1,0:T(8,128)S(1)}, u32[]{:S(2)}, u32[]{:S(2)}) collective-permute-start(f32[32,256]{1,0:T(8,128)S(1)} %broadcast_multiply_fusion.z.start_own), channel_id=1, source_target_pairs={{0,2},{1,4},{2,0},{3,6},{4,1},{5,8},{6,3},{7,10},{8,5},{9,12},{10,... | collective-permute-start | bytes 98312 | tf_op jit(solution)/shard_map/ppermute | solution.py:480
  6.8 2.5 %copy-start.4 = (s32[1,64]{1,0:T(1,128)S(1)}, s32[1,64]{1,0:T(1,128)}, u32[]{:S(2)}) copy-start(s32[1,64]{1,0:T(1,128)} %pad_rows.1) | copy-start | bytes 772
  6.8 2.5 %copy-start.5 = (f32[1,64]{1,0:T(1,128)S(1)}, f32[1,64]{1,0:T(1,128)}, u32[]{:S(2)}) copy-start(f32[1,64]{1,0:T(1,128)} %pad_cond.1) | copy-start | bytes 772
  9.2 1.3 %collective-permute-start.4 = (f32[2,32,256]{2,1,0:T(8,128)S(1)}, f32[2,32,256]{2,1,0:T(8,128)S(1)}, u32[]{:S(2)}, u32[]{:S(2)}) collective-permute-start(f32[2,32,256]{2,1,0:T(8,128)S(1)} %collective-permute-done.2.p1), channel_id=1, source_target_pairs={{0,1},{1,0},{2,3},{3,2},{4,5},{5,4},{6,7},{7,6},{8,9},{9,8},{10,11... | collective-permute-start | bytes 196616 | tf_op jit(solution)/shard_map/ppermute | solution.py:483
  10.5 5.4 %copy-start.2 = (f32[1,256]{1,0:T(1,128)S(1)}, f32[1,256]{1,0:T(1,128)}, u32[]{:S(2)}) copy-start(f32[1,256]{1,0:T(1,128)} %sink.5) | copy-start | bytes 3076
  10.5 7.2 %copy-start.1 = (f32[1,256]{1,0:T(1,128)S(1)}, f32[1,256]{1,0:T(1,128)}, u32[]{:S(2)}) copy-start(f32[1,256]{1,0:T(1,128)} %precond.5) | copy-start | bytes 3076
  11.2 12.2 %copy-start = (f32[1,32,256]{2,1,0:T(8,128)S(1)}, f32[1,32,256]{2,1,0:T(8,128)}, u32[]{:S(2)}) copy-start(f32[1,32,256]{2,1,0:T(8,128)} %param.7) | copy-start | bytes 98308
  11.2 1.7 %collective-permute-start.6 = (f32[4,32,128]{2,1,0:T(8,128)S(1)}, f32[4,32,128]{2,1,0:T(8,128)S(1)}, u32[]{:S(2)}, u32[]{:S(2)}) collective-permute-start(f32[4,32,128]{2,1,0:T(8,128)S(1)} %get-tuple-element.71), channel_id=1, source_target_pairs={{0,1},{1,0},{2,3},{3,2},{4,5},{5,4},{6,7},{7,6},{8,9},{9,8},{10,11... | collective-permute-start | bytes 196616 | tf_op jit(solution)/shard_map/ppermute | solution.py:475
  11.4 4.4 %collective-permute-start.5 = (f32[136,128]{1,0:T(8,128)S(1)}, f32[136,128]{1,0:T(8,128)S(1)}, u32[]{:S(2)}, u32[]{:S(2)}) collective-permute-start(f32[136,128]{1,0:T(8,128)S(1)} %get-tuple-element.67.mine), channel_id=1, source_target_pairs={{0,16},{16,0},{1,17},{17,1},{2,18},{18,2},{3,19},{19,3},{4,20},{20... | collective-permute-start | bytes 208904 | tf_op jit(solution)/shard_map/ppermute | solution.py:491
  13.0 4.7 %collective-permute-start.7 = (f32[4,32,128]{2,1,0:T(8,128)S(1)}, f32[4,32,128]{2,1,0:T(8,128)S(1)}, u32[]{:S(2)}, u32[]{:S(2)}) collective-permute-start(f32[4,32,128]{2,1,0:T(8,128)S(1)} %add.3), channel_id=1, source_target_pairs={{2,0},{0,1},{4,2},{1,3},{6,4},{3,5},{8,6},{5,7},{10,8},{7,9},{12,1... | collective-permute-start | bytes 196616 | tf_op jit(solution)/shard_map/ppermute | solution.py:498
  13.1 4.5 %collective-permute-start.8 = (f32[2,32,128]{2,1,0:T(8,128)S(1)}, f32[2,32,128]{2,1,0:T(8,128)S(1)}, u32[]{:S(2)}, u32[]{:S(2)}) collective-permute-start(f32[2,32,128]{2,1,0:T(8,128)S(1)} %get-tuple-element.72), channel_id=1, source_target_pairs={{0,2},{1,4},{2,0},{3,6},{4,1},{5,8},{6,3},{7,10},{8,5},{9,12},{10,... | collective-permute-start | bytes 98312 | tf_op jit(solution)/shard_map/ppermute | solution.py:474
  17.7 1.8 %collective-permute-start.9 = (f32[5,32,128]{2,1,0:T(8,128)S(1)}, f32[5,32,128]{2,1,0:T(8,128)S(1)}, u32[]{:S(2)}, u32[]{:S(2)}) collective-permute-start(f32[5,32,128]{2,1,0:T(8,128)S(1)} %shard_map.91.part), channel_id=1, source_target_pairs={{0,1},{1,0},{2,3},{3,2},{4,5},{5,4},{6,7},{7,6},{8,9},{9,8},{10,11... | collective-permute-start | bytes 245768 | tf_op jit(solution)/shard_map/ppermute | solution.py:500
  19.5 5.6 %collective-permute-start.10 = (f32[4,32,128]{2,1,0:T(8,128)S(1)}, f32[4,32,128]{2,1,0:T(8,128)S(1)}, u32[]{:S(2)}, u32[]{:S(2)}) collective-permute-start(f32[4,32,128]{2,1,0:T(8,128)S(1)} %get-tuple-element.76), channel_id=1, source_target_pairs={{0,2},{1,0},{2,4},{3,1},{4,6},{5,3},{6,8},{7,5},{8,10},{9,7},{10,1... | collective-permute-start | bytes 196616 | tf_op jit(solution)/shard_map/ppermute | solution.py:507
  21.2 3.9 %collective-permute-start.11 = (f32[2,32,128]{2,1,0:T(8,128)S(1)}, f32[2,32,128]{2,1,0:T(8,128)S(1)}, u32[]{:S(2)}, u32[]{:S(2)}) collective-permute-start(f32[2,32,128]{2,1,0:T(8,128)S(1)} %get-tuple-element.75.scaled.own), channel_id=1, source_target_pairs={{0,2},{1,4},{2,0},{3,6},{4,1},{5,8},{6,3},{7,10},{8,5},{9,12},{10,... | collective-permute-start | bytes 98312 | tf_op jit(solution)/shard_map/ppermute | solution.py:508
  22.3 4.3 %collective-permute-start.13 = (f32[4,32,128]{2,1,0:T(8,128)S(1)}, f32[4,32,128]{2,1,0:T(8,128)S(1)}, u32[]{:S(2)}, u32[]{:S(2)}) collective-permute-start(f32[4,32,128]{2,1,0:T(8,128)S(1)} %get-tuple-element.76), channel_id=1, source_target_pairs={{0,16},{16,0},{1,17},{17,1},{2,18},{18,2},{3,19},{19,3},{4,20},{20... | collective-permute-start | bytes 196616 | tf_op jit(solution)/shard_map/ppermute | solution.py:509
  25.1 1.5 %collective-permute-start.12 = (f32[4,32,128]{2,1,0:T(8,128)S(1)}, f32[4,32,128]{2,1,0:T(8,128)S(1)}, u32[]{:S(2)}, u32[]{:S(2)}) collective-permute-start(f32[4,32,128]{2,1,0:T(8,128)S(1)} %collective-permute-done.10.p1), channel_id=1, source_target_pairs={{0,1},{1,0},{2,3},{3,2},{4,5},{5,4},{6,7},{7,6},{8,9},{9,8},{10,11... | collective-permute-start | bytes 196616 | tf_op jit(solution)/shard_map/ppermute | solution.py:511
  28.3 3.8 %collective-permute-start.14 = (f32[24,8,128]{2,1,0:T(8,128)S(1)}, f32[24,8,128]{2,1,0:T(8,128)S(1)}, u32[]{:S(2)}, u32[]{:S(2)}) collective-permute-start(f32[24,8,128]{2,1,0:T(8,128)S(1)} %get-tuple-element.90), channel_id=1, source_target_pairs={{0,1},{1,0},{2,3},{3,2},{4,5},{5,4},{6,7},{7,6},{8,9},{9,8},{10,11... | collective-permute-start | bytes 294920 | tf_op jit(solution)/shard_map/ppermute | solution.py:521
  28.3 11.3 %all-to-all-start = ((f32[32,4,128]{2,1,0:T(4,128)}), f32[32,4,128]{2,1,0:T(4,128)S(1)}, u32[]{:S(2)}, u32[]{:S(2)}) async-start(f32[32,4,128]{2,1,0:T(4,128)} %get-tuple-element.99), calls=%async_computation | async-start | bytes 131072 | tf_op jit(solution)/shard_map/all_to_all | solution.py:527
  32.1 7.4 %collective-permute-start.15 = (f32[9,8,128]{2,1,0:T(8,128)S(1)}, f32[9,8,128]{2,1,0:T(8,128)S(1)}, u32[]{:S(2)}, u32[]{:S(2)}) collective-permute-start(f32[9,8,128]{2,1,0:T(8,128)S(1)} %get-tuple-element.96), channel_id=1, source_target_pairs={{0,1},{1,0},{2,4},{3,5},{4,2},{5,3},{6,8},{7,9},{8,6},{9,7},{10,12... | collective-permute-start | bytes 110600 | tf_op jit(solution)/shard_map/ppermute | solution.py:524
  32.5 7.1 %collective-permute-start.16 = (f32[9,8,128]{2,1,0:T(8,128)S(1)}, f32[9,8,128]{2,1,0:T(8,128)S(1)}, u32[]{:S(2)}, u32[]{:S(2)}) collective-permute-start(f32[9,8,128]{2,1,0:T(8,128)S(1)} %get-tuple-element.97), channel_id=1, source_target_pairs={{0,2},{1,3},{2,0},{3,1},{4,6},{5,7},{6,4},{7,5},{8,10},{9,11},{10,... | collective-permute-start | bytes 110600 | tf_op jit(solution)/shard_map/ppermute | solution.py:525
  35.4 4.1 %collective-permute-start.17 = (f32[9,8,128]{2,1,0:T(8,128)S(1)}, f32[9,8,128]{2,1,0:T(8,128)S(1)}, u32[]{:S(2)}, u32[]{:S(2)}) collective-permute-start(f32[9,8,128]{2,1,0:T(8,128)S(1)} %get-tuple-element.98), channel_id=1, source_target_pairs={{0,2},{1,4},{2,0},{3,6},{4,1},{5,8},{6,3},{7,10},{8,5},{9,12},{10,... | collective-permute-start | bytes 110600 | tf_op jit(solution)/shard_map/ppermute | solution.py:526
  (1 other events, 2.4 us)

commit v6 on v5

--- a/solution.py
+++ b/solution.py
@@ -265,7 +265,7 @@
     curve = across_lanes(folded(start * image[...]))
     reach = jnp.max(jnp.abs(image[...]), axis=1, keepdims=True)
     still = reach <= 0.0
-    scale = size / jnp.where(still, 1.0, reach)
+    scale = jnp.clip(size / jnp.where(still, 1.0, reach), 1e-34, 1e30)
     guess = jnp.where(curve > 0.0, norm / jnp.where(curve > 0.0, curve, 1.0), 0.0)
     guess = jnp.where(still, 1.0, jnp.clip(guess, scale * (1.0 / 1024.0), scale * 8.0))
     moved = guess * image[...]

time: 40.7 us -> 40.7 us (level)
  no operation moved by 1% of the time
where the time goes in v6:
time: 40.7 us; the launch traced here: 40.4 us
  starting transfers between devices  20.6 us (51%)
  waiting for transfers between devices  12.2 us (30%)
  Pallas kernels  6.02 us (15%)
  other arithmetic  0.8 us (2%)
  between operations  0.76 us (2%)
    pallas_call x12, Pallas kernels, call(): pl.pallas_call(kernel, in_specs=[space(far, i) for i in range(len(operand...  6.02 us
    ppermute x2, starting transfers between devices, on_device(): p1 = lax.ppermute(four, 'sub', near)  4.4 us
    all_to_all x1, waiting for transfers between devices, on_device(): all_sums = lax.all_to_all(sums, ('board', 'sub'), 0, 0)  4.08 us
    all_to_all x1, starting transfers between devices, on_device(): all_sums = lax.all_to_all(sums, ('board', 'sub'), 0, 0)  3.83 us
    ppermute x1, starting transfers between devices, on_device(): from_e = lax.ppermute(to_e, 'sub', [(i, i ^ 2) for i in range(count)])  2.98 us
    ppermute x1, starting transfers between devices, collect(): from_p2 = lax.ppermute(to_p2, 'sub', far)  1.95 us
    ppermute x1, waiting for transfers between devices, collect(): from_p2 = lax.ppermute(to_p2, 'sub', far)  1.62 us
    ppermute x1, starting transfers between devices, on_device(): p2 = lax.ppermute(z, 'sub', far)  1.55 us
  transfers between devices with their start and end apart: 19, of which 10 were waited for; matrix products, arithmetic and copies ran while one was open for 2% of the time, Pallas kernels for 7%

profile of v6, /device:TPU:0, one launch (start us, length us, event | category | flops | bytes accessed | tf_op | source)
XLA Modules:
  0.0 40.4 jit_solution(3271036393818564916)
XLA Ops:
  0.6 0.5 %collective-permute-start = (f32[1,256]{1,0:T(1,128)}, f32[1,256]{1,0:T(1,128)S(1)}, u32[]{:S(2)}, u32[]{:S(2)}) collective-permute-start(f32[1,256]{1,0:T(1,128)} %precond.5), channel_id=1, source_target_pairs={{0,1},{1,0},{2,3},{3,2},{4,5},{5,4},{6,7},{7,6},{8,9},{9,8},{10,11... | collective-permute-start | bytes 3080 | tf_op jit(solution)/shard_map/ppermute | solution.py:478
  1.2 0.8 %broadcast_multiply_fusion.z.start_own = f32[32,256]{1,0:T(8,128)S(1)} fusion(f32[256]{0:T(256)} %bitcast.14, f32[1,32,256]{2,1,0:T(8,128)} %param.7), kind=kLoop, calls=%fused_computation.2 | loop fusion | flops 8192 | bytes 66560 | tf_op jit(solution)/shard_map/mul | solution.py:459
  2.2 0.4 collective-permute-done.1
  2.6 2.7 %collective-permute-start.2 = (f32[2,32,256]{2,1,0:T(8,128)S(1)}, f32[2,32,256]{2,1,0:T(8,128)S(1)}, u32[]{:S(2)}, u32[]{:S(2)}) collective-permute-start(f32[2,32,256]{2,1,0:T(8,128)S(1)} %pad_maximum_fusion.four), channel_id=1, source_target_pairs={{0,2},{1,0},{2,4},{3,1},{4,6},{5,3},{6,8},{7,5},{8,10},{9,7},{10,1... | collective-permute-start | bytes 196616 | tf_op jit(solution)/shard_map/ppermute | solution.py:481
  5.3 1.5 %collective-permute-start.3 = (f32[32,256]{1,0:T(8,128)S(1)}, f32[32,256]{1,0:T(8,128)S(1)}, u32[]{:S(2)}, u32[]{:S(2)}) collective-permute-start(f32[32,256]{1,0:T(8,128)S(1)} %broadcast_multiply_fusion.z.start_own), channel_id=1, source_target_pairs={{0,2},{1,4},{2,0},{3,6},{4,1},{5,8},{6,3},{7,10},{8,5},{9,12},{10,... | collective-permute-start | bytes 98312 | tf_op jit(solution)/shard_map/ppermute | solution.py:480
  6.8 2.0 %shard_map.87 = (bf16[768,768]{1,0:T(8,128)(2,1)S(1)}, bf16[768,768]{1,0:T(8,128)(2,1)S(1)}, bf16[768,768]{1,0:T(8,128)(2,1)S(1)}, f32[8,128]{1,0:T(8,128)S(1)}) custom-call(f32[768,768]{1,0:T(8,128)} %bitcast.15), custom_call_target="tpu_custom_call" | custom-call | tf_op jit(solution)/shard_map/pallas_call | solution.py:431
  9.5 1.0 %collective-permute-done.4.b = f32[2,32,256]{2,1,0:T(8,128)S(1)} collective-permute-done((f32[2,32,256]{2,1,0:T(8,128)S(1)}, f32[2,32,256]{2,1,0:T(8,128)S(1)}, u32[]{:S(2)}, u32[]{:S(2)}) %collective-permute-start.4) | collective-permute-done | bytes 65568 | tf_op jit(solution)/shard_map/ppermute | solution.py:483
  10.5 0.7 %shard_map.89 = (f32[4,32,128]{2,1,0:T(8,128)S(1)}, f32[4,32,128]{2,1,0:T(8,128)S(1)}, f32[2,32,128]{2,1,0:T(8,128)S(1)}, f32[4,32,128]{2,1,0:T(8,128)S(1)}, f32...) custom-call(f32[88,8,128]{2,1,0:T(8,128)S(1)} %shard_map.86.places, bf16[768,768]{1,0:T(8,128)(2,1)S(1)} %get-tuple-element.58.high, ...), custom_call_target="tpu_custom_call" | custom-call | tf_op jit(solution)/shard_map/pallas_call | solution.py:431
  11.4 1.5 %collective-permute-start.5 = (f32[136,128]{1,0:T(8,128)S(1)}, f32[136,128]{1,0:T(8,128)S(1)}, u32[]{:S(2)}, u32[]{:S(2)}) collective-permute-start(f32[136,128]{1,0:T(8,128)S(1)} %get-tuple-element.67.mine), channel_id=1, source_target_pairs={{0,16},{16,0},{1,17},{17,1},{2,18},{18,2},{3,19},{19,3},{4,20},{20... | collective-permute-start | bytes 208904 | tf_op jit(solution)/shard_map/ppermute | solution.py:491
  13.1 2.0 %collective-permute-start.8 = (f32[2,32,128]{2,1,0:T(8,128)S(1)}, f32[2,32,128]{2,1,0:T(8,128)S(1)}, u32[]{:S(2)}, u32[]{:S(2)}) collective-permute-start(f32[2,32,128]{2,1,0:T(8,128)S(1)} %get-tuple-element.72), channel_id=1, source_target_pairs={{0,2},{1,4},{2,0},{3,6},{4,1},{5,8},{6,3},{7,10},{8,5},{9,12},{10,... | collective-permute-start | bytes 98312 | tf_op jit(solution)/shard_map/ppermute | solution.py:474
  15.1 0.8 %collective-permute-done.5.conds = f32[136,128]{1,0:T(8,128)S(1)} collective-permute-done((f32[136,128]{1,0:T(8,128)S(1)}, f32[136,128]{1,0:T(8,128)S(1)}, u32[]{:S(2)}, u32[]{:S(2)}) %collective-permute-start.5) | collective-permute-done | bytes 69664 | tf_op jit(solution)/shard_map/ppermute | solution.py:491
  16.0 1.6 %collective-permute-done.8.from_p2 = f32[2,32,128]{2,1,0:T(8,128)S(1)} collective-permute-done((f32[2,32,128]{2,1,0:T(8,128)S(1)}, f32[2,32,128]{2,1,0:T(8,128)S(1)}, u32[]{:S(2)}, u32[]{:S(2)}) %collective-permute-start.8) | collective-permute-done | bytes 32800 | tf_op jit(solution)/shard_map/ppermute | solution.py:474
  17.7 0.9 %collective-permute-start.9 = (f32[5,32,128]{2,1,0:T(8,128)S(1)}, f32[5,32,128]{2,1,0:T(8,128)S(1)}, u32[]{:S(2)}, u32[]{:S(2)}) collective-permute-start(f32[5,32,128]{2,1,0:T(8,128)S(1)} %shard_map.91.part), channel_id=1, source_target_pairs={{0,1},{1,0},{2,3},{3,2},{4,5},{5,4},{6,7},{7,6},{8,9},{9,8},{10,11... | collective-permute-start | bytes 245768 | tf_op jit(solution)/shard_map/ppermute | solution.py:500
  18.5 0.9 %collective-permute-done.9.there = f32[5,32,128]{2,1,0:T(8,128)S(1)} collective-permute-done((f32[5,32,128]{2,1,0:T(8,128)S(1)}, f32[5,32,128]{2,1,0:T(8,128)S(1)}, u32[]{:S(2)}, u32[]{:S(2)}) %collective-permute-start.9) | collective-permute-done | bytes 81952 | tf_op jit(solution)/shard_map/ppermute | solution.py:500
  19.5 1.7 %collective-permute-start.10 = (f32[4,32,128]{2,1,0:T(8,128)S(1)}, f32[4,32,128]{2,1,0:T(8,128)S(1)}, u32[]{:S(2)}, u32[]{:S(2)}) collective-permute-start(f32[4,32,128]{2,1,0:T(8,128)S(1)} %get-tuple-element.76), channel_id=1, source_target_pairs={{0,2},{1,0},{2,4},{3,1},{4,6},{5,3},{6,8},{7,5},{8,10},{9,7},{10,1... | collective-permute-start | bytes 196616 | tf_op jit(solution)/shard_map/ppermute | solution.py:507
  21.2 1.1 %collective-permute-start.11 = (f32[2,32,128]{2,1,0:T(8,128)S(1)}, f32[2,32,128]{2,1,0:T(8,128)S(1)}, u32[]{:S(2)}, u32[]{:S(2)}) collective-permute-start(f32[2,32,128]{2,1,0:T(8,128)S(1)} %get-tuple-element.75.scaled.own), channel_id=1, source_target_pairs={{0,2},{1,4},{2,0},{3,6},{4,1},{5,8},{6,3},{7,10},{8,5},{9,12},{10,... | collective-permute-start | bytes 98312 | tf_op jit(solution)/shard_map/ppermute | solution.py:508
  22.3 1.1 %collective-permute-start.13 = (f32[4,32,128]{2,1,0:T(8,128)S(1)}, f32[4,32,128]{2,1,0:T(8,128)S(1)}, u32[]{:S(2)}, u32[]{:S(2)}) collective-permute-start(f32[4,32,128]{2,1,0:T(8,128)S(1)} %get-tuple-element.76), channel_id=1, source_target_pairs={{0,16},{16,0},{1,17},{17,1},{2,18},{18,2},{3,19},{19,3},{4,20},{20... | collective-permute-start | bytes 196616 | tf_op jit(solution)/shard_map/ppermute | solution.py:509
  23.7 1.4 %collective-permute-done.11.p2 = f32[2,32,128]{2,1,0:T(8,128)S(1)} collective-permute-done((f32[2,32,128]{2,1,0:T(8,128)S(1)}, f32[2,32,128]{2,1,0:T(8,128)S(1)}, u32[]{:S(2)}, u32[]{:S(2)}) %collective-permute-start.11) | collective-permute-done | bytes 32800 | tf_op jit(solution)/shard_map/ppermute | solution.py:508
  25.1 1.5 %collective-permute-done.13.there = f32[4,32,128]{2,1,0:T(8,128)S(1)} collective-permute-done((f32[4,32,128]{2,1,0:T(8,128)S(1)}, f32[4,32,128]{2,1,0:T(8,128)S(1)}, u32[]{:S(2)}, u32[]{:S(2)}) %collective-permute-start.13) | collective-permute-done | bytes 65568 | tf_op jit(solution)/shard_map/ppermute | solution.py:509
  26.6 1.7 %shard_map.94 = (f32[24,8,128]{2,1,0:T(8,128)S(1)}, f32[24,8,128]{2,1,0:T(8,128)S(1)}, f32[9,8,128]{2,1,0:T(8,128)S(1)}, f32[32,4,128]{2,1,0:T(4,128)}) custom-call(f32[88,8,128]{2,1,0:T(8,128)S(1)} %shard_map.86.places, bf16[768,768]{1,0:T(8,128)(2,1)S(1)} %get-tuple-element.58.high, bf16[768,768]{1,0:T(8,128)(2,1)S(1)} %get-tuple-element.59.middle, ...), custom_call_target="tpu_custom_call" | custom-call | tf_op jit(solution)/shard_map/pallas_call | solution.py:431
  28.3 3.8 %all-to-all-start = ((f32[32,4,128]{2,1,0:T(4,128)}), f32[32,4,128]{2,1,0:T(4,128)S(1)}, u32[]{:S(2)}, u32[]{:S(2)}) async-start(f32[32,4,128]{2,1,0:T(4,128)} %get-tuple-element.99), calls=%async_computation | async-start | bytes 131072 | tf_op jit(solution)/shard_map/all_to_all | solution.py:527
  32.5 3.0 %collective-permute-start.16 = (f32[9,8,128]{2,1,0:T(8,128)S(1)}, f32[9,8,128]{2,1,0:T(8,128)S(1)}, u32[]{:S(2)}, u32[]{:S(2)}) collective-permute-start(f32[9,8,128]{2,1,0:T(8,128)S(1)} %get-tuple-element.97), channel_id=1, source_target_pairs={{0,2},{1,3},{2,0},{3,1},{4,6},{5,7},{6,4},{7,5},{8,10},{9,11},{10,... | collective-permute-start | bytes 110600 | tf_op jit(solution)/shard_map/ppermute | solution.py:525
  35.5 4.1 %all-to-all-done.sums = f32[32,4,128]{2,1,0:T(4,128)S(1)} async-done(((f32[32,4,128]{2,1,0:T(4,128)}), f32[32,4,128]{2,1,0:T(4,128)S(1)}, u32[]{:S(2)}, u32[]{:S(2)}) %all-to-all-start) | async-done | bytes 65568 | tf_op jit(solution)/shard_map/all_to_all | solution.py:527
  39.8 0.7 %shard_map.97 = (f32[32,256]{1,0:T(8,128)}, f32[32,256]{1,0:T(8,128)}) custom-call(f32[32,256]{1,0:T(8,128)S(1)} %bitcast.13, f32[32,256]{1,0:T(8,128)S(1)} %broadcast_multiply_fusion.z.start_own, f32[32,256]{1,0:T(8,128)S(1)} %get-tuple-element.74.image, f32[2,32,128]{2,1,0:T(8,128)S(1)} %get-tuple-element.75.scaled.own, ...), custom_call_target="tpu_custom_call" | custom-call | tf_op jit(solution)/shard_map/pallas_call | solution.py:431
  (43 shorter events, 2.3 us)
Async XLA Ops:
  0.6 1.5 %collective-permute-start = (f32[1,256]{1,0:T(1,128)}, f32[1,256]{1,0:T(1,128)S(1)}, u32[]{:S(2)}, u32[]{:S(2)}) collective-permute-start(f32[1,256]{1,0:T(1,128)} %precond.5), channel_id=1, source_target_pairs={{0,1},{1,0},{2,3},{3,2},{4,5},{5,4},{6,7},{7,6},{8,9},{9,8},{10,11... | collective-permute-start | bytes 3080 | tf_op jit(solution)/shard_map/ppermute | solution.py:478
  1.1 1.4 %collective-permute-start.1 = (f32[32,256]{1,0:T(8,128)}, f32[32,256]{1,0:T(8,128)S(1)}, u32[]{:S(2)}, u32[]{:S(2)}) collective-permute-start(f32[32,256]{1,0:T(8,128)} %bitcast.11), channel_id=1, source_target_pairs={{0,1},{1,0},{2,3},{3,2},{4,5},{5,4},{6,7},{7,6},{8,9},{9,8},{10,11... | collective-permute-start | bytes 98312 | tf_op jit(solution)/shard_map/ppermute | solution.py:479
  2.6 6.6 %collective-permute-start.2 = (f32[2,32,256]{2,1,0:T(8,128)S(1)}, f32[2,32,256]{2,1,0:T(8,128)S(1)}, u32[]{:S(2)}, u32[]{:S(2)}) collective-permute-start(f32[2,32,256]{2,1,0:T(8,128)S(1)} %pad_maximum_fusion.four), channel_id=1, source_target_pairs={{0,2},{1,0},{2,4},{3,1},{4,6},{5,3},{6,8},{7,5},{8,10},{9,7},{10,1... | collective-permute-start | bytes 196616 | tf_op jit(solution)/shard_map/ppermute | solution.py:481
  5.3 3.9 %collective-permute-start.3 = (f32[32,256]{1,0:T(8,128)S(1)}, f32[32,256]{1,0:T(8,128)S(1)}, u32[]{:S(2)}, u32[]{:S(2)}) collective-permute-start(f32[32,256]{1,0:T(8,128)S(1)} %broadcast_multiply_fusion.z.start_own), channel_id=1, source_target_pairs={{0,2},{1,4},{2,0},{3,6},{4,1},{5,8},{6,3},{7,10},{8,5},{9,12},{10,... | collective-permute-start | bytes 98312 | tf_op jit(solution)/shard_map/ppermute | solution.py:480
  6.8 2.5 %copy-start.4 = (s32[1,64]{1,0:T(1,128)S(1)}, s32[1,64]{1,0:T(1,128)}, u32[]{:S(2)}) copy-start(s32[1,64]{1,0:T(1,128)} %pad_rows.1) | copy-start | bytes 772
  6.8 2.5 %copy-start.5 = (f32[1,64]{1,0:T(1,128)S(1)}, f32[1,64]{1,0:T(1,128)}, u32[]{:S(2)}) copy-start(f32[1,64]{1,0:T(1,128)} %pad_cond.1) | copy-start | bytes 772
  9.2 1.3 %collective-permute-start.4 = (f32[2,32,256]{2,1,0:T(8,128)S(1)}, f32[2,32,256]{2,1,0:T(8,128)S(1)}, u32[]{:S(2)}, u32[]{:S(2)}) collective-permute-start(f32[2,32,256]{2,1,0:T(8,128)S(1)} %collective-permute-done.2.p1), channel_id=1, source_target_pairs={{0,1},{1,0},{2,3},{3,2},{4,5},{5,4},{6,7},{7,6},{8,9},{9,8},{10,11... | collective-permute-start | bytes 196616 | tf_op jit(solution)/shard_map/ppermute | solution.py:483
  10.5 5.4 %copy-start.2 = (f32[1,256]{1,0:T(1,128)S(1)}, f32[1,256]{1,0:T(1,128)}, u32[]{:S(2)}) copy-start(f32[1,256]{1,0:T(1,128)} %sink.5) | copy-start | bytes 3076
  10.5 7.2 %copy-start.1 = (f32[1,256]{1,0:T(1,128)S(1)}, f32[1,256]{1,0:T(1,128)}, u32[]{:S(2)}) copy-start(f32[1,256]{1,0:T(1,128)} %precond.5) | copy-start | bytes 3076
  11.2 12.2 %copy-start = (f32[1,32,256]{2,1,0:T(8,128)S(1)}, f32[1,32,256]{2,1,0:T(8,128)}, u32[]{:S(2)}) copy-start(f32[1,32,256]{2,1,0:T(8,128)} %param.7) | copy-start | bytes 98308
  11.2 1.7 %collective-permute-start.6 = (f32[4,32,128]{2,1,0:T(8,128)S(1)}, f32[4,32,128]{2,1,0:T(8,128)S(1)}, u32[]{:S(2)}, u32[]{:S(2)}) collective-permute-start(f32[4,32,128]{2,1,0:T(8,128)S(1)} %get-tuple-element.71), channel_id=1, source_target_pairs={{0,1},{1,0},{2,3},{3,2},{4,5},{5,4},{6,7},{7,6},{8,9},{9,8},{10,11... | collective-permute-start | bytes 196616 | tf_op jit(solution)/shard_map/ppermute | solution.py:475
  11.4 4.4 %collective-permute-start.5 = (f32[136,128]{1,0:T(8,128)S(1)}, f32[136,128]{1,0:T(8,128)S(1)}, u32[]{:S(2)}, u32[]{:S(2)}) collective-permute-start(f32[136,128]{1,0:T(8,128)S(1)} %get-tuple-element.67.mine), channel_id=1, source_target_pairs={{0,16},{16,0},{1,17},{17,1},{2,18},{18,2},{3,19},{19,3},{4,20},{20... | collective-permute-start | bytes 208904 | tf_op jit(solution)/shard_map/ppermute | solution.py:491
  13.0 4.7 %collective-permute-start.7 = (f32[4,32,128]{2,1,0:T(8,128)S(1)}, f32[4,32,128]{2,1,0:T(8,128)S(1)}, u32[]{:S(2)}, u32[]{:S(2)}) collective-permute-start(f32[4,32,128]{2,1,0:T(8,128)S(1)} %add.3), channel_id=1, source_target_pairs={{2,0},{0,1},{4,2},{1,3},{6,4},{3,5},{8,6},{5,7},{10,8},{7,9},{12,1... | collective-permute-start | bytes 196616 | tf_op jit(solution)/shard_map/ppermute | solution.py:498
  13.1 4.5 %collective-permute-start.8 = (f32[2,32,128]{2,1,0:T(8,128)S(1)}, f32[2,32,128]{2,1,0:T(8,128)S(1)}, u32[]{:S(2)}, u32[]{:S(2)}) collective-permute-start(f32[2,32,128]{2,1,0:T(8,128)S(1)} %get-tuple-element.72), channel_id=1, source_target_pairs={{0,2},{1,4},{2,0},{3,6},{4,1},{5,8},{6,3},{7,10},{8,5},{9,12},{10,... | collective-permute-start | bytes 98312 | tf_op jit(solution)/shard_map/ppermute | solution.py:474
  17.7 1.8 %collective-permute-start.9 = (f32[5,32,128]{2,1,0:T(8,128)S(1)}, f32[5,32,128]{2,1,0:T(8,128)S(1)}, u32[]{:S(2)}, u32[]{:S(2)}) collective-permute-start(f32[5,32,128]{2,1,0:T(8,128)S(1)} %shard_map.91.part), channel_id=1, source_target_pairs={{0,1},{1,0},{2,3},{3,2},{4,5},{5,4},{6,7},{7,6},{8,9},{9,8},{10,11... | collective-permute-start | bytes 245768 | tf_op jit(solution)/shard_map/ppermute | solution.py:500
  19.5 5.6 %collective-permute-start.10 = (f32[4,32,128]{2,1,0:T(8,128)S(1)}, f32[4,32,128]{2,1,0:T(8,128)S(1)}, u32[]{:S(2)}, u32[]{:S(2)}) collective-permute-start(f32[4,32,128]{2,1,0:T(8,128)S(1)} %get-tuple-element.76), channel_id=1, source_target_pairs={{0,2},{1,0},{2,4},{3,1},{4,6},{5,3},{6,8},{7,5},{8,10},{9,7},{10,1... | collective-permute-start | bytes 196616 | tf_op jit(solution)/shard_map/ppermute | solution.py:507
  21.2 3.9 %collective-permute-start.11 = (f32[2,32,128]{2,1,0:T(8,128)S(1)}, f32[2,32,128]{2,1,0:T(8,128)S(1)}, u32[]{:S(2)}, u32[]{:S(2)}) collective-permute-start(f32[2,32,128]{2,1,0:T(8,128)S(1)} %get-tuple-element.75.scaled.own), channel_id=1, source_target_pairs={{0,2},{1,4},{2,0},{3,6},{4,1},{5,8},{6,3},{7,10},{8,5},{9,12},{10,... | collective-permute-start | bytes 98312 | tf_op jit(solution)/shard_map/ppermute | solution.py:508
  22.3 4.3 %collective-permute-start.13 = (f32[4,32,128]{2,1,0:T(8,128)S(1)}, f32[4,32,128]{2,1,0:T(8,128)S(1)}, u32[]{:S(2)}, u32[]{:S(2)}) collective-permute-start(f32[4,32,128]{2,1,0:T(8,128)S(1)} %get-tuple-element.76), channel_id=1, source_target_pairs={{0,16},{16,0},{1,17},{17,1},{2,18},{18,2},{3,19},{19,3},{4,20},{20... | collective-permute-start | bytes 196616 | tf_op jit(solution)/shard_map/ppermute | solution.py:509
  25.1 1.5 %collective-permute-start.12 = (f32[4,32,128]{2,1,0:T(8,128)S(1)}, f32[4,32,128]{2,1,0:T(8,128)S(1)}, u32[]{:S(2)}, u32[]{:S(2)}) collective-permute-start(f32[4,32,128]{2,1,0:T(8,128)S(1)} %collective-permute-done.10.p1), channel_id=1, source_target_pairs={{0,1},{1,0},{2,3},{3,2},{4,5},{5,4},{6,7},{7,6},{8,9},{9,8},{10,11... | collective-permute-start | bytes 196616 | tf_op jit(solution)/shard_map/ppermute | solution.py:511
  28.3 3.8 %collective-permute-start.14 = (f32[24,8,128]{2,1,0:T(8,128)S(1)}, f32[24,8,128]{2,1,0:T(8,128)S(1)}, u32[]{:S(2)}, u32[]{:S(2)}) collective-permute-start(f32[24,8,128]{2,1,0:T(8,128)S(1)} %get-tuple-element.90), channel_id=1, source_target_pairs={{0,1},{1,0},{2,3},{3,2},{4,5},{5,4},{6,7},{7,6},{8,9},{9,8},{10,11... | collective-permute-start | bytes 294920 | tf_op jit(solution)/shard_map/ppermute | solution.py:521
  28.3 11.3 %all-to-all-start = ((f32[32,4,128]{2,1,0:T(4,128)}), f32[32,4,128]{2,1,0:T(4,128)S(1)}, u32[]{:S(2)}, u32[]{:S(2)}) async-start(f32[32,4,128]{2,1,0:T(4,128)} %get-tuple-element.99), calls=%async_computation | async-start | bytes 131072 | tf_op jit(solution)/shard_map/all_to_all | solution.py:527
  32.1 7.4 %collective-permute-start.15 = (f32[9,8,128]{2,1,0:T(8,128)S(1)}, f32[9,8,128]{2,1,0:T(8,128)S(1)}, u32[]{:S(2)}, u32[]{:S(2)}) collective-permute-start(f32[9,8,128]{2,1,0:T(8,128)S(1)} %get-tuple-element.96), channel_id=1, source_target_pairs={{0,1},{1,0},{2,4},{3,5},{4,2},{5,3},{6,8},{7,9},{8,6},{9,7},{10,12... | collective-permute-start | bytes 110600 | tf_op jit(solution)/shard_map/ppermute | solution.py:524
  32.5 7.1 %collective-permute-start.16 = (f32[9,8,128]{2,1,0:T(8,128)S(1)}, f32[9,8,128]{2,1,0:T(8,128)S(1)}, u32[]{:S(2)}, u32[]{:S(2)}) collective-permute-start(f32[9,8,128]{2,1,0:T(8,128)S(1)} %get-tuple-element.97), channel_id=1, source_target_pairs={{0,2},{1,3},{2,0},{3,1},{4,6},{5,7},{6,4},{7,5},{8,10},{9,11},{10,... | collective-permute-start | bytes 110600 | tf_op jit(solution)/shard_map/ppermute | solution.py:525
  35.4 4.1 %collective-permute-start.17 = (f32[9,8,128]{2,1,0:T(8,128)S(1)}, f32[9,8,128]{2,1,0:T(8,128)S(1)}, u32[]{:S(2)}, u32[]{:S(2)}) collective-permute-start(f32[9,8,128]{2,1,0:T(8,128)S(1)} %get-tuple-element.98), channel_id=1, source_target_pairs={{0,2},{1,4},{2,0},{3,6},{4,1},{5,8},{6,3},{7,10},{8,5},{9,12},{10,... | collective-permute-start | bytes 110600 | tf_op jit(solution)/shard_map/ppermute | solution.py:526
  (1 other events, 2.4 us)

commit v7 on v6

--- a/solution.py
+++ b/solution.py
@@ -153,17 +153,41 @@
     top[...] = jnp.broadcast_to(jnp.max(largest, axis=1, keepdims=True), top.shape)
 
 
+def late_kernel(blocks, high, middle, low, late_high, late_middle, late_low):
+    position = lax.axis_index("sub")
+    core = lax.rem(position, 2)
+    touched = blocks.shape[1]
+    spots = []
+    for i in range(touched):
+        offset = blocks[0, i] // 2 - position
+        mirrored = jnp.where(core == 0, offset, -offset)
+        place = jnp.where(mirrored == 2, 6, jnp.where(mirrored == 3, 5, mirrored + REACH))
+        spots.append(place * 2 + lax.rem(blocks[0, i], 2))
+    for j in range(LATE):
+        source = jnp.int32(-1)
+        for i in range(touched):
+            source = jnp.where(spots[i] == SPOTS - LATE + j, i, source)
+        rows = pl.ds(pl.multiple_of(jnp.maximum(source, 0) * BR, BR), BR)
+        keep = jnp.where(source >= 0, 1.0, 0.0)
+        for part, late in ((high, late_high), (middle, late_middle), (low, late_low)):
+            late[j * BR : (j + 1) * BR] = (part[rows].astype(F32) * keep).astype(HALF)
+
+
 def spot(places, i, cases):
     return jnp.concatenate([places[i]] * (cases // 8))
 
 
-def picked_blocks(places, held, touched):
-    cases, spots = held[0].shape[0], len(held)
+SPOTS = 2 * (2 * REACH + 1)
+LATE = 4
+
+
+def picked_blocks(places, held, touched, begin):
+    cases = held[0].shape[0]
     picked = []
     for i in range(touched):
-        total = spot(places, i * spots, cases) * held[0]
-        for j in range(1, spots):
-            total = total + spot(places, i * spots + j, cases) * held[j]
+        total = spot(places, i * SPOTS + begin, cases) * held[0]
+        for j in range(1, len(held)):
+            total = total + spot(places, i * SPOTS + begin + j, cases) * held[j]
         picked.append(total)
     return jnp.concatenate(picked, axis=1)
 
@@ -184,10 +208,6 @@
     return [value[:, start : start + BR] for value in values for start in (0, BR)]
 
 
-def held_blocks(p2, p1, own, a, b):
-    return [p2[0], p2[1], p1[0], p1[1], p1[2], p1[3], own[0], own[1], a[0], a[1], b[0], b[1], b[2], b[3]]
-
-
 def mean_of(mine, conds, cases, count):
     return 0.5 * (mine[cases : cases + 1, :count] + conds[cases : cases + 1, :count])
 
@@ -195,8 +215,7 @@
 def first_kernel(
     places, high, middle, low, p2, p1, four, b, back, to_p1, to_p2, kept, picked_out, product_out
 ):
-    touched = high.shape[0] // BR
-    picked = picked_blocks(places, halves(p2, p1[0], p1[1], four[0], four[1], b[0], b[1]), touched)
+    picked = picked_blocks(places, halves(p2, p1[0], p1[1], four[0], four[1], b[0], b[1]), high.shape[0] // BR, 0)
     product = product_of(4.0 * picked, high, middle, low)
     landed = landed_blocks(places, product)
     for j in range(2):
@@ -285,19 +304,29 @@
     ref[start * tiles : (start + 1) * tiles] = block.reshape(tiles, 8, BR)
 
 
+def second_early_kernel(places, high, middle, low, p2, p1, own, a, top, picked_out, product_out):
+    held = [p2[0], p2[1], p1[0], p1[1], p1[2], p1[3], own[0], own[1], a[0], a[1]]
+    picked = picked_blocks(places, held, high.shape[0] // BR, 0)
+    picked_out[...] = picked
+    product_out[...] = product_of((picked * (4.0 / top[0:1, 0:1])) * (1.0 / 1024.0), high, middle, low)
+
+
 def second_kernel(
-    places, high, middle, low, p2, p1, own, a, b, there, conds, mine, ones, ones_there, at_pads, sink, top,
+    places, high, middle, low, own, b, early, early_product, there, conds, mine, ones, ones_there, at_pads, sink, top,
     start_picked, start_product, start_jump, start_own, known, guide,
     given, stays, to_p2, sums,
 ):
-    touched = high.shape[0] // BR
     cases = own.shape[1]
     count = ones.shape[1]
     less = 4.0 / top[0:1, 0:1]
-    picked = picked_blocks(places, held_blocks(p2, p1, own, a, b), touched)
-    product = product_of((picked * less) * (1.0 / 1024.0), high, middle, low)
+    held = [b[j] for j in range(LATE)]
+    picked = early[...] + picked_blocks(places, held, early.shape[1] // BR, SPOTS - LATE)
+    late = (jnp.concatenate(held, axis=1) * less) * (1.0 / 1024.0)
+    product = early_product[...] + product_of(late, high, middle, low)
+    scales = jnp.concatenate([there[4, 0:1], there[4, 1:2]], axis=1)
+    values = scales * wide(there[0:2] + b[4:6])
     here = wide(own)
-    jump = at_pads[...] - times_ones(wide(there[0:2]), ones_there[...], False)
+    jump = at_pads[...] - times_ones(values, ones_there[...], False)
     mean = mean_of(mine, conds, cases, count)
     local = sink[...] * here + times_ones(mean * jump, ones[...], True)
     local = (local * less) * (1.0 / 4096.0)
@@ -424,13 +453,13 @@
     residual[...] = rhs[...] - alpha * image[...] - step * (grown * image[...] - second)
 
 
-def call(kernel, outs, *operands, scratch=(), far=(), grant=32):
+def call(kernel, outs, *operands, scratch=(), far=(), scalar=(), grant=32):
     def space(outside, i):
         return pl.BlockSpec(memory_space=pl.ANY if i in outside else pltpu.VMEM)
 
     return pl.pallas_call(
         kernel,
-        in_specs=[space(far, i) for i in range(len(operands))],
+        in_specs=[pl.BlockSpec(memory_space=pltpu.SMEM) if i in scalar else space(far, i) for i in range(len(operands))],
         out_specs=[space((), i) for i in range(len(outs))],
         out_shape=[jax.ShapeDtypeStruct(shape, kind) for shape, kind in outs],
         scratch_shapes=list(scratch),
@@ -483,11 +512,11 @@
     b = lax.ppermute(p1, "sub", swap)
     b, ones, pads_sent = barrier((b, ones, pads_sent))
     split = (places, high, middle, low)
+    half = [((cases, inner), F32)] * 2
     back, to_p1, to_p2, kept, start_picked, start_product = call(
-        first_kernel,
-        [both, both, pair, both, ((cases, inner), F32), ((cases, inner), F32)],
-        *split, p2, p1, four, b,
-    )
+        first_kernel, [both, both, pair, both] + half, *split, p2, p1, four, b
+    )
+    late = call(late_kernel, [((LATE * BR, inner), HALF)] * 3, block_list, high, middle, low, scalar=(0,))
     conds = lax.ppermute(pads_sent, "board", across)
     local, start_jump, ones_there = call(
         ties_kernel,
@@ -496,8 +525,10 @@
     )
     to_p1, from_p2 = collect(back, to_p1, to_p2)
     from_p1 = lax.ppermute(to_p1, "sub", turned(near))
+    from_p1, from_p2, late = barrier((from_p1, from_p2, late))
     (part,) = call(part_kernel, [((2 * blocks + 1, cases, BR), F32)], places, kept, local, from_p1, from_p2, precond, top)
     part_there = lax.ppermute(part, "sub", swap)
+    part_across = lax.ppermute(part, "board", across)
     image, four, own, top = call(turn_kernel, [full, both, pair, tile], part, part_there, precond)
     known, guide, at_pads = call(
         shares_kernel,
@@ -506,16 +537,17 @@
     )
     p1 = lax.ppermute(four, "sub", near)
     p2 = lax.ppermute(own, "sub", far)
-    there = lax.ppermute(four, "board", across)
-    p1, p2, known, guide, at_pads = barrier((p1, p2, known, guide, at_pads))
-    b = lax.ppermute(p1, "sub", swap)
+    p1, p2, part_across, known, guide, at_pads = barrier((p1, p2, part_across, known, guide, at_pads))
+    b = lax.ppermute(jnp.concatenate([p1, part_across[blocks : 2 * blocks]]), "sub", swap)
+    early = call(second_early_kernel, half, *split, p2, p1, own, four[blocks:], top)
+    b, early = barrier((b, early))
     tiles = cases // 8
     pair_tiles = ((2 * tiles, 8, BR), F32)
     sent = ((2 * tiles + 1, 8, BR), F32)
     given, stays, to_p2, sums = call(
         second_kernel,
         [((6 * tiles, 8, BR), F32)] * 2 + [sent, ((everyone, 4, BR), F32)],
-        *split, p2, p1, own, four[blocks:], b, there, conds, pads_sent, ones, ones_there, at_pads, sink, top,
+        places, *late, own, b, *early, part_across, conds, pads_sent, ones, ones_there, at_pads, sink, top,
         start_picked, start_product, start_jump, z, known, guide,
     )
     given = lax.ppermute(given, "sub", swap)

time: 40.7 us -> 40.6 us (level)
  waiting for transfers between devices: 12.2 us -> 10.5 us
  Pallas kernels: 6.02 us -> 7.56 us
    pallas_call x12 -> x14, Pallas kernels: 6.02 us -> 7.56 us  [call(): pl.pallas_call(kernel, in_specs=[pl.BlockSpec(memory_space=pltpu.SMEM) if...]
    ppermute x1, waiting for transfers between devices: 0.92 us -> 0.01 us  [on_device(): part_there = lax.ppermute(part, 'sub', swap)]
    ppermute x1, waiting for transfers between devices: 0.82 us -> 0.01 us  [on_device(): conds = lax.ppermute(pads_sent, 'board', across)]
    ppermute x1, waiting for transfers between devices: 1.42 us -> 2.11 us  [on_device(): p2 = lax.ppermute(own, 'sub', far)]
    ppermute x1 -> x2, waiting for transfers between devices: 1.47 us -> 0.94 us  [the longest x1 0.54 us: on_device(): lax.ppermute(jnp.concatenate([p1, part_across[blocks:2 * blocks]]), 'sub'...]
    ppermute x1 -> x2, starting transfers between devices: 1.09 us -> 1.16 us  [the longest x1 1.09 us: on_device(): part_across = lax.ppermute(part, 'board', across)]
    ppermute x2 -> x1, waiting for transfers between devices: 0.96 us -> 0.96 us  [on_device(): b = lax.ppermute(p1, 'sub', swap)]
  transfers between devices with their start and end apart: 19 -> 19, of which waited for: 10 -> 9; matrix products, arithmetic and copies ran while one was open for 2% -> 2% of each run, Pallas kernels for 7% -> 11%
where the time goes in v7:
time: 40.6 us; the launch traced here: 40.4 us
  starting transfers between devices  20.7 us (51%)
  waiting for transfers between devices  10.5 us (26%)
  Pallas kernels  7.56 us (19%)
  other arithmetic  0.81 us (2%)
  between operations  0.79 us (2%)
    pallas_call x14, Pallas kernels, call(): pl.pallas_call(kernel, in_specs=[pl.BlockSpec(memory_space=pltpu.SMEM) if...  7.56 us
    ppermute x2, starting transfers between devices, on_device(): p1 = lax.ppermute(four, 'sub', near)  4.23 us
    all_to_all x1, waiting for transfers between devices, on_device(): all_sums = lax.all_to_all(sums, ('board', 'sub'), 0, 0)  4.08 us
    all_to_all x1, starting transfers between devices, on_device(): all_sums = lax.all_to_all(sums, ('board', 'sub'), 0, 0)  3.9 us
    ppermute x1, starting transfers between devices, on_device(): from_e = lax.ppermute(to_e, 'sub', [(i, i ^ 2) for i in range(count)])  2.98 us
    ppermute x1, waiting for transfers between devices, on_device(): p2 = lax.ppermute(own, 'sub', far)  2.11 us
    ppermute x1, starting transfers between devices, collect(): from_p2 = lax.ppermute(to_p2, 'sub', far)  1.96 us
    ppermute x1, starting transfers between devices, on_device(): p2 = lax.ppermute(z, 'sub', far)  1.55 us
  transfers between devices with their start and end apart: 19, of which 9 were waited for; matrix products, arithmetic and copies ran while one was open for 2% of the time, Pallas kernels for 11%

profile of v7, /device:TPU:0, one launch (start us, length us, event | category | flops | bytes accessed | tf_op | source)
XLA Modules:
  0.0 40.4 jit_solution(18215362175083447863)
XLA Ops:
  0.6 0.5 %collective-permute-start = (f32[1,256]{1,0:T(1,128)}, f32[1,256]{1,0:T(1,128)S(1)}, u32[]{:S(2)}, u32[]{:S(2)}) collective-permute-start(f32[1,256]{1,0:T(1,128)} %precond.5), channel_id=1, source_target_pairs={{0,1},{1,0},{2,3},{3,2},{4,5},{5,4},{6,7},{7,6},{8,9},{9,8},{10,11... | collective-permute-start | bytes 3080 | tf_op jit(solution)/shard_map/ppermute | solution.py:507
  1.2 0.8 %broadcast_multiply_fusion.z.start_own = f32[32,256]{1,0:T(8,128)S(1)} fusion(f32[256]{0:T(256)} %bitcast.14, f32[1,32,256]{2,1,0:T(8,128)} %param.7), kind=kLoop, calls=%fused_computation.3 | loop fusion | flops 8192 | bytes 66560 | tf_op jit(solution)/shard_map/mul | solution.py:488
  2.6 2.7 %collective-permute-start.2 = (f32[2,32,256]{2,1,0:T(8,128)S(1)}, f32[2,32,256]{2,1,0:T(8,128)S(1)}, u32[]{:S(2)}, u32[]{:S(2)}) collective-permute-start(f32[2,32,256]{2,1,0:T(8,128)S(1)} %pad_maximum_fusion.1.four), channel_id=1, source_target_pairs={{0,2},{1,0},{2,4},{3,1},{4,6},{5,3},{6,8},{7,5},{8,10},{9,7},{10,1... | collective-permute-start | bytes 196616 | tf_op jit(solution)/shard_map/ppermute | solution.py:510
  5.3 1.5 %collective-permute-start.3 = (f32[32,256]{1,0:T(8,128)S(1)}, f32[32,256]{1,0:T(8,128)S(1)}, u32[]{:S(2)}, u32[]{:S(2)}) collective-permute-start(f32[32,256]{1,0:T(8,128)S(1)} %broadcast_multiply_fusion.z.start_own), channel_id=1, source_target_pairs={{0,2},{1,4},{2,0},{3,6},{4,1},{5,8},{6,3},{7,10},{8,5},{9,12},{10,... | collective-permute-start | bytes 98312 | tf_op jit(solution)/shard_map/ppermute | solution.py:509
  6.8 2.0 %shard_map.87 = (bf16[768,768]{1,0:T(8,128)(2,1)S(1)}, bf16[768,768]{1,0:T(8,128)(2,1)S(1)}, bf16[768,768]{1,0:T(8,128)(2,1)S(1)}, f32[8,128]{1,0:T(8,128)S(1)}) custom-call(f32[768,768]{1,0:T(8,128)} %bitcast.15), custom_call_target="tpu_custom_call" | custom-call | tf_op jit(solution)/shard_map/pallas_call | solution.py:460
  9.5 1.0 %collective-permute-done.4.b = f32[2,32,256]{2,1,0:T(8,128)S(1)} collective-permute-done((f32[2,32,256]{2,1,0:T(8,128)S(1)}, f32[2,32,256]{2,1,0:T(8,128)S(1)}, u32[]{:S(2)}, u32[]{:S(2)}) %collective-permute-start.4) | collective-permute-done | bytes 65568 | tf_op jit(solution)/shard_map/ppermute | solution.py:512
  10.5 0.7 %shard_map.89 = (f32[4,32,128]{2,1,0:T(8,128)S(1)}, f32[4,32,128]{2,1,0:T(8,128)S(1)}, f32[2,32,128]{2,1,0:T(8,128)S(1)}, f32[4,32,128]{2,1,0:T(8,128)S(1)}, f32...) custom-call(f32[88,8,128]{2,1,0:T(8,128)S(1)} %shard_map.86.places, bf16[768,768]{1,0:T(8,128)(2,1)S(1)} %get-tuple-element.72.high, ...), custom_call_target="tpu_custom_call" | custom-call | tf_op jit(solution)/shard_map/pallas_call | solution.py:460
  11.4 1.5 %collective-permute-start.5 = (f32[136,128]{1,0:T(8,128)S(1)}, f32[136,128]{1,0:T(8,128)S(1)}, u32[]{:S(2)}, u32[]{:S(2)}) collective-permute-start(f32[136,128]{1,0:T(8,128)S(1)} %get-tuple-element.81.mine), channel_id=1, source_target_pairs={{0,16},{16,0},{1,17},{17,1},{2,18},{18,2},{3,19},{19,3},{4,20},{20... | collective-permute-start | bytes 208904 | tf_op jit(solution)/shard_map/ppermute | solution.py:520
  13.1 2.0 %collective-permute-start.8 = (f32[2,32,128]{2,1,0:T(8,128)S(1)}, f32[2,32,128]{2,1,0:T(8,128)S(1)}, u32[]{:S(2)}, u32[]{:S(2)}) collective-permute-start(f32[2,32,128]{2,1,0:T(8,128)S(1)} %get-tuple-element.86), channel_id=1, source_target_pairs={{0,2},{1,4},{2,0},{3,6},{4,1},{5,8},{6,3},{7,10},{8,5},{9,12},{10,... | collective-permute-start | bytes 98312 | tf_op jit(solution)/shard_map/ppermute | solution.py:503
  15.0 1.0 %shard_map.91 = (bf16[512,768]{1,0:T(8,128)(2,1)S(1)}, bf16[512,768]{1,0:T(8,128)(2,1)S(1)}, bf16[512,768]{1,0:T(8,128)(2,1)S(1)}) custom-call(s32[1,6]{1,0:T(1,128)S(1)} %copy-done.3, bf16[768,768]{1,0:T(8,128)(2,1)S(1)} %get-tuple-element.72.high, bf16[768,768]{1,0:T(8,128)(2,1)S(1)} %get-tuple-element.73.middle, bf16[768,768]{1,0:T(8,128)(2,1)S(1)} %get-tuple-element.74.low), custom_call_target="tpu_custom_call" | custom-call | tf_op jit(solution)/shard_map/pallas_call | solution.py:460
  16.2 1.4 %collective-permute-done.8.from_p2 = f32[2,32,128]{2,1,0:T(8,128)S(1)} collective-permute-done((f32[2,32,128]{2,1,0:T(8,128)S(1)}, f32[2,32,128]{2,1,0:T(8,128)S(1)}, u32[]{:S(2)}, u32[]{:S(2)}) %collective-permute-start.8) | collective-permute-done | bytes 32800 | tf_op jit(solution)/shard_map/ppermute | solution.py:503
  17.7 0.9 %collective-permute-start.9 = (f32[5,32,128]{2,1,0:T(8,128)S(1)}, f32[5,32,128]{2,1,0:T(8,128)S(1)}, u32[]{:S(2)}, u32[]{:S(2)}) collective-permute-start(f32[5,32,128]{2,1,0:T(8,128)S(1)} %shard_map.92.part), channel_id=1, source_target_pairs={{0,1},{1,0},{2,3},{3,2},{4,5},{5,4},{6,7},{7,6},{8,9},{9,8},{10,11... | collective-permute-start | bytes 245768 | tf_op jit(solution)/shard_map/ppermute | solution.py:530
  18.5 1.1 %collective-permute-start.12 = (f32[5,32,128]{2,1,0:T(8,128)S(1)}, f32[5,32,128]{2,1,0:T(8,128)S(1)}, u32[]{:S(2)}, u32[]{:S(2)}) collective-permute-start(f32[5,32,128]{2,1,0:T(8,128)S(1)} %shard_map.92.part), channel_id=1, source_target_pairs={{0,16},{16,0},{1,17},{17,1},{2,18},{18,2},{3,19},{19,3},{4,20},{20... | collective-permute-start | bytes 245768 | tf_op jit(solution)/shard_map/ppermute | solution.py:531
  19.6 1.5 %collective-permute-start.10 = (f32[4,32,128]{2,1,0:T(8,128)S(1)}, f32[4,32,128]{2,1,0:T(8,128)S(1)}, u32[]{:S(2)}, u32[]{:S(2)}) collective-permute-start(f32[4,32,128]{2,1,0:T(8,128)S(1)} %get-tuple-element.98), channel_id=1, source_target_pairs={{0,2},{1,0},{2,4},{3,1},{4,6},{5,3},{6,8},{7,5},{8,10},{9,7},{10,1... | collective-permute-start | bytes 196616 | tf_op jit(solution)/shard_map/ppermute | solution.py:538
  21.2 1.1 %collective-permute-start.11 = (f32[2,32,128]{2,1,0:T(8,128)S(1)}, f32[2,32,128]{2,1,0:T(8,128)S(1)}, u32[]{:S(2)}, u32[]{:S(2)}) collective-permute-start(f32[2,32,128]{2,1,0:T(8,128)S(1)} %get-tuple-element.94.scaled.own), channel_id=1, source_target_pairs={{0,2},{1,4},{2,0},{3,6},{4,1},{5,8},{6,3},{7,10},{8,5},{9,12},{10,... | collective-permute-start | bytes 98312 | tf_op jit(solution)/shard_map/ppermute | solution.py:539
  22.6 0.4 collective-permute-done.12.there
  23.0 2.1 %collective-permute-done.11.p2 = f32[2,32,128]{2,1,0:T(8,128)S(1)} collective-permute-done((f32[2,32,128]{2,1,0:T(8,128)S(1)}, f32[2,32,128]{2,1,0:T(8,128)S(1)}, u32[]{:S(2)}, u32[]{:S(2)}) %collective-permute-start.11) | collective-permute-done | bytes 32800 | tf_op jit(solution)/shard_map/ppermute | solution.py:539
  25.2 0.7 %shard_map.95 = (f32[32,768]{1,0:T(8,128)S(1)}, f32[32,768]{1,0:T(8,128)S(1)}) custom-call(f32[88,8,128]{2,1,0:T(8,128)S(1)} %shard_map.86.places, bf16[768,768]{1,0:T(8,128)(2,1)S(1)} %get-tuple-element.72.high, bf16[768,768]{1,0:T(8,128)(2,1)S(1)} %get-tuple-element.73.middle, bf16[768,768]{1,0:T(8,128)(2,1)S(1)} %get-tuple-element.74.low, ...), custom_call_target="tpu_custom_call" | custom-call | tf_op jit(solution)/shard_map/pallas_call | solution.py:460
  25.9 0.5 %collective-permute-done.13.b = f32[6,32,128]{2,1,0:T(8,128)S(1)} collective-permute-done((f32[6,32,128]{2,1,0:T(8,128)S(1)}, f32[6,32,128]{2,1,0:T(8,128)S(1)}, u32[]{:S(2)}, u32[]{:S(2)}) %collective-permute-start.13) | collective-permute-done | bytes 98336 | tf_op jit(solution)/shard_map/ppermute | solution.py:541
  26.5 1.5 %shard_map.96 = (f32[24,8,128]{2,1,0:T(8,128)S(1)}, f32[24,8,128]{2,1,0:T(8,128)S(1)}, f32[9,8,128]{2,1,0:T(8,128)S(1)}, f32[32,4,128]{2,1,0:T(4,128)}) custom-call(f32[88,8,128]{2,1,0:T(8,128)S(1)} %shard_map.86.places, bf16[512,768]{1,0:T(8,128)(2,1)S(1)} %get-tuple-element.95.high, bf16[512,768]{1,0:T(8,128)(2,1)S(1)} %get-tuple-element.96.middle, ...), custom_call_target="tpu_custom_call" | custom-call | tf_op jit(solution)/shard_map/pallas_call | solution.py:460
  28.1 3.9 %all-to-all-start = ((f32[32,4,128]{2,1,0:T(4,128)}), f32[32,4,128]{2,1,0:T(4,128)S(1)}, u32[]{:S(2)}, u32[]{:S(2)}) async-start(f32[32,4,128]{2,1,0:T(4,128)} %get-tuple-element.127), calls=%async_computation | async-start | bytes 131072 | tf_op jit(solution)/shard_map/all_to_all | solution.py:559
  32.4 3.0 %collective-permute-start.16 = (f32[9,8,128]{2,1,0:T(8,128)S(1)}, f32[9,8,128]{2,1,0:T(8,128)S(1)}, u32[]{:S(2)}, u32[]{:S(2)}) collective-permute-start(f32[9,8,128]{2,1,0:T(8,128)S(1)} %get-tuple-element.125), channel_id=1, source_target_pairs={{0,2},{1,3},{2,0},{3,1},{4,6},{5,7},{6,4},{7,5},{8,10},{9,11},{10,... | collective-permute-start | bytes 110600 | tf_op jit(solution)/shard_map/ppermute | solution.py:557
  35.4 4.1 %all-to-all-done.sums = f32[32,4,128]{2,1,0:T(4,128)S(1)} async-done(((f32[32,4,128]{2,1,0:T(4,128)}), f32[32,4,128]{2,1,0:T(4,128)S(1)}, u32[]{:S(2)}, u32[]{:S(2)}) %all-to-all-start) | async-done | bytes 65568 | tf_op jit(solution)/shard_map/all_to_all | solution.py:559
  39.7 0.7 %shard_map.99 = (f32[32,256]{1,0:T(8,128)}, f32[32,256]{1,0:T(8,128)}) custom-call(f32[32,256]{1,0:T(8,128)S(1)} %bitcast.13, f32[32,256]{1,0:T(8,128)S(1)} %broadcast_multiply_fusion.z.start_own, f32[32,256]{1,0:T(8,128)S(1)} %get-tuple-element.93.image, f32[2,32,128]{2,1,0:T(8,128)S(1)} %get-tuple-element.94.scaled.own, ...), custom_call_target="tpu_custom_call" | custom-call | tf_op jit(solution)/shard_map/pallas_call | solution.py:460
  (47 shorter events, 3.0 us)
Async XLA Ops:
  0.6 1.5 %collective-permute-start = (f32[1,256]{1,0:T(1,128)}, f32[1,256]{1,0:T(1,128)S(1)}, u32[]{:S(2)}, u32[]{:S(2)}) collective-permute-start(f32[1,256]{1,0:T(1,128)} %precond.5), channel_id=1, source_target_pairs={{0,1},{1,0},{2,3},{3,2},{4,5},{5,4},{6,7},{7,6},{8,9},{9,8},{10,11... | collective-permute-start | bytes 3080 | tf_op jit(solution)/shard_map/ppermute | solution.py:507
  1.1 1.4 %collective-permute-start.1 = (f32[32,256]{1,0:T(8,128)}, f32[32,256]{1,0:T(8,128)S(1)}, u32[]{:S(2)}, u32[]{:S(2)}) collective-permute-start(f32[32,256]{1,0:T(8,128)} %bitcast.11), channel_id=1, source_target_pairs={{0,1},{1,0},{2,3},{3,2},{4,5},{5,4},{6,7},{7,6},{8,9},{9,8},{10,11... | collective-permute-start | bytes 98312 | tf_op jit(solution)/shard_map/ppermute | solution.py:508
  2.6 6.6 %collective-permute-start.2 = (f32[2,32,256]{2,1,0:T(8,128)S(1)}, f32[2,32,256]{2,1,0:T(8,128)S(1)}, u32[]{:S(2)}, u32[]{:S(2)}) collective-permute-start(f32[2,32,256]{2,1,0:T(8,128)S(1)} %pad_maximum_fusion.1.four), channel_id=1, source_target_pairs={{0,2},{1,0},{2,4},{3,1},{4,6},{5,3},{6,8},{7,5},{8,10},{9,7},{10,1... | collective-permute-start | bytes 196616 | tf_op jit(solution)/shard_map/ppermute | solution.py:510
  5.3 3.9 %collective-permute-start.3 = (f32[32,256]{1,0:T(8,128)S(1)}, f32[32,256]{1,0:T(8,128)S(1)}, u32[]{:S(2)}, u32[]{:S(2)}) collective-permute-start(f32[32,256]{1,0:T(8,128)S(1)} %broadcast_multiply_fusion.z.start_own), channel_id=1, source_target_pairs={{0,2},{1,4},{2,0},{3,6},{4,1},{5,8},{6,3},{7,10},{8,5},{9,12},{10,... | collective-permute-start | bytes 98312 | tf_op jit(solution)/shard_map/ppermute | solution.py:509
  6.8 2.5 %copy-start.4 = (s32[1,64]{1,0:T(1,128)S(1)}, s32[1,64]{1,0:T(1,128)}, u32[]{:S(2)}) copy-start(s32[1,64]{1,0:T(1,128)} %pad_rows.1) | copy-start | bytes 772
  6.8 2.5 %copy-start.5 = (f32[1,64]{1,0:T(1,128)S(1)}, f32[1,64]{1,0:T(1,128)}, u32[]{:S(2)}) copy-start(f32[1,64]{1,0:T(1,128)} %pad_cond.1) | copy-start | bytes 772
  9.2 1.3 %collective-permute-start.4 = (f32[2,32,256]{2,1,0:T(8,128)S(1)}, f32[2,32,256]{2,1,0:T(8,128)S(1)}, u32[]{:S(2)}, u32[]{:S(2)}) collective-permute-start(f32[2,32,256]{2,1,0:T(8,128)S(1)} %collective-permute-done.2.p1), channel_id=1, source_target_pairs={{0,1},{1,0},{2,3},{3,2},{4,5},{5,4},{6,7},{7,6},{8,9},{9,8},{10,11... | collective-permute-start | bytes 196616 | tf_op jit(solution)/shard_map/ppermute | solution.py:512
  11.2 1.7 %collective-permute-start.6 = (f32[4,32,128]{2,1,0:T(8,128)S(1)}, f32[4,32,128]{2,1,0:T(8,128)S(1)}, u32[]{:S(2)}, u32[]{:S(2)}) collective-permute-start(f32[4,32,128]{2,1,0:T(8,128)S(1)} %get-tuple-element.85), channel_id=1, source_target_pairs={{0,1},{1,0},{2,3},{3,2},{4,5},{5,4},{6,7},{7,6},{8,9},{9,8},{10,11... | collective-permute-start | bytes 196616 | tf_op jit(solution)/shard_map/ppermute | solution.py:504
  11.4 4.6 %collective-permute-start.5 = (f32[136,128]{1,0:T(8,128)S(1)}, f32[136,128]{1,0:T(8,128)S(1)}, u32[]{:S(2)}, u32[]{:S(2)}) collective-permute-start(f32[136,128]{1,0:T(8,128)S(1)} %get-tuple-element.81.mine), channel_id=1, source_target_pairs={{0,16},{16,0},{1,17},{17,1},{2,18},{18,2},{3,19},{19,3},{4,20},{20... | collective-permute-start | bytes 208904 | tf_op jit(solution)/shard_map/ppermute | solution.py:520
  13.0 4.7 %collective-permute-start.7 = (f32[4,32,128]{2,1,0:T(8,128)S(1)}, f32[4,32,128]{2,1,0:T(8,128)S(1)}, u32[]{:S(2)}, u32[]{:S(2)}) collective-permute-start(f32[4,32,128]{2,1,0:T(8,128)S(1)} %add.3), channel_id=1, source_target_pairs={{2,0},{0,1},{4,2},{1,3},{6,4},{3,5},{8,6},{5,7},{10,8},{7,9},{12,1... | collective-permute-start | bytes 196616 | tf_op jit(solution)/shard_map/ppermute | solution.py:527
  13.1 3.0 %copy-start.2 = (f32[1,256]{1,0:T(1,128)S(1)}, f32[1,256]{1,0:T(1,128)}, u32[]{:S(2)}) copy-start(f32[1,256]{1,0:T(1,128)} %sink.5) | copy-start | bytes 3076
  13.1 4.5 %copy-start.1 = (f32[1,256]{1,0:T(1,128)S(1)}, f32[1,256]{1,0:T(1,128)}, u32[]{:S(2)}) copy-start(f32[1,256]{1,0:T(1,128)} %precond.5) | copy-start | bytes 3076
  13.1 9.2 %copy-start = (f32[1,32,256]{2,1,0:T(8,128)S(1)}, f32[1,32,256]{2,1,0:T(8,128)}, u32[]{:S(2)}) copy-start(f32[1,32,256]{2,1,0:T(8,128)} %param.7) | copy-start | bytes 98308
  13.1 4.5 %collective-permute-start.8 = (f32[2,32,128]{2,1,0:T(8,128)S(1)}, f32[2,32,128]{2,1,0:T(8,128)S(1)}, u32[]{:S(2)}, u32[]{:S(2)}) collective-permute-start(f32[2,32,128]{2,1,0:T(8,128)S(1)} %get-tuple-element.86), channel_id=1, source_target_pairs={{0,2},{1,4},{2,0},{3,6},{4,1},{5,8},{6,3},{7,10},{8,5},{9,12},{10,... | collective-permute-start | bytes 98312 | tf_op jit(solution)/shard_map/ppermute | solution.py:503
  17.7 2.0 %collective-permute-start.9 = (f32[5,32,128]{2,1,0:T(8,128)S(1)}, f32[5,32,128]{2,1,0:T(8,128)S(1)}, u32[]{:S(2)}, u32[]{:S(2)}) collective-permute-start(f32[5,32,128]{2,1,0:T(8,128)S(1)} %shard_map.92.part), channel_id=1, source_target_pairs={{0,1},{1,0},{2,3},{3,2},{4,5},{5,4},{6,7},{7,6},{8,9},{9,8},{10,11... | collective-permute-start | bytes 245768 | tf_op jit(solution)/shard_map/ppermute | solution.py:530
  18.5 4.4 %collective-permute-start.12 = (f32[5,32,128]{2,1,0:T(8,128)S(1)}, f32[5,32,128]{2,1,0:T(8,128)S(1)}, u32[]{:S(2)}, u32[]{:S(2)}) collective-permute-start(f32[5,32,128]{2,1,0:T(8,128)S(1)} %shard_map.92.part), channel_id=1, source_target_pairs={{0,16},{16,0},{1,17},{17,1},{2,18},{18,2},{3,19},{19,3},{4,20},{20... | collective-permute-start | bytes 245768 | tf_op jit(solution)/shard_map/ppermute | solution.py:531
  19.6 5.4 %collective-permute-start.10 = (f32[4,32,128]{2,1,0:T(8,128)S(1)}, f32[4,32,128]{2,1,0:T(8,128)S(1)}, u32[]{:S(2)}, u32[]{:S(2)}) collective-permute-start(f32[4,32,128]{2,1,0:T(8,128)S(1)} %get-tuple-element.98), channel_id=1, source_target_pairs={{0,2},{1,0},{2,4},{3,1},{4,6},{5,3},{6,8},{7,5},{8,10},{9,7},{10,1... | collective-permute-start | bytes 196616 | tf_op jit(solution)/shard_map/ppermute | solution.py:538
  21.2 3.9 %collective-permute-start.11 = (f32[2,32,128]{2,1,0:T(8,128)S(1)}, f32[2,32,128]{2,1,0:T(8,128)S(1)}, u32[]{:S(2)}, u32[]{:S(2)}) collective-permute-start(f32[2,32,128]{2,1,0:T(8,128)S(1)} %get-tuple-element.94.scaled.own), channel_id=1, source_target_pairs={{0,2},{1,4},{2,0},{3,6},{4,1},{5,8},{6,3},{7,10},{8,5},{9,12},{10,... | collective-permute-start | bytes 98312 | tf_op jit(solution)/shard_map/ppermute | solution.py:539
  25.1 1.4 %collective-permute-start.13 = (f32[6,32,128]{2,1,0:T(8,128)S(1)}, f32[6,32,128]{2,1,0:T(8,128)S(1)}, u32[]{:S(2)}, u32[]{:S(2)}) collective-permute-start(f32[6,32,128]{2,1,0:T(8,128)S(1)} %pad_maximum_fusion), channel_id=1, source_target_pairs={{0,1},{1,0},{2,3},{3,2},{4,5},{5,4},{6,7},{7,6},{8,9},{9,8},{10,11... | collective-permute-start | bytes 294920 | tf_op jit(solution)/shard_map/ppermute | solution.py:541
  28.0 4.1 %collective-permute-start.14 = (f32[24,8,128]{2,1,0:T(8,128)S(1)}, f32[24,8,128]{2,1,0:T(8,128)S(1)}, u32[]{:S(2)}, u32[]{:S(2)}) collective-permute-start(f32[24,8,128]{2,1,0:T(8,128)S(1)} %get-tuple-element.118), channel_id=1, source_target_pairs={{0,1},{1,0},{2,3},{3,2},{4,5},{5,4},{6,7},{7,6},{8,9},{9,8},{10,11... | collective-permute-start | bytes 294920 | tf_op jit(solution)/shard_map/ppermute | solution.py:553
  28.1 11.4 %all-to-all-start = ((f32[32,4,128]{2,1,0:T(4,128)}), f32[32,4,128]{2,1,0:T(4,128)S(1)}, u32[]{:S(2)}, u32[]{:S(2)}) async-start(f32[32,4,128]{2,1,0:T(4,128)} %get-tuple-element.127), calls=%async_computation | async-start | bytes 131072 | tf_op jit(solution)/shard_map/all_to_all | solution.py:559
  32.1 7.4 %collective-permute-start.15 = (f32[9,8,128]{2,1,0:T(8,128)S(1)}, f32[9,8,128]{2,1,0:T(8,128)S(1)}, u32[]{:S(2)}, u32[]{:S(2)}) collective-permute-start(f32[9,8,128]{2,1,0:T(8,128)S(1)} %get-tuple-element.124), channel_id=1, source_target_pairs={{0,1},{1,0},{2,4},{3,5},{4,2},{5,3},{6,8},{7,9},{8,6},{9,7},{10,12... | collective-permute-start | bytes 110600 | tf_op jit(solution)/shard_map/ppermute | solution.py:556
  32.4 7.1 %collective-permute-start.16 = (f32[9,8,128]{2,1,0:T(8,128)S(1)}, f32[9,8,128]{2,1,0:T(8,128)S(1)}, u32[]{:S(2)}, u32[]{:S(2)}) collective-permute-start(f32[9,8,128]{2,1,0:T(8,128)S(1)} %get-tuple-element.125), channel_id=1, source_target_pairs={{0,2},{1,3},{2,0},{3,1},{4,6},{5,7},{6,4},{7,5},{8,10},{9,11},{10,... | collective-permute-start | bytes 110600 | tf_op jit(solution)/shard_map/ppermute | solution.py:557
  35.4 4.1 %collective-permute-start.17 = (f32[9,8,128]{2,1,0:T(8,128)S(1)}, f32[9,8,128]{2,1,0:T(8,128)S(1)}, u32[]{:S(2)}, u32[]{:S(2)}) collective-permute-start(f32[9,8,128]{2,1,0:T(8,128)S(1)} %get-tuple-element.126), channel_id=1, source_target_pairs={{0,2},{1,4},{2,0},{3,6},{4,1},{5,8},{6,3},{7,10},{8,5},{9,12},{10,... | collective-permute-start | bytes 110600 | tf_op jit(solution)/shard_map/ppermute | solution.py:558
  (1 other events, 2.4 us)

commit v8 on v7

--- a/solution.py
+++ b/solution.py
@@ -401,8 +401,7 @@
     to_o[pair] = top[...]
 
 
-def steps_kernel(sums, steps):
-    cases = steps.shape[1]
+def steps_of(sums, cases):
     rows = [sums[:, i, :] for i in range(3)]
 
     def value(i):
@@ -424,14 +423,13 @@
     two = alpha * other_size
     one = grown * size - two * tilt
     bend = everyone(((one * one) * energy + two * (two * other_energy - 2.0 * one * cross)) * top)
-    for i, row in enumerate((alpha, grown, fresh / bend)):
-        steps[i] = jnp.broadcast_to(as_column(row, 0, cases), steps.shape[1:])
-
-
-def end_kernel(rhs, z, image, scaled, places, own, from_e, from_o, from_p2, top, steps, solution, residual):
+    return [as_column(row, 0, cases) for row in (alpha, grown, fresh / bend)]
+
+
+def end_kernel(rhs, z, image, scaled, places, own, from_e, from_o, from_p2, top, sums, solution, residual):
     cases = solution.shape[0]
     tiles = cases // 8
-    alpha, grown, step = [wide([steps[i], steps[i]]) for i in range(3)]
+    alpha, grown, step = steps_of(sums, cases)
     start = z[...]
     direction = grown * start - alpha * wide(scaled)
     solution[...] = alpha * start + step * direction
@@ -558,11 +556,10 @@
     from_p2 = lax.ppermute(to_p2, "sub", far)
     all_sums = lax.all_to_all(sums, ("board", "sub"), 0, 0)
     from_o, from_e, from_p2, all_sums = barrier((from_o, from_e, from_p2, all_sums))
-    (steps,) = call(steps_kernel, [((3, cases, BR), F32)], all_sums)
     solution, residual = call(
         end_kernel,
         [full, full],
-        rhs[0], z, image, own, places, own_part, from_e, from_o, from_p2, top, steps,
+        rhs[0], z, image, own, places, own_part, from_e, from_o, from_p2, top, all_sums,
     )
     return (solution[None], residual[None])
 

time: 40.6 us -> 40.6 us (level)
    pallas_call x14 -> x13, Pallas kernels: 7.56 us -> 7.53 us  [call(): pl.pallas_call(kernel, in_specs=[pl.BlockSpec(memory_space=pltpu.SMEM) if...]
where the time goes in v8:
time: 40.6 us; the launch traced here: 40.3 us
  starting transfers between devices  20.7 us (51%)
  waiting for transfers between devices  10.5 us (26%)
  Pallas kernels  7.53 us (19%)
  other arithmetic  0.81 us (2%)
  between operations  0.79 us (2%)
    pallas_call x13, Pallas kernels, call(): pl.pallas_call(kernel, in_specs=[pl.BlockSpec(memory_space=pltpu.SMEM) if...  7.53 us
    ppermute x2, starting transfers between devices, on_device(): p1 = lax.ppermute(four, 'sub', near)  4.23 us
    all_to_all x1, waiting for transfers between devices, on_device(): all_sums = lax.all_to_all(sums, ('board', 'sub'), 0, 0)  4.08 us
    all_to_all x1, starting transfers between devices, on_device(): all_sums = lax.all_to_all(sums, ('board', 'sub'), 0, 0)  3.9 us
    ppermute x1, starting transfers between devices, on_device(): from_e = lax.ppermute(to_e, 'sub', [(i, i ^ 2) for i in range(count)])  2.98 us
    ppermute x1, waiting for transfers between devices, on_device(): p2 = lax.ppermute(own, 'sub', far)  2.11 us
    ppermute x1, starting transfers between devices, collect(): from_p2 = lax.ppermute(to_p2, 'sub', far)  1.96 us
    ppermute x1, starting transfers between devices, on_device(): p2 = lax.ppermute(z, 'sub', far)  1.55 us
  transfers between devices with their start and end apart: 19, of which 9 were waited for; matrix products, arithmetic and copies ran while one was open for 2% of the time, Pallas kernels for 11%

profile of v8, /device:TPU:0, one launch (start us, length us, event | category | flops | bytes accessed | tf_op | source)
XLA Modules:
  0.0 40.3 jit_solution(2336252293059760416)
XLA Ops:
  0.6 0.5 %collective-permute-start = (f32[1,256]{1,0:T(1,128)}, f32[1,256]{1,0:T(1,128)S(1)}, u32[]{:S(2)}, u32[]{:S(2)}) collective-permute-start(f32[1,256]{1,0:T(1,128)} %precond.5), channel_id=1, source_target_pairs={{0,1},{1,0},{2,3},{3,2},{4,5},{5,4},{6,7},{7,6},{8,9},{9,8},{10,11... | collective-permute-start | bytes 3080 | tf_op jit(solution)/shard_map/ppermute | solution.py:505
  1.2 0.8 %broadcast_multiply_fusion.z.start_own = f32[32,256]{1,0:T(8,128)S(1)} fusion(f32[256]{0:T(256)} %bitcast.14, f32[1,32,256]{2,1,0:T(8,128)} %param.7), kind=kLoop, calls=%fused_computation.3 | loop fusion | flops 8192 | bytes 66560 | tf_op jit(solution)/shard_map/mul | solution.py:486
  2.6 2.7 %collective-permute-start.2 = (f32[2,32,256]{2,1,0:T(8,128)S(1)}, f32[2,32,256]{2,1,0:T(8,128)S(1)}, u32[]{:S(2)}, u32[]{:S(2)}) collective-permute-start(f32[2,32,256]{2,1,0:T(8,128)S(1)} %pad_maximum_fusion.1.four), channel_id=1, source_target_pairs={{0,2},{1,0},{2,4},{3,1},{4,6},{5,3},{6,8},{7,5},{8,10},{9,7},{10,1... | collective-permute-start | bytes 196616 | tf_op jit(solution)/shard_map/ppermute | solution.py:508
  5.3 1.5 %collective-permute-start.3 = (f32[32,256]{1,0:T(8,128)S(1)}, f32[32,256]{1,0:T(8,128)S(1)}, u32[]{:S(2)}, u32[]{:S(2)}) collective-permute-start(f32[32,256]{1,0:T(8,128)S(1)} %broadcast_multiply_fusion.z.start_own), channel_id=1, source_target_pairs={{0,2},{1,4},{2,0},{3,6},{4,1},{5,8},{6,3},{7,10},{8,5},{9,12},{10,... | collective-permute-start | bytes 98312 | tf_op jit(solution)/shard_map/ppermute | solution.py:507
  6.8 2.0 %shard_map.87 = (bf16[768,768]{1,0:T(8,128)(2,1)S(1)}, bf16[768,768]{1,0:T(8,128)(2,1)S(1)}, bf16[768,768]{1,0:T(8,128)(2,1)S(1)}, f32[8,128]{1,0:T(8,128)S(1)}) custom-call(f32[768,768]{1,0:T(8,128)} %bitcast.15), custom_call_target="tpu_custom_call" | custom-call | tf_op jit(solution)/shard_map/pallas_call | solution.py:458
  9.5 1.0 %collective-permute-done.4.b = f32[2,32,256]{2,1,0:T(8,128)S(1)} collective-permute-done((f32[2,32,256]{2,1,0:T(8,128)S(1)}, f32[2,32,256]{2,1,0:T(8,128)S(1)}, u32[]{:S(2)}, u32[]{:S(2)}) %collective-permute-start.4) | collective-permute-done | bytes 65568 | tf_op jit(solution)/shard_map/ppermute | solution.py:510
  10.5 0.7 %shard_map.89 = (f32[4,32,128]{2,1,0:T(8,128)S(1)}, f32[4,32,128]{2,1,0:T(8,128)S(1)}, f32[2,32,128]{2,1,0:T(8,128)S(1)}, f32[4,32,128]{2,1,0:T(8,128)S(1)}, f32...) custom-call(f32[88,8,128]{2,1,0:T(8,128)S(1)} %shard_map.86.places, bf16[768,768]{1,0:T(8,128)(2,1)S(1)} %get-tuple-element.72.high, ...), custom_call_target="tpu_custom_call" | custom-call | tf_op jit(solution)/shard_map/pallas_call | solution.py:458
  11.4 1.5 %collective-permute-start.5 = (f32[136,128]{1,0:T(8,128)S(1)}, f32[136,128]{1,0:T(8,128)S(1)}, u32[]{:S(2)}, u32[]{:S(2)}) collective-permute-start(f32[136,128]{1,0:T(8,128)S(1)} %get-tuple-element.81.mine), channel_id=1, source_target_pairs={{0,16},{16,0},{1,17},{17,1},{2,18},{18,2},{3,19},{19,3},{4,20},{20... | collective-permute-start | bytes 208904 | tf_op jit(solution)/shard_map/ppermute | solution.py:518
  13.1 2.0 %collective-permute-start.8 = (f32[2,32,128]{2,1,0:T(8,128)S(1)}, f32[2,32,128]{2,1,0:T(8,128)S(1)}, u32[]{:S(2)}, u32[]{:S(2)}) collective-permute-start(f32[2,32,128]{2,1,0:T(8,128)S(1)} %get-tuple-element.86), channel_id=1, source_target_pairs={{0,2},{1,4},{2,0},{3,6},{4,1},{5,8},{6,3},{7,10},{8,5},{9,12},{10,... | collective-permute-start | bytes 98312 | tf_op jit(solution)/shard_map/ppermute | solution.py:501
  15.0 1.0 %shard_map.91 = (bf16[512,768]{1,0:T(8,128)(2,1)S(1)}, bf16[512,768]{1,0:T(8,128)(2,1)S(1)}, bf16[512,768]{1,0:T(8,128)(2,1)S(1)}) custom-call(s32[1,6]{1,0:T(1,128)S(1)} %copy-done.3, bf16[768,768]{1,0:T(8,128)(2,1)S(1)} %get-tuple-element.72.high, bf16[768,768]{1,0:T(8,128)(2,1)S(1)} %get-tuple-element.73.middle, bf16[768,768]{1,0:T(8,128)(2,1)S(1)} %get-tuple-element.74.low), custom_call_target="tpu_custom_call" | custom-call | tf_op jit(solution)/shard_map/pallas_call | solution.py:458
  16.2 1.4 %collective-permute-done.8.from_p2 = f32[2,32,128]{2,1,0:T(8,128)S(1)} collective-permute-done((f32[2,32,128]{2,1,0:T(8,128)S(1)}, f32[2,32,128]{2,1,0:T(8,128)S(1)}, u32[]{:S(2)}, u32[]{:S(2)}) %collective-permute-start.8) | collective-permute-done | bytes 32800 | tf_op jit(solution)/shard_map/ppermute | solution.py:501
  17.7 0.9 %collective-permute-start.9 = (f32[5,32,128]{2,1,0:T(8,128)S(1)}, f32[5,32,128]{2,1,0:T(8,128)S(1)}, u32[]{:S(2)}, u32[]{:S(2)}) collective-permute-start(f32[5,32,128]{2,1,0:T(8,128)S(1)} %shard_map.92.part), channel_id=1, source_target_pairs={{0,1},{1,0},{2,3},{3,2},{4,5},{5,4},{6,7},{7,6},{8,9},{9,8},{10,11... | collective-permute-start | bytes 245768 | tf_op jit(solution)/shard_map/ppermute | solution.py:528
  18.5 1.1 %collective-permute-start.12 = (f32[5,32,128]{2,1,0:T(8,128)S(1)}, f32[5,32,128]{2,1,0:T(8,128)S(1)}, u32[]{:S(2)}, u32[]{:S(2)}) collective-permute-start(f32[5,32,128]{2,1,0:T(8,128)S(1)} %shard_map.92.part), channel_id=1, source_target_pairs={{0,16},{16,0},{1,17},{17,1},{2,18},{18,2},{3,19},{19,3},{4,20},{20... | collective-permute-start | bytes 245768 | tf_op jit(solution)/shard_map/ppermute | solution.py:529
  19.6 1.5 %collective-permute-start.10 = (f32[4,32,128]{2,1,0:T(8,128)S(1)}, f32[4,32,128]{2,1,0:T(8,128)S(1)}, u32[]{:S(2)}, u32[]{:S(2)}) collective-permute-start(f32[4,32,128]{2,1,0:T(8,128)S(1)} %get-tuple-element.98), channel_id=1, source_target_pairs={{0,2},{1,0},{2,4},{3,1},{4,6},{5,3},{6,8},{7,5},{8,10},{9,7},{10,1... | collective-permute-start | bytes 196616 | tf_op jit(solution)/shard_map/ppermute | solution.py:536
  21.2 1.1 %collective-permute-start.11 = (f32[2,32,128]{2,1,0:T(8,128)S(1)}, f32[2,32,128]{2,1,0:T(8,128)S(1)}, u32[]{:S(2)}, u32[]{:S(2)}) collective-permute-start(f32[2,32,128]{2,1,0:T(8,128)S(1)} %get-tuple-element.94.scaled.own), channel_id=1, source_target_pairs={{0,2},{1,4},{2,0},{3,6},{4,1},{5,8},{6,3},{7,10},{8,5},{9,12},{10,... | collective-permute-start | bytes 98312 | tf_op jit(solution)/shard_map/ppermute | solution.py:537
  22.6 0.4 collective-permute-done.12.there
  23.0 2.1 %collective-permute-done.11.p2 = f32[2,32,128]{2,1,0:T(8,128)S(1)} collective-permute-done((f32[2,32,128]{2,1,0:T(8,128)S(1)}, f32[2,32,128]{2,1,0:T(8,128)S(1)}, u32[]{:S(2)}, u32[]{:S(2)}) %collective-permute-start.11) | collective-permute-done | bytes 32800 | tf_op jit(solution)/shard_map/ppermute | solution.py:537
  25.2 0.7 %shard_map.95 = (f32[32,768]{1,0:T(8,128)S(1)}, f32[32,768]{1,0:T(8,128)S(1)}) custom-call(f32[88,8,128]{2,1,0:T(8,128)S(1)} %shard_map.86.places, bf16[768,768]{1,0:T(8,128)(2,1)S(1)} %get-tuple-element.72.high, bf16[768,768]{1,0:T(8,128)(2,1)S(1)} %get-tuple-element.73.middle, bf16[768,768]{1,0:T(8,128)(2,1)S(1)} %get-tuple-element.74.low, ...), custom_call_target="tpu_custom_call" | custom-call | tf_op jit(solution)/shard_map/pallas_call | solution.py:458
  25.9 0.5 %collective-permute-done.13.b = f32[6,32,128]{2,1,0:T(8,128)S(1)} collective-permute-done((f32[6,32,128]{2,1,0:T(8,128)S(1)}, f32[6,32,128]{2,1,0:T(8,128)S(1)}, u32[]{:S(2)}, u32[]{:S(2)}) %collective-permute-start.13) | collective-permute-done | bytes 98336 | tf_op jit(solution)/shard_map/ppermute | solution.py:539
  26.5 1.5 %shard_map.96 = (f32[24,8,128]{2,1,0:T(8,128)S(1)}, f32[24,8,128]{2,1,0:T(8,128)S(1)}, f32[9,8,128]{2,1,0:T(8,128)S(1)}, f32[32,4,128]{2,1,0:T(4,128)}) custom-call(f32[88,8,128]{2,1,0:T(8,128)S(1)} %shard_map.86.places, bf16[512,768]{1,0:T(8,128)(2,1)S(1)} %get-tuple-element.95.high, bf16[512,768]{1,0:T(8,128)(2,1)S(1)} %get-tuple-element.96.middle, ...), custom_call_target="tpu_custom_call" | custom-call | tf_op jit(solution)/shard_map/pallas_call | solution.py:458
  28.1 3.9 %all-to-all-start = ((f32[32,4,128]{2,1,0:T(4,128)}), f32[32,4,128]{2,1,0:T(4,128)S(1)}, u32[]{:S(2)}, u32[]{:S(2)}) async-start(f32[32,4,128]{2,1,0:T(4,128)} %get-tuple-element.127), calls=%async_computation | async-start | bytes 131072 | tf_op jit(solution)/shard_map/all_to_all | solution.py:557
  32.4 3.0 %collective-permute-start.16 = (f32[9,8,128]{2,1,0:T(8,128)S(1)}, f32[9,8,128]{2,1,0:T(8,128)S(1)}, u32[]{:S(2)}, u32[]{:S(2)}) collective-permute-start(f32[9,8,128]{2,1,0:T(8,128)S(1)} %get-tuple-element.125), channel_id=1, source_target_pairs={{0,2},{1,3},{2,0},{3,1},{4,6},{5,7},{6,4},{7,5},{8,10},{9,11},{10,... | collective-permute-start | bytes 110600 | tf_op jit(solution)/shard_map/ppermute | solution.py:555
  35.4 4.1 %all-to-all-done.sums = f32[32,4,128]{2,1,0:T(4,128)S(1)} async-done(((f32[32,4,128]{2,1,0:T(4,128)}), f32[32,4,128]{2,1,0:T(4,128)S(1)}, u32[]{:S(2)}, u32[]{:S(2)}) %all-to-all-start) | async-done | bytes 65568 | tf_op jit(solution)/shard_map/all_to_all | solution.py:557
  39.5 0.9 %shard_map.98 = (f32[32,256]{1,0:T(8,128)}, f32[32,256]{1,0:T(8,128)}) custom-call(f32[32,256]{1,0:T(8,128)S(1)} %bitcast.13, f32[32,256]{1,0:T(8,128)S(1)} %broadcast_multiply_fusion.z.start_own, f32[32,256]{1,0:T(8,128)S(1)} %get-tuple-element.93.image, f32[2,32,128]{2,1,0:T(8,128)S(1)} %get-tuple-element.94.scaled.own, ...), custom_call_target="tpu_custom_call" | custom-call | tf_op jit(solution)/shard_map/pallas_call | solution.py:458
  (46 shorter events, 2.7 us)
Async XLA Ops:
  0.6 1.5 %collective-permute-start = (f32[1,256]{1,0:T(1,128)}, f32[1,256]{1,0:T(1,128)S(1)}, u32[]{:S(2)}, u32[]{:S(2)}) collective-permute-start(f32[1,256]{1,0:T(1,128)} %precond.5), channel_id=1, source_target_pairs={{0,1},{1,0},{2,3},{3,2},{4,5},{5,4},{6,7},{7,6},{8,9},{9,8},{10,11... | collective-permute-start | bytes 3080 | tf_op jit(solution)/shard_map/ppermute | solution.py:505
  1.1 1.4 %collective-permute-start.1 = (f32[32,256]{1,0:T(8,128)}, f32[32,256]{1,0:T(8,128)S(1)}, u32[]{:S(2)}, u32[]{:S(2)}) collective-permute-start(f32[32,256]{1,0:T(8,128)} %bitcast.11), channel_id=1, source_target_pairs={{0,1},{1,0},{2,3},{3,2},{4,5},{5,4},{6,7},{7,6},{8,9},{9,8},{10,11... | collective-permute-start | bytes 98312 | tf_op jit(solution)/shard_map/ppermute | solution.py:506
  2.6 6.6 %collective-permute-start.2 = (f32[2,32,256]{2,1,0:T(8,128)S(1)}, f32[2,32,256]{2,1,0:T(8,128)S(1)}, u32[]{:S(2)}, u32[]{:S(2)}) collective-permute-start(f32[2,32,256]{2,1,0:T(8,128)S(1)} %pad_maximum_fusion.1.four), channel_id=1, source_target_pairs={{0,2},{1,0},{2,4},{3,1},{4,6},{5,3},{6,8},{7,5},{8,10},{9,7},{10,1... | collective-permute-start | bytes 196616 | tf_op jit(solution)/shard_map/ppermute | solution.py:508
  5.3 3.9 %collective-permute-start.3 = (f32[32,256]{1,0:T(8,128)S(1)}, f32[32,256]{1,0:T(8,128)S(1)}, u32[]{:S(2)}, u32[]{:S(2)}) collective-permute-start(f32[32,256]{1,0:T(8,128)S(1)} %broadcast_multiply_fusion.z.start_own), channel_id=1, source_target_pairs={{0,2},{1,4},{2,0},{3,6},{4,1},{5,8},{6,3},{7,10},{8,5},{9,12},{10,... | collective-permute-start | bytes 98312 | tf_op jit(solution)/shard_map/ppermute | solution.py:507
  6.8 2.5 %copy-start.4 = (s32[1,64]{1,0:T(1,128)S(1)}, s32[1,64]{1,0:T(1,128)}, u32[]{:S(2)}) copy-start(s32[1,64]{1,0:T(1,128)} %pad_rows.1) | copy-start | bytes 772
  6.8 2.5 %copy-start.5 = (f32[1,64]{1,0:T(1,128)S(1)}, f32[1,64]{1,0:T(1,128)}, u32[]{:S(2)}) copy-start(f32[1,64]{1,0:T(1,128)} %pad_cond.1) | copy-start | bytes 772
  9.2 1.3 %collective-permute-start.4 = (f32[2,32,256]{2,1,0:T(8,128)S(1)}, f32[2,32,256]{2,1,0:T(8,128)S(1)}, u32[]{:S(2)}, u32[]{:S(2)}) collective-permute-start(f32[2,32,256]{2,1,0:T(8,128)S(1)} %collective-permute-done.2.p1), channel_id=1, source_target_pairs={{0,1},{1,0},{2,3},{3,2},{4,5},{5,4},{6,7},{7,6},{8,9},{9,8},{10,11... | collective-permute-start | bytes 196616 | tf_op jit(solution)/shard_map/ppermute | solution.py:510
  11.2 1.7 %collective-permute-start.6 = (f32[4,32,128]{2,1,0:T(8,128)S(1)}, f32[4,32,128]{2,1,0:T(8,128)S(1)}, u32[]{:S(2)}, u32[]{:S(2)}) collective-permute-start(f32[4,32,128]{2,1,0:T(8,128)S(1)} %get-tuple-element.85), channel_id=1, source_target_pairs={{0,1},{1,0},{2,3},{3,2},{4,5},{5,4},{6,7},{7,6},{8,9},{9,8},{10,11... | collective-permute-start | bytes 196616 | tf_op jit(solution)/shard_map/ppermute | solution.py:502
  11.4 4.6 %collective-permute-start.5 = (f32[136,128]{1,0:T(8,128)S(1)}, f32[136,128]{1,0:T(8,128)S(1)}, u32[]{:S(2)}, u32[]{:S(2)}) collective-permute-start(f32[136,128]{1,0:T(8,128)S(1)} %get-tuple-element.81.mine), channel_id=1, source_target_pairs={{0,16},{16,0},{1,17},{17,1},{2,18},{18,2},{3,19},{19,3},{4,20},{20... | collective-permute-start | bytes 208904 | tf_op jit(solution)/shard_map/ppermute | solution.py:518
  13.0 4.7 %collective-permute-start.7 = (f32[4,32,128]{2,1,0:T(8,128)S(1)}, f32[4,32,128]{2,1,0:T(8,128)S(1)}, u32[]{:S(2)}, u32[]{:S(2)}) collective-permute-start(f32[4,32,128]{2,1,0:T(8,128)S(1)} %add.3), channel_id=1, source_target_pairs={{2,0},{0,1},{4,2},{1,3},{6,4},{3,5},{8,6},{5,7},{10,8},{7,9},{12,1... | collective-permute-start | bytes 196616 | tf_op jit(solution)/shard_map/ppermute | solution.py:525
  13.1 3.0 %copy-start.2 = (f32[1,256]{1,0:T(1,128)S(1)}, f32[1,256]{1,0:T(1,128)}, u32[]{:S(2)}) copy-start(f32[1,256]{1,0:T(1,128)} %sink.5) | copy-start | bytes 3076
  13.1 4.5 %copy-start.1 = (f32[1,256]{1,0:T(1,128)S(1)}, f32[1,256]{1,0:T(1,128)}, u32[]{:S(2)}) copy-start(f32[1,256]{1,0:T(1,128)} %precond.5) | copy-start | bytes 3076
  13.1 9.2 %copy-start = (f32[1,32,256]{2,1,0:T(8,128)S(1)}, f32[1,32,256]{2,1,0:T(8,128)}, u32[]{:S(2)}) copy-start(f32[1,32,256]{2,1,0:T(8,128)} %param.7) | copy-start | bytes 98308
  13.1 4.5 %collective-permute-start.8 = (f32[2,32,128]{2,1,0:T(8,128)S(1)}, f32[2,32,128]{2,1,0:T(8,128)S(1)}, u32[]{:S(2)}, u32[]{:S(2)}) collective-permute-start(f32[2,32,128]{2,1,0:T(8,128)S(1)} %get-tuple-element.86), channel_id=1, source_target_pairs={{0,2},{1,4},{2,0},{3,6},{4,1},{5,8},{6,3},{7,10},{8,5},{9,12},{10,... | collective-permute-start | bytes 98312 | tf_op jit(solution)/shard_map/ppermute | solution.py:501
  17.7 2.0 %collective-permute-start.9 = (f32[5,32,128]{2,1,0:T(8,128)S(1)}, f32[5,32,128]{2,1,0:T(8,128)S(1)}, u32[]{:S(2)}, u32[]{:S(2)}) collective-permute-start(f32[5,32,128]{2,1,0:T(8,128)S(1)} %shard_map.92.part), channel_id=1, source_target_pairs={{0,1},{1,0},{2,3},{3,2},{4,5},{5,4},{6,7},{7,6},{8,9},{9,8},{10,11... | collective-permute-start | bytes 245768 | tf_op jit(solution)/shard_map/ppermute | solution.py:528
  18.5 4.4 %collective-permute-start.12 = (f32[5,32,128]{2,1,0:T(8,128)S(1)}, f32[5,32,128]{2,1,0:T(8,128)S(1)}, u32[]{:S(2)}, u32[]{:S(2)}) collective-permute-start(f32[5,32,128]{2,1,0:T(8,128)S(1)} %shard_map.92.part), channel_id=1, source_target_pairs={{0,16},{16,0},{1,17},{17,1},{2,18},{18,2},{3,19},{19,3},{4,20},{20... | collective-permute-start | bytes 245768 | tf_op jit(solution)/shard_map/ppermute | solution.py:529
  19.6 5.4 %collective-permute-start.10 = (f32[4,32,128]{2,1,0:T(8,128)S(1)}, f32[4,32,128]{2,1,0:T(8,128)S(1)}, u32[]{:S(2)}, u32[]{:S(2)}) collective-permute-start(f32[4,32,128]{2,1,0:T(8,128)S(1)} %get-tuple-element.98), channel_id=1, source_target_pairs={{0,2},{1,0},{2,4},{3,1},{4,6},{5,3},{6,8},{7,5},{8,10},{9,7},{10,1... | collective-permute-start | bytes 196616 | tf_op jit(solution)/shard_map/ppermute | solution.py:536
  21.2 3.9 %collective-permute-start.11 = (f32[2,32,128]{2,1,0:T(8,128)S(1)}, f32[2,32,128]{2,1,0:T(8,128)S(1)}, u32[]{:S(2)}, u32[]{:S(2)}) collective-permute-start(f32[2,32,128]{2,1,0:T(8,128)S(1)} %get-tuple-element.94.scaled.own), channel_id=1, source_target_pairs={{0,2},{1,4},{2,0},{3,6},{4,1},{5,8},{6,3},{7,10},{8,5},{9,12},{10,... | collective-permute-start | bytes 98312 | tf_op jit(solution)/shard_map/ppermute | solution.py:537
  25.1 1.4 %collective-permute-start.13 = (f32[6,32,128]{2,1,0:T(8,128)S(1)}, f32[6,32,128]{2,1,0:T(8,128)S(1)}, u32[]{:S(2)}, u32[]{:S(2)}) collective-permute-start(f32[6,32,128]{2,1,0:T(8,128)S(1)} %pad_maximum_fusion), channel_id=1, source_target_pairs={{0,1},{1,0},{2,3},{3,2},{4,5},{5,4},{6,7},{7,6},{8,9},{9,8},{10,11... | collective-permute-start | bytes 294920 | tf_op jit(solution)/shard_map/ppermute | solution.py:539
  28.0 4.1 %collective-permute-start.14 = (f32[24,8,128]{2,1,0:T(8,128)S(1)}, f32[24,8,128]{2,1,0:T(8,128)S(1)}, u32[]{:S(2)}, u32[]{:S(2)}) collective-permute-start(f32[24,8,128]{2,1,0:T(8,128)S(1)} %get-tuple-element.118), channel_id=1, source_target_pairs={{0,1},{1,0},{2,3},{3,2},{4,5},{5,4},{6,7},{7,6},{8,9},{9,8},{10,11... | collective-permute-start | bytes 294920 | tf_op jit(solution)/shard_map/ppermute | solution.py:551
  28.1 11.4 %all-to-all-start = ((f32[32,4,128]{2,1,0:T(4,128)}), f32[32,4,128]{2,1,0:T(4,128)S(1)}, u32[]{:S(2)}, u32[]{:S(2)}) async-start(f32[32,4,128]{2,1,0:T(4,128)} %get-tuple-element.127), calls=%async_computation | async-start | bytes 131072 | tf_op jit(solution)/shard_map/all_to_all | solution.py:557
  32.1 7.4 %collective-permute-start.15 = (f32[9,8,128]{2,1,0:T(8,128)S(1)}, f32[9,8,128]{2,1,0:T(8,128)S(1)}, u32[]{:S(2)}, u32[]{:S(2)}) collective-permute-start(f32[9,8,128]{2,1,0:T(8,128)S(1)} %get-tuple-element.124), channel_id=1, source_target_pairs={{0,1},{1,0},{2,4},{3,5},{4,2},{5,3},{6,8},{7,9},{8,6},{9,7},{10,12... | collective-permute-start | bytes 110600 | tf_op jit(solution)/shard_map/ppermute | solution.py:554
  32.4 7.1 %collective-permute-start.16 = (f32[9,8,128]{2,1,0:T(8,128)S(1)}, f32[9,8,128]{2,1,0:T(8,128)S(1)}, u32[]{:S(2)}, u32[]{:S(2)}) collective-permute-start(f32[9,8,128]{2,1,0:T(8,128)S(1)} %get-tuple-element.125), channel_id=1, source_target_pairs={{0,2},{1,3},{2,0},{3,1},{4,6},{5,7},{6,4},{7,5},{8,10},{9,11},{10,... | collective-permute-start | bytes 110600 | tf_op jit(solution)/shard_map/ppermute | solution.py:555
  35.4 4.1 %collective-permute-start.17 = (f32[9,8,128]{2,1,0:T(8,128)S(1)}, f32[9,8,128]{2,1,0:T(8,128)S(1)}, u32[]{:S(2)}, u32[]{:S(2)}) collective-permute-start(f32[9,8,128]{2,1,0:T(8,128)S(1)} %get-tuple-element.126), channel_id=1, source_target_pairs={{0,2},{1,4},{2,0},{3,6},{4,1},{5,8},{6,3},{7,10},{8,5},{9,12},{10,... | collective-permute-start | bytes 110600 | tf_op jit(solution)/shard_map/ppermute | solution.py:556
  (1 other events, 2.4 us)
